TPU v7x, 256 devices: a whole 4x4x8 slice. The times are simulated.
256 devices in a mesh: dp: 64 (over x, z_hi, y), seq: 4 (over z_lo, core).
Axes of the slice: x: 4, y: 4, z: 8 (z_hi: 4, z_lo: 2; z = z_hi * 2 + z_lo), core: 2. Of those that a mesh axis runs over, the one named last changes fastest.
Arguments:
- features: bfloat16 [64, 4096, 512], P('dp', 'seq'), may hold values from -6 to 6
- w_five: bfloat16 [1536, 512], P('dp'), may hold values from -0.15625 to 0.15625
- w_six: bfloat16 [1024, 512], P('dp'), may hold values from -0.1875 to 0.1875
- w_seven: bfloat16 [1024, 512], P('dp'), may hold values from -0.1875 to 0.1875
- channel_params: bfloat16 [512, 11], P('dp'), may hold values from -1.2 to 1.5, as said below
- w_proj: bfloat16 [512, 1920], P('dp'), may hold values from -0.25 to 0.25
- proj_bias: bfloat16 [1920], P('dp'), may hold values from -3 to 3
- out_cotangent: bfloat16 [64, 512, 1920], P('dp', 'seq'), may hold values from -0.5 to 0.5
Outputs:
- projected: bfloat16 [64, 512, 1920], P('dp', 'seq')
- input_grad: bfloat16 [64, 4096, 512], P('dp', 'seq')
- grad_five: float32 [1536, 512], P('dp')
- grad_six: float32 [1024, 512], P('dp')
- grad_seven: float32 [1024, 512], P('dp')
- grad_channel: float32 [512, 11], P('dp')
- grad_proj: float32 [512, 1920], P('dp')
- grad_bias: float32 [1920], P('dp')
Inputs may be any that keep to these rules, and one draw needn't show every extreme that they name: `channel_params`: columns 1, 4, 7 and 9 lie between 0.5 and 1.5; the other columns lie between -1.2 and 1.2.
All inputs are finite; a program needn't handle non-finite values.
Results may differ from a plain program's by a relative error of at most 0.017.
Values may be sent and summed in bfloat16 or wider, within the bound.
No kernel may reach another device: no remote copies, remote signals or barrier semaphores. Data moves between devices by JAX's collectives and lax.ppermute only.
A program may use at most 128 MiB of HBM per device.

v0:
```python
import jax
import jax.numpy as jnp
from jax import lax
from jax.experimental import pallas as pl
from jax.experimental.pallas import tpu as pltpu
from jax.sharding import Mesh, PartitionSpec as P

epsilon = 1e-05
f32 = jnp.float32
bf16 = jnp.bfloat16
CH = 512
WIDTH = 1920
HALF = 256
STEP = 32


def dot(left, right, contract=(1, 0)):
    return lax.dot_general(
        left, right, (((contract[0],), (contract[1],)), ((), ())), preferred_element_type=f32
    )


def call(body, outs, scratch=(), flops=0, moved=0):
    return pl.pallas_call(
        body,
        out_shape=[jax.ShapeDtypeStruct(shape, kind) for shape, kind in outs],
        scratch_shapes=[pltpu.VMEM(shape, kind) for shape, kind in scratch],
        compiler_params=pltpu.CompilerParams(vmem_limit_bytes=40 * 2**20),
        cost_estimate=pl.CostEstimate(flops=flops, bytes_accessed=moved, transcendentals=0),
    )


def scalar_call(body, arrays, outs, scratch, flops, moved):
    whole = pl.BlockSpec(memory_space=pltpu.VMEM)
    return pl.pallas_call(
        body,
        out_shape=[jax.ShapeDtypeStruct(shape, kind) for shape, kind in outs],
        in_specs=[pl.BlockSpec(memory_space=pltpu.SMEM)] + [whole] * arrays,
        scratch_shapes=[pltpu.VMEM(shape, kind) for shape, kind in scratch],
        compiler_params=pltpu.CompilerParams(vmem_limit_bytes=40 * 2**20),
        cost_estimate=pl.CostEstimate(flops=flops, bytes_accessed=moved, transcendentals=0),
    )


def place(index):
    return (index // 16) * 16 + (index % 4) * 4 + (index // 4) % 4


def rows(index, size):
    return pl.ds(pl.multiple_of(index * size, size), size)


def by_core(core_ref, body):
    @pl.when(core_ref[0] == 0)
    def _():
        body(0, HALF)

    @pl.when(core_ref[0] != 0)
    def _():
        body(HALF, 0)


def row_mean(values):
    return jnp.sum(values, -1, keepdims=True) * (1.0 / CH)


def standard(values):
    centred = values - row_mean(values)
    scale = lax.rsqrt(row_mean(centred * centred) + epsilon)
    return centred * scale, scale


def fold(values):
    return jnp.sum(values.reshape(-1, 8, values.shape[-1]), 0)


def block_forward(pre_ref, cp_ref, first, act_ref, unit_ref, slope_ref, scale_ref):
    offset, gain, shift = (cp_ref[first + i : first + i + 1] for i in range(3))

    def step(i, _):
        at = rows(i, STEP)
        unit, scale = standard(pre_ref[at, :] + offset)
        z = unit * gain + shift
        cdf = 0.5 + 0.5 * lax.erf(z * 0.7071067811865476)
        act_ref[at, :] = (z * cdf).astype(bf16)
        slope_ref[at, :] = cdf + z * (0.3989422804014327 * jnp.exp(-0.5 * z * z))
        unit_ref[at, :] = unit
        scale_ref[at, :] = jnp.broadcast_to(scale, (STEP, 128))
        return 0

    lax.fori_loop(0, pre_ref.shape[0] // STEP, step, 0)


def block_backward(grad_ref, cp_ref, first, unit_ref, slope_ref, scale_ref, out_ref):
    gain = cp_ref[first + 1 : first + 2]

    def step(i, sums):
        at = rows(i, STEP)
        unit = unit_ref[at, :]
        dz = grad_ref[at, :] * slope_ref[at, :]
        dunit = dz * gain
        du = scale_ref[at, :1] * (dunit - row_mean(dunit) - unit * row_mean(dunit * unit))
        out_ref[at, :] = du.astype(bf16)
        return (sums[0] + fold(du), sums[1] + fold(dz * unit), sums[2] + fold(dz))

    zero = jnp.zeros((8, CH), f32)
    return lax.fori_loop(0, grad_ref.shape[0] // STEP, step, (zero, zero, zero))


def total(values):
    return jnp.sum(values, 0, keepdims=True)


def spread(transposed):
    group = lax.broadcasted_iota(jnp.int32, (256, 256), 1 if transposed else 0)
    position = lax.broadcasted_iota(jnp.int32, (256, 256), 0 if transposed else 1)
    return (position == 8 * (group % 32) + group // 32).astype(bf16)


def split_kernel(x_ref, next_ref, even_ref, odd_ref, third_ref, first_ref):
    matrix = spread(False)
    for j in range(4):
        groups = dot(matrix, x_ref[256 * j : 256 * j + 256, :])
        first_ref[32 * j : 32 * j + 32, :] = groups[:32]
        groups = groups.astype(bf16)
        for r in range(4):
            at = slice(128 * r + 32 * j, 128 * r + 32 * j + 32)
            even_ref[at, :] = groups[64 * r : 64 * r + 32]
            odd_ref[at, :] = groups[64 * r + 32 : 64 * r + 64]
            if r > 0:
                third_ref[128 * r - 128 + 32 * j : 128 * r - 96 + 32 * j, :] = groups[64 * r : 64 * r + 32]
    later = pltpu.roll(first_ref[...], 127, 0)
    last = lax.broadcasted_iota(jnp.int32, (128, CH), 0) == 127
    third_ref[384:512, :] = jnp.where(last, next_ref[:1, :].astype(f32), later).astype(bf16)


def five_forward_kernel(
    core_ref, even_ref, odd_ref, third_ref, mine_ref, other_ref,
    act_ref, unit_ref, slope_ref, scale_ref, w_ref, cp_ref, wide_ref, small_ref, pre_ref,
):
    def body(mine_at, other_at):
        def step(i, _):
            to = place(i)
            for ref, at in ((mine_ref, mine_at), (other_ref, other_at)):
                block = ref[i].astype(f32)
                wide_ref[rows(to, 24), at : at + HALF] = block[:24]
                if at == 0:
                    small_ref[rows(to, 8), :] = block[24:, :128]
            return 0

        lax.fori_loop(0, 64, step, 0)

    by_core(core_ref, body)
    cp_ref[...] = small_ref[...].T[:16]

    def narrow(i, _):
        w_ref[rows(i, 128), :] = wide_ref[rows(i, 128), :].astype(bf16)
        return 0

    lax.fori_loop(0, 12, narrow, 0)

    def multiply(r, _):
        at = rows(r, 128)
        pre_ref[at, :] = (
            dot(even_ref[at, :], w_ref[:512, :]) + dot(odd_ref[at, :], w_ref[512:1024, :])
        ) + dot(third_ref[at, :], w_ref[1024:, :])
        return 0

    lax.fori_loop(0, 4, multiply, 0)
    block_forward(pre_ref, cp_ref, 0, act_ref, unit_ref, slope_ref, scale_ref)


def upper_kernel(
    core_ref, five_ref, mine_ref, other_ref, cp_ref, bias_ref, cot_ref,
    out_ref, grad_ref, sums_ref, give_ref, send_ref,
    w6_ref, w7_ref, wp_ref, wide_ref,
    pre6_ref, act6_ref, unit6_ref, slope6_ref, scale6_ref,
    pre7_ref, act7_ref, unit7_ref, slope7_ref, scale7_ref,
    g6_ref, g7_ref, gp_ref, d6_ref, d7_ref,
):
    def unpack(mine_at, other_at):
        def step(i, _):
            to = place(i)
            for ref, at in ((mine_ref, mine_at), (other_ref, other_at)):
                w6_ref[rows(to, 16), at : at + HALF] = ref[i, :16]
                w7_ref[rows(to, 16), at : at + HALF] = ref[i, 16:32]
                block = ref[i, 32:].astype(f32)
                for b in range(4):
                    wide_ref[rows(to, 8), 4 * at + HALF * b : 4 * at + HALF * (b + 1)] = block[8 * b : 8 * b + 8]
            return 0

        lax.fori_loop(0, 64, step, 0)

    by_core(core_ref, unpack)

    def narrow(i, _):
        wp_ref[rows(i, 64), :] = wide_ref[rows(i, 64), :WIDTH].astype(bf16)
        return 0

    lax.fori_loop(0, 8, narrow, 0)

    for s in range(2):
        pre6_ref[128 * s : 128 * s + 128, :] = dot(five_ref[256 * s : 256 * s + 128, :], w6_ref[:512, :]) + dot(
            five_ref[256 * s + 128 : 256 * s + 256, :], w6_ref[512:, :]
        )
    block_forward(pre6_ref, cp_ref, 3, act6_ref, unit6_ref, slope6_ref, scale6_ref)
    pre7_ref[...] = dot(act6_ref[:128, :], w7_ref[:512, :]) + dot(act6_ref[128:, :], w7_ref[512:, :])
    block_forward(pre7_ref, cp_ref, 6, act7_ref, unit7_ref, slope7_ref, scale7_ref)

    unit, scale = standard(act7_ref[...].astype(f32))
    normed = (unit * cp_ref[9:10] + cp_ref[10:11]).astype(bf16)
    flipped = normed.astype(f32).T.astype(bf16)
    normed_grad = jnp.zeros((128, CH), f32)
    for b in range(8):
        cols = slice(HALF * b, min(HALF * (b + 1), WIDTH))
        out_ref[:, cols] = (dot(normed, wp_ref[:, cols]) + bias_ref[:, cols]).astype(bf16)
        cot = cot_ref[:, cols]
        gp_ref[:, cols] = dot(flipped, cot)
        normed_grad = normed_grad + dot(cot, wp_ref[:, cols], (1, 1))
    gp_ref[:, WIDTH:] = jnp.zeros((CH, 8 * HALF - WIDTH), f32)

    dunit = normed_grad * cp_ref[9:10]
    sums_ref[9:10, :] = total(normed_grad * unit)
    sums_ref[10:11, :] = total(normed_grad)
    pre7_ref[...] = scale * (dunit - row_mean(dunit) - unit * row_mean(dunit * unit))

    for i, part in enumerate(block_backward(pre7_ref, cp_ref, 6, unit7_ref, slope7_ref, scale7_ref, d7_ref)):
        sums_ref[6 + i : 7 + i, :] = total(part)
    for s in range(2):
        half = slice(512 * s, 512 * s + 512)
        g7_ref[half, :] = dot(act6_ref[128 * s : 128 * s + 128, :], d7_ref[...], (0, 0))
        pre6_ref[128 * s : 128 * s + 128, :] = dot(d7_ref[...], w7_ref[half, :], (1, 1))
    for i, part in enumerate(block_backward(pre6_ref, cp_ref, 3, unit6_ref, slope6_ref, scale6_ref, d6_ref)):
        sums_ref[3 + i : 4 + i, :] = total(part)
    for r in range(2):
        half = slice(512 * r, 512 * r + 512)
        g6_ref[half, :] = dot(five_ref[128 * r : 128 * r + 128, :], d6_ref[:128, :], (0, 0)) + dot(
            five_ref[256 + 128 * r : 384 + 128 * r, :], d6_ref[128:, :], (0, 0)
        )
        for s in range(2):
            at = 256 * s + 128 * r
            grad_ref[at : at + 128, :] = dot(d6_ref[128 * s : 128 * s + 128, :], w6_ref[half, :], (1, 1))
    for i in (0, 1, 2, 11, 12, 13, 14, 15):
        sums_ref[i : i + 1, :] = jnp.zeros((1, CH), f32)

    def pack(mine_at, other_at):
        def step(i, _):
            to = place(i)
            for ref, at in ((give_ref, mine_at), (send_ref, other_at)):
                ref[i, :16, :] = g6_ref[rows(to, 16), at : at + HALF].astype(bf16)
                ref[i, 16:32, :] = g7_ref[rows(to, 16), at : at + HALF].astype(bf16)
                block = gp_ref[rows(to, 8), 4 * at : 4 * at + 4 * HALF]
                parts = [block[:, HALF * b : HALF * (b + 1)] for b in range(4)]
                ref[i, 32:, :] = jnp.concatenate(parts, 0).astype(bf16)
            return 0

        lax.fori_loop(0, 64, step, 0)

    by_core(core_ref, pack)


def five_backward_kernel(
    core_ref, grad_ref, even_ref, odd_ref, third_ref, unit_ref, slope_ref, scale_ref, w_ref, cp_ref, sums_ref, gb_ref,
    give_ref, send_ref, d_ref, edge_ref, g_ref, small_ref,
):
    parts = block_backward(grad_ref, cp_ref, 0, unit_ref, slope_ref, scale_ref, d_ref)
    for i, part in enumerate(parts):
        small_ref[i : i + 1, :] = total(part)
    small_ref[3:11, :] = sums_ref[3:11, :]
    small_ref[11:, :] = jnp.zeros((117, CH), f32)
    columns = small_ref[...].T
    edge_ref[...] = dot(d_ref[496:512, :], w_ref[1024:, :], (1, 1))[8:]
    for k, ref in enumerate((even_ref, odd_ref, third_ref)):
        g_ref[512 * k : 512 * k + 512, :] = dot(ref[...], d_ref[...], (0, 0))
    for i in range(4):
        small_ref[:, 128 * i : 128 * i + 128] = columns[128 * i : 128 * i + 128, :]

    def pack(mine_at, other_at):
        for x in range(4):

            def step(i, _, x=x):
                at_shard = 16 * x + i
                to = place(at_shard)
                for ref, at in ((give_ref, mine_at), (send_ref, other_at)):
                    if at == 0:
                        low = small_ref[rows(to - 16 * x, 8), 128 * x : 128 * x + 128]
                        tail = jnp.concatenate([low, gb_ref[rows(to, 8), :]], 1)
                    else:
                        tail = jnp.zeros((8, HALF), f32)
                    block = jnp.concatenate([g_ref[rows(to, 24), at : at + HALF], tail], 0)
                    ref[at_shard] = block.astype(bf16)
                return 0

            lax.fori_loop(0, 16, step, 0)

    by_core(core_ref, pack)


def input_kernel(d_ref, w_ref, carried_ref, out_ref, even_ref, odd_ref, third_ref):
    def multiply(r, _):
        at = rows(r, 128)
        d = d_ref[at, :]
        even_ref[at, :] = dot(d, w_ref[:512, :], (1, 1))
        odd_ref[at, :] = dot(d, w_ref[512:1024, :], (1, 1))
        third_ref[at, :] = dot(d, w_ref[1024:, :], (1, 1))
        return 0

    lax.fori_loop(0, 4, multiply, 0)
    earlier = pltpu.roll(third_ref[384:512, :], 1, 0)
    first = lax.broadcasted_iota(jnp.int32, (128, CH), 0) == 0
    even_ref[:128, :] += jnp.where(first, carried_ref[...], earlier)
    even_ref[128:, :] += third_ref[:384, :]
    matrix = spread(True)
    for j in range(4):
        parts = []
        for r in range(4):
            at = slice(128 * r + 32 * j, 128 * r + 32 * j + 32)
            parts += [even_ref[at, :].astype(bf16), odd_ref[at, :].astype(bf16)]
        out_ref[256 * j : 256 * j + 256, :] = dot(matrix, jnp.concatenate(parts, 0)).astype(bf16)


def swap_cores(value):
    return lax.ppermute(value, "core", [(0, 1), (1, 0)])


def gather(shard, core):
    count = shard.shape[0]
    half = jnp.where(core == 0, shard[:, :HALF], shard[:, HALF:])
    line = lax.all_to_all(jnp.broadcast_to(half[None], (4, count, HALF)), "zh", 0, 0, tiled=True)
    plane = lax.all_to_all(
        jnp.broadcast_to(line[None], (16, 4, count, HALF)), ("x", "y"), 0, 0, tiled=True
    )
    mine = plane.reshape(64, count, HALF)
    return mine, swap_cores(mine)


def reduce(give, send):
    count = give.shape[1]
    summed = (give.astype(f32) + swap_cores(send).astype(f32)).astype(bf16)
    plane = lax.all_to_all(summed.reshape(16, 4, count, HALF), ("x", "y"), 0, 0, tiled=True)
    summed = jnp.sum(plane.astype(f32), 0).astype(bf16)
    line = jnp.broadcast_to(summed[:, None], (4, 4, count, HALF)).reshape(16, count, HALF)
    line = lax.all_to_all(line, ("zh", "zl", "core"), 0, 0, tiled=True)
    return jnp.sum(line.reshape(8, 2, count, HALF).astype(f32), 0)


def proj_blocks(value):
    value = jnp.pad(value, [(0, 0), (0, 8 * HALF - WIDTH)]).reshape(8, 2, 4, HALF)
    return value.transpose(2, 0, 1, 3).reshape(32, 512)


def proj_rows(halves):
    return halves.reshape(2, 4, 8, HALF).transpose(2, 0, 1, 3).reshape(8, 8 * HALF)[:, :WIDTH]


def shards(features, w_five, w_six, w_seven, channel_params, w_proj, proj_bias, out_cotangent):
    core = lax.axis_index("core")
    core_at = core.astype(jnp.int32).reshape(1)
    inputs, cotangent = features[0], out_cotangent[0]

    small = jnp.concatenate(
        [
            jnp.pad(channel_params, [(0, 0), (0, 117)]),
            jnp.pad(proj_bias[None], [(0, 7), (0, 98)]),
            jnp.zeros((8, HALF), bf16),
        ],
        1,
    )
    mine_a, other_a = gather(jnp.concatenate([w_five, small], 0), core)
    mine_b, other_b = gather(jnp.concatenate([w_six, w_seven, proj_blocks(w_proj)], 0), core)
    next_row = lax.ppermute(inputs[:8], ("zl", "core"), [(1, 0), (2, 1), (3, 2)])

    square = (512, CH)
    even, odd, third, _ = call(
        split_kernel, [(square, bf16)] * 3 + [((128, CH), f32)], flops=2**28, moved=3 * 2**20
    )(inputs, next_row)
    grad_bias = jnp.sum(cotangent.astype(f32), 0).reshape(64, 1, 30)
    grad_bias = jnp.pad(grad_bias, [(0, 0), (0, 7), (0, 98)]).reshape(512, 128)

    low_a = jnp.where(core == 0, mine_a[:, 24, 128:158], other_a[:, 24, 128:158])
    bias = low_a.reshape(4, 4, 4, 30).transpose(0, 2, 1, 3).reshape(1, WIDTH).astype(f32)

    act_five, unit_five, slope_five, scale_five, w5, cp = scalar_call(
        five_forward_kernel,
        5,
        [(square, bf16), (square, f32), (square, f32), ((512, 128), f32), ((1536, CH), bf16), ((16, CH), f32)],
        [((1536, CH), f32), ((512, 128), f32), (square, f32)],
        flops=2**30,
        moved=8 * 2**20,
    )(core_at, even, odd, third, mine_a, other_a)

    half_rows = lambda n: [((n, CH), f32), ((n, CH), bf16), ((n, CH), f32), ((n, CH), f32), ((n, 128), f32)]
    projected, act_grad, sums, give_b, send_b = scalar_call(
        upper_kernel,
        6,
        [((128, WIDTH), bf16), (square, f32), ((16, CH), f32), ((64, 64, HALF), bf16), ((64, 64, HALF), bf16)],
        [((1024, CH), bf16), ((1024, CH), bf16), ((CH, WIDTH), bf16), ((CH, 8 * HALF), f32)]
        + half_rows(256)
        + half_rows(128)
        + [((1024, CH), f32), ((1024, CH), f32), ((CH, 8 * HALF), f32), ((256, CH), bf16), ((128, CH), bf16)],
        flops=2**31,
        moved=12 * 2**20,
    )(core_at, act_five, mine_b, other_b, cp, bias, cotangent)
    sum_b = reduce(give_b, send_b)

    give_a, send_a, d_five, edge = scalar_call(
        five_backward_kernel,
        11,
        [((64, 32, HALF), bf16), ((64, 32, HALF), bf16), (square, bf16), ((8, CH), f32)],
        [((1536, CH), f32), ((128, CH), f32)],
        flops=2**30,
        moved=8 * 2**20,
    )(core_at, act_grad, even, odd, third, unit_five, slope_five, scale_five, w5, cp, sums, grad_bias)
    sum_a = reduce(give_a, send_a)

    carried = lax.ppermute(edge[7:8], ("zl", "core"), [(0, 1), (1, 2), (2, 3)])
    (input_grad,) = call(
        input_kernel, [((1024, CH), bf16)], [(square, f32)] * 3, flops=2**30, moved=4 * 2**20
    )(d_five, w5, carried)

    joined = lambda halves: jnp.concatenate([halves[0], halves[1]], 1)
    return (
        projected[None],
        input_grad[None],
        joined(sum_a[:, :24]),
        joined(sum_b[:, :16]),
        joined(sum_b[:, 16:32]),
        sum_a[0, 24:, :11],
        proj_rows(sum_b[:, 32:]),
        sum_a[0, 24, 128:158],
    )


def solution(mesh):
    fine = Mesh(mesh.devices.reshape(4, 4, 4, 2, 2), ("x", "zh", "y", "zl", "core"))
    dp, seq = ("x", "zh", "y"), ("zl", "core")
    placed = (
        P(dp, seq, None),
        P(dp, None),
        P(dp, None),
        P(dp, None),
        P(dp, None),
        P(dp, None),
        P(dp),
        P(dp, seq, None),
    )
    return jax.shard_map(
        shards,
        mesh=fine,
        in_specs=placed,
        out_specs=(
            P(dp, seq, None),
            P(dp, seq, None),
            P(dp, None),
            P(dp, None),
            P(dp, None),
            P(dp, None),
            P(dp, None),
            P(dp),
        ),
        check_vma=False,
    )
```

profile of v0, /device:TPU:1, one launch (start us, length us, event | category | flops | bytes accessed | tf_op | source)
XLA Modules:
  0.0 222.9 jit_solution(17098086465564009078)
XLA Ops:
  2.1 9.0 %all-to-all-start = ((bf16[4,32,256]{2,1,0:T(8,128)(2,1)}), bf16[4,32,256]{2,1,0:T(8,128)(2,1)S(1)}, u32[]{:S(2)}, u32[]{:S(2)}) async-start(bf16[4,32,256]{2,1,0:T(8,128)(2,1)} %broadcast_in_dim.22), calls=%async_computation | async-start | bytes 131072 | tf_op jit(solution)/shard_map/all_to_all | solution.py:329
  13.4 4.8 %all-to-all-done = bf16[4,32,256]{2,1,0:T(8,128)(2,1)S(1)} async-done(((bf16[4,32,256]{2,1,0:T(8,128)(2,1)}), bf16[4,32,256]{2,1,0:T(8,128)(2,1)S(1)}, u32[]{:S(2)}, u32[]{:S(2)}) %all-to-all-start) | async-done | bytes 65568 | tf_op jit(solution)/shard_map/all_to_all | solution.py:329
  18.1 9.7 %all_to_all.40 = bf16[4,64,256]{2,1,0:T(8,128)(2,1)S(1)} all-to-all(bf16[4,64,256]{2,1,0:T(8,128)(2,1)S(1)} %broadcast_in_dim.24), channel_id=1, replica_groups=mesh['x'=4,'zh'=4,'y'=4,'zl'=2,'core'=2] {'zh'}, dimensions={0} | all-to-all | bytes 262144 | tf_op jit(solution)/shard_map/all_to_all | solution.py:329
  28.1 31.0 %all_to_all.41 = bf16[16,4,64,256]{3,2,1,0:T(8,128)(2,1)S(1)} all-to-all(bf16[16,4,64,256]{3,2,1,0:T(8,128)(2,1)S(1)} %broadcast_in_dim.25), channel_id=1, replica_groups=mesh['x'=4,'zh'=4,'y'=4,'zl'=2,'core'=2] {'x','y'}, dimensions={0} | all-to-all | bytes 4194304 | tf_op jit(solution)/shard_map/all_to_all | solution.py:330
  59.1 1.2 broadcast_in_dim.23
  60.3 3.7 %all-to-all-start.1 = ((bf16[16,4,32,256]{3,2,1,0:T(8,128)(2,1)}), bf16[16,4,32,256]{3,2,1,0:T(8,128)(2,1)S(1)}, u32[]{:S(2)}, u32[]{:S(2)}) async-start(bf16[16,4,32,256]{3,2,1,0:T(8,128)(2,1)} %broadcast_in_dim.23), calls=%async_computation.1 | async-start | bytes 2097152 | tf_op jit(solution)/shard_map/all_to_all | solution.py:330
  64.0 4.9 %collective-permute-start.2 = (bf16[64,64,256]{2,1,0:T(8,128)(2,1)S(1)}, bf16[64,64,256]{2,1,0:T(8,128)(2,1)}, u32[]{:S(2)}, u32[]{:S(2)}) collective-permute-start(bf16[64,64,256]{2,1,0:T(8,128)(2,1)S(1)} %bitcast.54), channel_id=1, source_target_pairs={{0,1},{1,0},{2,3},{3,2},{4,5},{5,4},{6,7},{7,6},{8,9},{9,8},{10,11... | collective-permute-start | bytes 6291464 | tf_op jit(solution)/shard_map/ppermute | solution.py:323
  68.9 7.1 %all-to-all-done.1 = bf16[16,4,32,256]{3,2,1,0:T(8,128)(2,1)S(1)} async-done(((bf16[16,4,32,256]{3,2,1,0:T(8,128)(2,1)}), bf16[16,4,32,256]{3,2,1,0:T(8,128)(2,1)S(1)}, u32[]{:S(2)}, u32[]{:S(2)}) %all-to-all-start.1) | async-done | bytes 1048608 | tf_op jit(solution)/shard_map/all_to_all | solution.py:330
  76.0 6.2 %collective-permute-start.1 = (bf16[64,32,256]{2,1,0:T(8,128)(2,1)S(1)}, bf16[64,32,256]{2,1,0:T(8,128)(2,1)}, u32[]{:S(2)}, u32[]{:S(2)}) collective-permute-start(bf16[64,32,256]{2,1,0:T(8,128)(2,1)S(1)} %bitcast.56), channel_id=1, source_target_pairs={{0,1},{1,0},{2,3},{3,2},{4,5},{5,4},{6,7},{7,6},{8,9},{9,8},{10,11... | collective-permute-start | bytes 3145736 | tf_op jit(solution)/shard_map/ppermute | solution.py:323
  82.9 1.9 collective-permute-start
  84.8 1.1 convert_reduce_fusion.1
  86.1 1.8 collective-permute-done.next_ref
  87.9 1.2 copy-done.4
  93.7 1.2 copy-done.6
  97.0 7.6 %shard_map.144 = (bf16[512,512]{1,0:T(8,128)(2,1)S(1)}, f32[512,512]{1,0:T(8,128)S(1)}, f32[512,512]{1,0:T(8,128)S(1)}, f32[512,128]{1,0:T(8,128)S(1)}, bf16[153...) custom-call(s32[1]{0:T(128)} %bitcast.core_ref, bf16[512,512]{1,0:T(8,128)(2,1)S(1)} %copy-done.6, ...), custom_call_target="tpu_custom_call" | custom-call | flops 1073741824 | bytes 8388608 | tf_op jit(solution)/shard_map/pallas_call | solution.py:383
  104.7 15.1 %shard_map.145 = (bf16[128,1920]{1,0:T(8,128)(2,1)}, f32[512,512]{1,0:T(8,128)S(1)}, f32[16,512]{1,0:T(8,128)S(1)}, bf16[64,64,256]{2,1,0:T(8,128)(2,1)S(1)}, bf16[64,64,256]{2,1,0:T(8,128)(2,1)}) custom-call(s32[1]{0:T(128)} %bitcast.core_ref, bf16[512,512]{1,0:T(8,128)(2,1)S(1)} %get-tuple-element.29.five_ref, bf16[64,64,256]{2,1,0:T(8,128)(2,1)S(1)} %bitcast.55, ...), custom_call_target="tpu_custom_call" | custom-call | flops 2147483648 | bytes 12582912 | tf_op jit(solution)/shard_map/pallas_call | solution.py:393
  119.8 4.3 %shard_map.146 = (bf16[64,32,256]{2,1,0:T(8,128)(2,1)S(1)}, bf16[64,32,256]{2,1,0:T(8,128)(2,1)S(1)}, bf16[512,512]{1,0:T(8,128)(2,1)S(1)}, f32[8,512]{1,0:T(8,128)S(1)}) custom-call(s32[1]{0:T(128)} %bitcast.core_ref, f32[512,512]{1,0:T(8,128)S(1)} %get-tuple-element.32.grad_ref, bf16[512,512]{1,0:T(8,128)(2,1)S(1)} %copy-done.7, ...), custom_call_target="tpu_custom_call" | custom-call | flops 1073741824 | bytes 8388608 | tf_op jit(solution)/shard_map/pallas_call | solution.py:406
  124.7 2.3 %collective-permute-done.4 = bf16[64,32,256]{2,1,0:T(8,128)(2,1)S(1)} collective-permute-done((bf16[64,32,256]{2,1,0:T(8,128)(2,1)S(1)}, bf16[64,32,256]{2,1,0:T(8,128)(2,1)S(1)}, u32[]{:S(2)}, u32[]{:S(2)}) %collective-permute-start.4) | collective-permute-done | bytes 1048608 | tf_op jit(solution)/shard_map/ppermute | solution.py:323
  127.0 1.4 add_convert_fusion.1
  128.4 4.4 %all-to-all-start.4 = ((bf16[16,4,32,256]{3,2,1,0:T(8,128)(2,1)}), bf16[16,4,32,256]{3,2,1,0:T(8,128)(2,1)}, u32[]{:S(2)}, u32[]{:S(2)}) async-start(bf16[16,4,32,256]{3,2,1,0:T(8,128)(2,1)} %bitcast.62), calls=%async_computation.4 | async-start | bytes 2097152 | tf_op jit(solution)/shard_map/all_to_all | solution.py:340
  132.8 3.8 %add_convert_fusion = bf16[64,64,256]{2,1,0:T(8,128)(2,1)} fusion(bf16[64,64,256]{2,1,0:T(8,128)(2,1)} %collective-permute-done.5, bf16[64,64,256]{2,1,0:T(8,128)(2,1)S(1)} %get-tuple-element.42), kind=kLoop, calls=%fused_computation | loop fusion | flops 4194304 | bytes 6291456 | tf_op jit(solution)/shard_map/convert_element_type | solution.py:339
  136.6 12.7 %all-to-all-done.4 = bf16[16,4,32,256]{3,2,1,0:T(8,128)(2,1)} async-done(((bf16[16,4,32,256]{3,2,1,0:T(8,128)(2,1)}), bf16[16,4,32,256]{3,2,1,0:T(8,128)(2,1)}, u32[]{:S(2)}, u32[]{:S(2)}) %all-to-all-start.4) | async-done | bytes 1048608 | tf_op jit(solution)/shard_map/all_to_all | solution.py:340
  149.4 4.0 %all-to-all-start.6 = ((bf16[16,4,64,256]{3,2,1,0:T(8,128)(2,1)}), bf16[16,4,64,256]{3,2,1,0:T(8,128)(2,1)S(1)}, u32[]{:S(2)}, u32[]{:S(2)}) async-start(bf16[16,4,64,256]{3,2,1,0:T(8,128)(2,1)} %bitcast.61), calls=%async_computation.6 | async-start | bytes 4194304 | tf_op jit(solution)/shard_map/all_to_all | solution.py:340
  153.3 1.4 reduce_sum.52
  154.7 24.1 %all-to-all-done.6 = bf16[16,4,64,256]{3,2,1,0:T(8,128)(2,1)S(1)} async-done(((bf16[16,4,64,256]{3,2,1,0:T(8,128)(2,1)}), bf16[16,4,64,256]{3,2,1,0:T(8,128)(2,1)S(1)}, u32[]{:S(2)}, u32[]{:S(2)}) %all-to-all-start.6) | async-done | bytes 2097184 | tf_op jit(solution)/shard_map/all_to_all | solution.py:340
  180.3 8.5 %all-to-all-start.5 = ((bf16[16,32,256]{2,1,0:T(8,128)(2,1)}), bf16[16,32,256]{2,1,0:T(8,128)(2,1)S(1)}, u32[]{:S(2)}, u32[]{:S(2)}) async-start(bf16[16,32,256]{2,1,0:T(8,128)(2,1)} %bitcast.15), calls=%async_computation.5 | async-start | bytes 524288 | tf_op jit(solution)/shard_map/all_to_all | solution.py:343
  188.8 3.7 %collective-permute-start.3 = (f32[1,512]{1,0:T(1,128)S(1)}, f32[1,512]{1,0:T(1,128)S(1)}, u32[]{:S(2)}, u32[]{:S(2)}) collective-permute-start(f32[1,512]{1,0:T(1,128)S(1)} %slice.74), channel_id=1, source_target_pairs={{0,1},{1,2},{2,3},{4,5},{5,6},{6,7},{8,9},{9,10},{10,11},{12,13},{... | collective-permute-start | bytes 6152 | tf_op jit(solution)/shard_map/ppermute | solution.py:416
  192.5 2.0 reduce_sum.54
  194.5 6.3 %all-to-all-done.5 = bf16[16,32,256]{2,1,0:T(8,128)(2,1)S(1)} async-done(((bf16[16,32,256]{2,1,0:T(8,128)(2,1)}), bf16[16,32,256]{2,1,0:T(8,128)(2,1)S(1)}, u32[]{:S(2)}, u32[]{:S(2)}) %all-to-all-start.5) | async-done | bytes 262176 | tf_op jit(solution)/shard_map/all_to_all | solution.py:343
  201.6 3.5 %all-to-all-start.7 = ((bf16[16,64,256]{2,1,0:T(8,128)(2,1)}), bf16[16,64,256]{2,1,0:T(8,128)(2,1)S(1)}, u32[]{:S(2)}, u32[]{:S(2)}) async-start(bf16[16,64,256]{2,1,0:T(8,128)(2,1)} %bitcast.20), calls=%async_computation.7 | async-start | bytes 1048576 | tf_op jit(solution)/shard_map/all_to_all | solution.py:343
  205.1 4.0 %shard_map.147 = bf16[1024,512]{1,0:T(8,128)(2,1)} custom-call(bf16[512,512]{1,0:T(8,128)(2,1)S(1)} %get-tuple-element.38.d_ref, bf16[1536,512]{1,0:T(8,128)(2,1)S(1)} %copy-done.3, f32[1,512]{1,0:T(1,128)S(1)} %collective-permute-done.3.carried_ref), custom_call_target="tpu_custom_call" | custom-call | flops 1073741824 | bytes 4194304 | tf_op jit(solution)/shard_map/pallas_call | solution.py:417
  210.9 10.7 %all-to-all-done.7 = bf16[16,64,256]{2,1,0:T(8,128)(2,1)S(1)} async-done(((bf16[16,64,256]{2,1,0:T(8,128)(2,1)}), bf16[16,64,256]{2,1,0:T(8,128)(2,1)S(1)}, u32[]{:S(2)}, u32[]{:S(2)}) %all-to-all-start.7) | async-done | bytes 524320 | tf_op jit(solution)/shard_map/all_to_all | solution.py:343
  (69 shorter events, 17.5 us)
Async XLA Ops:
  2.1 16.1 %all-to-all-start = ((bf16[4,32,256]{2,1,0:T(8,128)(2,1)}), bf16[4,32,256]{2,1,0:T(8,128)(2,1)S(1)}, u32[]{:S(2)}, u32[]{:S(2)}) async-start(bf16[4,32,256]{2,1,0:T(8,128)(2,1)} %broadcast_in_dim.22), calls=%async_computation | async-start | bytes 131072 | tf_op jit(solution)/shard_map/all_to_all | solution.py:329
  59.1 31.0 %copy-start = (bf16[16,4,64,256]{3,2,1,0:T(8,128)(2,1)}, bf16[16,4,64,256]{3,2,1,0:T(8,128)(2,1)S(1)}, u32[]{:S(2)}) copy-start(bf16[16,4,64,256]{3,2,1,0:T(8,128)(2,1)S(1)} %all_to_all.41) | copy-start | bytes 6291460
  60.3 15.7 %all-to-all-start.1 = ((bf16[16,4,32,256]{3,2,1,0:T(8,128)(2,1)}), bf16[16,4,32,256]{3,2,1,0:T(8,128)(2,1)S(1)}, u32[]{:S(2)}, u32[]{:S(2)}) async-start(bf16[16,4,32,256]{3,2,1,0:T(8,128)(2,1)} %broadcast_in_dim.23), calls=%async_computation.1 | async-start | bytes 2097152 | tf_op jit(solution)/shard_map/all_to_all | solution.py:330
  64.0 40.6 %collective-permute-start.2 = (bf16[64,64,256]{2,1,0:T(8,128)(2,1)S(1)}, bf16[64,64,256]{2,1,0:T(8,128)(2,1)}, u32[]{:S(2)}, u32[]{:S(2)}) collective-permute-start(bf16[64,64,256]{2,1,0:T(8,128)(2,1)S(1)} %bitcast.54), channel_id=1, source_target_pairs={{0,1},{1,0},{2,3},{3,2},{4,5},{5,4},{6,7},{7,6},{8,9},{9,8},{10,11... | collective-permute-start | bytes 6291464 | tf_op jit(solution)/shard_map/ppermute | solution.py:323
  76.0 16.6 %collective-permute-start.1 = (bf16[64,32,256]{2,1,0:T(8,128)(2,1)S(1)}, bf16[64,32,256]{2,1,0:T(8,128)(2,1)}, u32[]{:S(2)}, u32[]{:S(2)}) collective-permute-start(bf16[64,32,256]{2,1,0:T(8,128)(2,1)S(1)} %bitcast.56), channel_id=1, source_target_pairs={{0,1},{1,0},{2,3},{3,2},{4,5},{5,4},{6,7},{7,6},{8,9},{9,8},{10,11... | collective-permute-start | bytes 3145736 | tf_op jit(solution)/shard_map/ppermute | solution.py:323
  82.9 5.0 %collective-permute-start = (bf16[8,512]{1,0:T(8,128)(2,1)S(1)}, bf16[8,512]{1,0:T(8,128)(2,1)S(1)}, u32[]{:S(2)}, u32[]{:S(2)}) collective-permute-start(bf16[8,512]{1,0:T(8,128)(2,1)S(1)} %slice_bitcast_fusion.6), channel_id=1, source_target_pairs={{1,0},{2,1},{3,2},{5,4},{6,5},{7,6},{9,8},{10,9},{11,10},{13,12},{... | collective-permute-start | bytes 24584 | tf_op jit(solution)/shard_map/ppermute | solution.py:371
  87.9 1.2 copy-start.4
  90.2 0.8 copy-start.5
  91.0 0.8 copy-start.8
  91.8 0.8 copy-start.11
  93.7 10.9 %copy-start.1 = (bf16[16,4,64,256]{3,2,1,0:T(8,128)(2,1)S(1)}, bf16[16,4,64,256]{3,2,1,0:T(8,128)(2,1)}, u32[]{:S(2)}) copy-start(bf16[16,4,64,256]{3,2,1,0:T(8,128)(2,1)} %copy-done) | copy-start | bytes 6291460
  93.7 1.2 copy-start.6
  94.9 1.0 copy-start.9
  95.9 1.0 copy-start.12
  97.0 7.7 %copy-start.14 = (bf16[1,128,1920]{2,1,0:T(8,128)(2,1)S(1)}, bf16[1,128,1920]{2,1,0:T(8,128)(2,1)}, u32[]{:S(2)}) copy-start(bf16[1,128,1920]{2,1,0:T(8,128)(2,1)} %param.15) | copy-start | bytes 1474564
  104.6 15.2 %copy-start.2 = (bf16[1536,512]{1,0:T(8,128)(2,1)}, bf16[1536,512]{1,0:T(8,128)(2,1)S(1)}, u32[]{:S(2)}) copy-start(bf16[1536,512]{1,0:T(8,128)(2,1)S(1)} %get-tuple-element.36.w_ref) | copy-start | bytes 4718596
  104.7 15.1 %copy-start.7 = (bf16[512,512]{1,0:T(8,128)(2,1)S(1)}, bf16[512,512]{1,0:T(8,128)(2,1)}, u32[]{:S(2)}) copy-start(bf16[512,512]{1,0:T(8,128)(2,1)} %copy-done.5) | copy-start | bytes 1572868
  104.7 15.1 %copy-start.10 = (bf16[512,512]{1,0:T(8,128)(2,1)S(1)}, bf16[512,512]{1,0:T(8,128)(2,1)}, u32[]{:S(2)}) copy-start(bf16[512,512]{1,0:T(8,128)(2,1)} %copy-done.8) | copy-start | bytes 1572868
  104.7 15.1 %copy-start.13 = (bf16[512,512]{1,0:T(8,128)(2,1)S(1)}, bf16[512,512]{1,0:T(8,128)(2,1)}, u32[]{:S(2)}) copy-start(bf16[512,512]{1,0:T(8,128)(2,1)} %copy-done.11) | copy-start | bytes 1572868
  119.8 13.0 %collective-permute-start.5 = (bf16[64,64,256]{2,1,0:T(8,128)(2,1)}, bf16[64,64,256]{2,1,0:T(8,128)(2,1)}, u32[]{:S(2)}, u32[]{:S(2)}) collective-permute-start(bf16[64,64,256]{2,1,0:T(8,128)(2,1)} %get-tuple-element.43), channel_id=1, source_target_pairs={{0,1},{1,0},{2,3},{3,2},{4,5},{5,4},{6,7},{7,6},{8,9},{9,8},{10,11... | collective-permute-start | bytes 6291464 | tf_op jit(solution)/shard_map/ppermute | solution.py:323
  124.2 2.9 %collective-permute-start.4 = (bf16[64,32,256]{2,1,0:T(8,128)(2,1)S(1)}, bf16[64,32,256]{2,1,0:T(8,128)(2,1)S(1)}, u32[]{:S(2)}, u32[]{:S(2)}) collective-permute-start(bf16[64,32,256]{2,1,0:T(8,128)(2,1)S(1)} %get-tuple-element.41), channel_id=1, source_target_pairs={{0,1},{1,0},{2,3},{3,2},{4,5},{5,4},{6,7},{7,6},{8,9},{9,8},{10,11... | collective-permute-start | bytes 3145736 | tf_op jit(solution)/shard_map/ppermute | solution.py:323
  128.4 20.9 %all-to-all-start.4 = ((bf16[16,4,32,256]{3,2,1,0:T(8,128)(2,1)}), bf16[16,4,32,256]{3,2,1,0:T(8,128)(2,1)}, u32[]{:S(2)}, u32[]{:S(2)}) async-start(bf16[16,4,32,256]{3,2,1,0:T(8,128)(2,1)} %bitcast.62), calls=%async_computation.4 | async-start | bytes 2097152 | tf_op jit(solution)/shard_map/all_to_all | solution.py:340
  149.4 29.5 %all-to-all-start.6 = ((bf16[16,4,64,256]{3,2,1,0:T(8,128)(2,1)}), bf16[16,4,64,256]{3,2,1,0:T(8,128)(2,1)S(1)}, u32[]{:S(2)}, u32[]{:S(2)}) async-start(bf16[16,4,64,256]{3,2,1,0:T(8,128)(2,1)} %bitcast.61), calls=%async_computation.6 | async-start | bytes 4194304 | tf_op jit(solution)/shard_map/all_to_all | solution.py:340
  178.9 1.4 copy-start.15
  180.3 20.4 %all-to-all-start.5 = ((bf16[16,32,256]{2,1,0:T(8,128)(2,1)}), bf16[16,32,256]{2,1,0:T(8,128)(2,1)S(1)}, u32[]{:S(2)}, u32[]{:S(2)}) async-start(bf16[16,32,256]{2,1,0:T(8,128)(2,1)} %bitcast.15), calls=%async_computation.5 | async-start | bytes 524288 | tf_op jit(solution)/shard_map/all_to_all | solution.py:343
  188.8 16.3 %copy-start.3 = (bf16[1536,512]{1,0:T(8,128)(2,1)S(1)}, bf16[1536,512]{1,0:T(8,128)(2,1)}, u32[]{:S(2)}) copy-start(bf16[1536,512]{1,0:T(8,128)(2,1)} %copy-done.2) | copy-start | bytes 4718596
  188.8 16.3 %collective-permute-start.3 = (f32[1,512]{1,0:T(1,128)S(1)}, f32[1,512]{1,0:T(1,128)S(1)}, u32[]{:S(2)}, u32[]{:S(2)}) collective-permute-start(f32[1,512]{1,0:T(1,128)S(1)} %slice.74), channel_id=1, source_target_pairs={{0,1},{1,2},{2,3},{4,5},{5,6},{6,7},{8,9},{9,10},{10,11},{12,13},{... | collective-permute-start | bytes 6152 | tf_op jit(solution)/shard_map/ppermute | solution.py:416
  201.6 20.0 %all-to-all-start.7 = ((bf16[16,64,256]{2,1,0:T(8,128)(2,1)}), bf16[16,64,256]{2,1,0:T(8,128)(2,1)S(1)}, u32[]{:S(2)}, u32[]{:S(2)}) async-start(bf16[16,64,256]{2,1,0:T(8,128)(2,1)} %bitcast.20), calls=%async_computation.7 | async-start | bytes 1048576 | tf_op jit(solution)/shard_map/all_to_all | solution.py:343
where the time goes:
time: 224 us; the launch traced here: 223 us
  waiting for transfers between devices  69.7 us (31%)
  starting transfers between devices  50.3 us (22%)
  blocking collectives  40.7 us (18%)
  Pallas kernels  32.1 us (14%)
  local copies, waits for them, and re-layouts  16.3 us (7%)
  other arithmetic  12.8 us (6%)
    all_to_all x2, waiting for transfers between devices, reduce(): lax.all_to_all(summed.reshape(16, 4, count, HALF), ('x', 'y'), 0, 0, tile...  36.9 us
    all_to_all x1, blocking collectives, gather(): lax.all_to_all(jnp.broadcast_to(line[None], (16, 4, count, HALF)), ('x',...  31 us
    all_to_all x2, waiting for transfers between devices, reduce(): line = lax.all_to_all(line, ('zh', 'zl', 'core'), 0, 0, tiled=True)  16.9 us
    pallas_call x1, Pallas kernels, shards(): scalar_call(upper_kernel, 6, [((128, WIDTH), bf16), (square, f32), ((16,...  15.1 us
    all_to_all x2, starting transfers between devices, reduce(): line = lax.all_to_all(line, ('zh', 'zl', 'core'), 0, 0, tiled=True)  12 us
    ppermute x4, starting transfers between devices, swap_cores(): return lax.ppermute(value, 'core', [(0, 1), (1, 0)])  11.7 us
    all_to_all x1, blocking collectives, gather(): lax.all_to_all(jnp.broadcast_to(half[None], (4, count, HALF)), 'zh', 0, 0...  9.72 us
    all_to_all x1, starting transfers between devices, gather(): lax.all_to_all(jnp.broadcast_to(half[None], (4, count, HALF)), 'zh', 0, 0...  9.01 us
  transfers between devices with their start and end apart: 12, of which 8 were waited for; matrix products, arithmetic and copies ran while one was open for 7% of the time, Pallas kernels for 8%

commit v1 on v0

v1 whole, which is shorter than its diff:
```python
import jax
import jax.numpy as jnp
from jax import lax
from jax.experimental import pallas as pl
from jax.experimental.pallas import tpu as pltpu
from jax.sharding import Mesh, PartitionSpec as P

epsilon = 1e-05
f32 = jnp.float32
bf16 = jnp.bfloat16
CH = 512
WIDTH = 1920
HALF = 256
STEP = 32
ALL_VMEM = 2**26 - 2**18


def dot(left, right, contract=(1, 0)):
    return lax.dot_general(
        left, right, (((contract[0],), (contract[1],)), ((), ())), preferred_element_type=f32
    )


def staged(body, operands, outs, scratch, flops, moved):
    count, made = len(operands) - 1, len(outs)

    def kernel(place_ref, *refs):
        refs = list(refs)
        groups = []
        for size in (count, made, count, made):
            groups.append(refs[:size])
            refs = refs[size:]
        from_hbm, to_hbm, ins, results = groups
        in_sems, out_sems, *rest = refs
        loads = [pltpu.make_async_copy(a, b, in_sems.at[i]) for i, (a, b) in enumerate(zip(from_hbm, ins))]
        stores = [pltpu.make_async_copy(a, b, out_sems.at[i]) for i, (a, b) in enumerate(zip(results, to_hbm))]
        for load in loads:
            load.start()
        waited, sent = set(), set()

        def need(*which):
            for ref in which:
                index = next(i for i, own in enumerate(ins) if own is ref)
                if index not in waited:
                    waited.add(index)
                    loads[index].wait()

        def give(*which):
            for ref in which:
                index = next(i for i, own in enumerate(results) if own is ref)
                if index not in sent:
                    sent.add(index)
                    stores[index].start()

        body(place_ref, ins, results, rest, need, give)
        need(*ins)
        give(*results)
        for store in stores:
            store.wait()

    hbm = pl.BlockSpec(memory_space=pltpu.HBM)
    return pl.pallas_call(
        kernel,
        out_shape=[jax.ShapeDtypeStruct(shape, kind) for shape, kind in outs],
        in_specs=[pl.BlockSpec(memory_space=pltpu.SMEM)] + [hbm] * count,
        out_specs=[hbm] * made,
        scratch_shapes=[pltpu.VMEM(array.shape, array.dtype) for array in operands[1:]]
        + [pltpu.VMEM(shape, kind) for shape, kind in outs]
        + [pltpu.SemaphoreType.DMA((count,)), pltpu.SemaphoreType.DMA((made,))]
        + [pltpu.VMEM(shape, kind) for shape, kind in scratch],
        compiler_params=pltpu.CompilerParams(vmem_limit_bytes=ALL_VMEM),
        cost_estimate=pl.CostEstimate(flops=flops, bytes_accessed=moved, transcendentals=0),
    )(*operands)


def place(index):
    return (index // 16) * 16 + (index % 4) * 4 + (index // 4) % 4


def rows(index, size):
    return pl.ds(pl.multiple_of(index * size, size), size)


def by_core(core_ref, body):
    @pl.when(core_ref[0] == 0)
    def _():
        body(0, HALF)

    @pl.when(core_ref[0] != 0)
    def _():
        body(HALF, 0)


def row_mean(values):
    return jnp.sum(values, -1, keepdims=True) * (1.0 / CH)


def standard(values):
    centred = values - row_mean(values)
    scale = lax.rsqrt(row_mean(centred * centred) + epsilon)
    return centred * scale, scale


def fold(values):
    return jnp.sum(values.reshape(-1, 8, values.shape[-1]), 0)


def block_forward(pre_ref, cp_ref, first, act_ref, unit_ref, slope_ref, scale_ref):
    offset, gain, shift = (cp_ref[first + i : first + i + 1] for i in range(3))

    def step(i, _):
        at = rows(i, STEP)
        unit, scale = standard(pre_ref[at, :] + offset)
        z = unit * gain + shift
        cdf = 0.5 + 0.5 * lax.erf(z * 0.7071067811865476)
        act_ref[at, :] = (z * cdf).astype(bf16)
        slope_ref[at, :] = cdf + z * (0.3989422804014327 * jnp.exp(-0.5 * z * z))
        unit_ref[at, :] = unit
        scale_ref[at, :] = jnp.broadcast_to(scale, (STEP, 128))
        return 0

    lax.fori_loop(0, pre_ref.shape[0] // STEP, step, 0, unroll=2)


def block_backward(grad_ref, cp_ref, first, unit_ref, slope_ref, scale_ref, out_ref):
    gain = cp_ref[first + 1 : first + 2]

    def step(i, sums):
        at = rows(i, STEP)
        unit = unit_ref[at, :]
        dz = grad_ref[at, :] * slope_ref[at, :]
        dunit = dz * gain
        du = scale_ref[at, :1] * (dunit - row_mean(dunit) - unit * row_mean(dunit * unit))
        out_ref[at, :] = du.astype(bf16)
        return (sums[0] + fold(du), sums[1] + fold(dz * unit), sums[2] + fold(dz))

    zero = jnp.zeros((8, CH), f32)
    return lax.fori_loop(0, grad_ref.shape[0] // STEP, step, (zero, zero, zero), unroll=2)


def total(values):
    return jnp.sum(values, 0, keepdims=True)


def spread(transposed):
    group = lax.broadcasted_iota(jnp.int32, (256, 256), 1 if transposed else 0)
    position = lax.broadcasted_iota(jnp.int32, (256, 256), 0 if transposed else 1)
    return (position == 8 * (group % 32) + group // 32).astype(bf16)


def pack_kernel(place_ref, ins, outs, scratch, need, give):
    w5_ref, w6_ref, w7_ref, wp_ref, cp_ref, bias_ref = ins
    (out_ref,) = outs
    (small_ref,) = scratch
    need(*ins)
    small_ref[...] = jnp.zeros((8, HALF), f32)
    small_ref[:, :11] = cp_ref[...].astype(f32)
    small_ref[:1, 128:158] = bias_ref[...].astype(f32)

    def body(at, _):
        tail = small_ref[...] if at == 0 else jnp.zeros((8, HALF), f32)
        first = jnp.concatenate([w5_ref[:, at : at + HALF].astype(f32), tail], 0).astype(bf16)
        parts = []
        for b in range(4):
            start = 4 * at + HALF * b
            part = wp_ref[:, start : min(start + HALF, WIDTH)].astype(f32)
            if start + HALF > WIDTH:
                part = jnp.concatenate([part, jnp.zeros((8, start + HALF - WIDTH), f32)], 1)
            parts.append(part)
        last = jnp.concatenate(parts, 0).astype(bf16)
        for k in range(4):
            out_ref[k, :32, :] = first
            out_ref[k, 32:48, :] = w6_ref[:, at : at + HALF]
            out_ref[k, 48:64, :] = w7_ref[:, at : at + HALF]
            out_ref[k, 64:, :] = last

    by_core(place_ref, body)


def split_kernel(place_ref, ins, outs, scratch, need, give):
    x_ref, next_ref, line_ref = ins
    even_ref, odd_ref, third_ref, spread_c_ref = outs
    (first_ref,) = scratch
    need(*ins)
    for k in range(16):
        spread_c_ref[k] = line_ref[:, 64:]
    give(spread_c_ref)
    matrix = spread(False)
    for j in range(4):
        groups = dot(matrix, x_ref[256 * j : 256 * j + 256, :])
        first_ref[32 * j : 32 * j + 32, :] = groups[:32]
        groups = groups.astype(bf16)
        for r in range(4):
            at = slice(128 * r + 32 * j, 128 * r + 32 * j + 32)
            even_ref[at, :] = groups[64 * r : 64 * r + 32]
            odd_ref[at, :] = groups[64 * r + 32 : 64 * r + 64]
            if r > 0:
                third_ref[128 * r - 128 + 32 * j : 128 * r - 96 + 32 * j, :] = groups[64 * r : 64 * r + 32]
    later = pltpu.roll(first_ref[...], 127, 0)
    last = lax.broadcasted_iota(jnp.int32, (128, CH), 0) == 127
    third_ref[384:512, :] = jnp.where(last, next_ref[:1, :].astype(f32), later).astype(bf16)


def forward_kernel(core_ref, ins, outs, scratch, need, give):
    mine_ref, other_ref, even_ref, odd_ref, third_ref, cot_ref = ins
    (
        cp_ref, w5_ref, five_ref, unit5_ref, slope5_ref, scale5_ref,
        w6_ref, w7_ref, act6_ref, unit6_ref, slope6_ref, scale6_ref, unit7_ref, slope7_ref, scale7_ref,
        normed_ref, unit_ref, scale_ref, give_ref, send_ref,
    ) = outs
    wide_ref, small_ref, pre5_ref, pre6_ref, pre7_ref, act7_ref, gp_ref = scratch
    need(mine_ref, other_ref)

    def unpack(mine_at, other_at):
        def step(i, _):
            to = place(i)
            for ref, at in ((mine_ref, mine_at), (other_ref, other_at)):
                block = ref[i, :32].astype(f32)
                wide_ref[rows(to, 24), at : at + HALF] = block[:24]
                if at == 0:
                    small_ref[rows(to, 8), :] = block[24:, :128]
                w6_ref[rows(to, 16), at : at + HALF] = ref[i, 32:48]
                w7_ref[rows(to, 16), at : at + HALF] = ref[i, 48:]
            return 0

        lax.fori_loop(0, 64, step, 0, unroll=4)

    by_core(core_ref, unpack)
    cp_ref[...] = small_ref[...].T[:16]

    def narrow(i, _):
        w5_ref[rows(i, 128), :] = wide_ref[rows(i, 128), :].astype(bf16)
        return 0

    lax.fori_loop(0, 12, narrow, 0)
    give(cp_ref, w5_ref, w6_ref, w7_ref)
    need(even_ref, odd_ref, third_ref)

    def multiply(r, _):
        at = rows(r, 128)
        pre5_ref[at, :] = (
            dot(even_ref[at, :], w5_ref[:512, :]) + dot(odd_ref[at, :], w5_ref[512:1024, :])
        ) + dot(third_ref[at, :], w5_ref[1024:, :])
        return 0

    lax.fori_loop(0, 4, multiply, 0)
    block_forward(pre5_ref, cp_ref, 0, five_ref, unit5_ref, slope5_ref, scale5_ref)
    give(five_ref, unit5_ref, slope5_ref, scale5_ref)
    for s in range(2):
        pre6_ref[128 * s : 128 * s + 128, :] = dot(five_ref[256 * s : 256 * s + 128, :], w6_ref[:512, :]) + dot(
            five_ref[256 * s + 128 : 256 * s + 256, :], w6_ref[512:, :]
        )
    block_forward(pre6_ref, cp_ref, 3, act6_ref, unit6_ref, slope6_ref, scale6_ref)
    pre7_ref[...] = dot(act6_ref[:128, :], w7_ref[:512, :]) + dot(act6_ref[128:, :], w7_ref[512:, :])
    block_forward(pre7_ref, cp_ref, 6, act7_ref, unit7_ref, slope7_ref, scale7_ref)

    unit, scale = standard(act7_ref[...].astype(f32))
    normed = (unit * cp_ref[9:10] + cp_ref[10:11]).astype(bf16)
    unit_ref[...] = unit
    scale_ref[...] = jnp.broadcast_to(scale, (128, 128))
    normed_ref[...] = normed
    flipped = normed.astype(f32).T.astype(bf16)
    give(act6_ref, unit6_ref, slope6_ref, scale6_ref, unit7_ref, slope7_ref, scale7_ref)
    need(cot_ref)
    for b in range(8):
        cols = slice(HALF * b, min(HALF * (b + 1), WIDTH))
        gp_ref[:, cols] = dot(flipped, cot_ref[:, cols])
    gp_ref[:, WIDTH:] = jnp.zeros((CH, 8 * HALF - WIDTH), f32)

    def pack(mine_at, other_at):
        def step(i, _):
            to = place(i)
            for ref, at in ((give_ref, mine_at), (send_ref, other_at)):
                block = gp_ref[rows(to, 8), 4 * at : 4 * at + 4 * HALF]
                parts = [block[:, HALF * b : HALF * (b + 1)] for b in range(4)]
                ref[i] = jnp.concatenate(parts, 0).astype(bf16)
            return 0

        lax.fori_loop(0, 64, step, 0, unroll=4)

    by_core(core_ref, pack)


def backward_kernel(core_ref, ins, outs, scratch, need, give):
    (
        mine_ref, other_ref, cp_ref, bias_ref, cot_ref, normed_ref, unit_ref, scale_ref,
        unit7_ref, slope7_ref, scale7_ref, w7_ref, act6_ref, unit6_ref, slope6_ref, scale6_ref, w6_ref, five_ref,
        unit5_ref, slope5_ref, scale5_ref, w5_ref, even_ref, odd_ref, third_ref, gb_ref,
    ) = ins
    out_ref, edge_ref, d5_ref, give_ref, send_ref = outs
    wp_ref, wide_ref, pre5_ref, pre6_ref, pre7_ref, g5_ref, g6_ref, g7_ref, d6_ref, d7_ref, small_ref, sums_ref = scratch
    need(mine_ref, other_ref)

    def unpack(mine_at, other_at):
        def step(i, _):
            to = place(i)
            for ref, at in ((mine_ref, mine_at), (other_ref, other_at)):
                block = ref[i].astype(f32)
                for b in range(4):
                    wide_ref[rows(to, 8), 4 * at + HALF * b : 4 * at + HALF * (b + 1)] = block[8 * b : 8 * b + 8]
            return 0

        lax.fori_loop(0, 64, step, 0, unroll=4)

    by_core(core_ref, unpack)

    def narrow(i, _):
        wp_ref[rows(i, 64), :] = wide_ref[rows(i, 64), :WIDTH].astype(bf16)
        return 0

    lax.fori_loop(0, 8, narrow, 0)
    need(cp_ref, bias_ref, cot_ref, normed_ref)

    normed_grad = jnp.zeros((128, CH), f32)
    for b in range(8):
        cols = slice(HALF * b, min(HALF * (b + 1), WIDTH))
        out_ref[:, cols] = (dot(normed_ref[...], wp_ref[:, cols]) + bias_ref[:, cols]).astype(bf16)
        normed_grad = normed_grad + dot(cot_ref[:, cols], wp_ref[:, cols], (1, 1))

    need(unit_ref, scale_ref, unit7_ref, slope7_ref, scale7_ref)
    give(out_ref)
    unit = unit_ref[...]
    dunit = normed_grad * cp_ref[9:10]
    sums_ref[...] = jnp.zeros((128, CH), f32)
    sums_ref[9:10, :] = total(normed_grad * unit)
    sums_ref[10:11, :] = total(normed_grad)
    pre7_ref[...] = scale_ref[:, :1] * (dunit - row_mean(dunit) - unit * row_mean(dunit * unit))

    for i, part in enumerate(block_backward(pre7_ref, cp_ref, 6, unit7_ref, slope7_ref, scale7_ref, d7_ref)):
        sums_ref[6 + i : 7 + i, :] = total(part)
    need(w7_ref, act6_ref)
    for s in range(2):
        half = slice(512 * s, 512 * s + 512)
        pre6_ref[128 * s : 128 * s + 128, :] = dot(d7_ref[...], w7_ref[half, :], (1, 1))
        g7_ref[half, :] = dot(act6_ref[128 * s : 128 * s + 128, :], d7_ref[...], (0, 0))
    need(unit6_ref, slope6_ref, scale6_ref)
    for i, part in enumerate(block_backward(pre6_ref, cp_ref, 3, unit6_ref, slope6_ref, scale6_ref, d6_ref)):
        sums_ref[3 + i : 4 + i, :] = total(part)
    need(w6_ref, five_ref)
    for r in range(2):
        half = slice(512 * r, 512 * r + 512)
        for s in range(2):
            at = 256 * s + 128 * r
            pre5_ref[at : at + 128, :] = dot(d6_ref[128 * s : 128 * s + 128, :], w6_ref[half, :], (1, 1))
        g6_ref[half, :] = dot(five_ref[128 * r : 128 * r + 128, :], d6_ref[:128, :], (0, 0)) + dot(
            five_ref[256 + 128 * r : 384 + 128 * r, :], d6_ref[128:, :], (0, 0)
        )
    need(unit5_ref, slope5_ref, scale5_ref)
    for i, part in enumerate(block_backward(pre5_ref, cp_ref, 0, unit5_ref, slope5_ref, scale5_ref, d5_ref)):
        sums_ref[i : i + 1, :] = total(part)
    need(*ins)
    give(d5_ref)
    edge_ref[...] = dot(d5_ref[496:512, :], w5_ref[1024:, :], (1, 1))[8:]
    for k, ref in enumerate((even_ref, odd_ref, third_ref)):
        g5_ref[512 * k : 512 * k + 512, :] = dot(ref[...], d5_ref[...], (0, 0))
    small_ref[...] = sums_ref[...].T

    def pack(mine_at, other_at):
        def step(i, _):
            to = place(i)
            for ref, at in ((give_ref, mine_at), (send_ref, other_at)):
                if at == 0:
                    tail = jnp.concatenate([small_ref[rows(to, 8), :], gb_ref[rows(to, 8), :]], 1)
                else:
                    tail = jnp.zeros((8, HALF), f32)
                block = jnp.concatenate([g5_ref[rows(to, 24), at : at + HALF], tail], 0)
                ref[i, :32, :] = block.astype(bf16)
                ref[i, 32:48, :] = g6_ref[rows(to, 16), at : at + HALF].astype(bf16)
                ref[i, 48:, :] = g7_ref[rows(to, 16), at : at + HALF].astype(bf16)
            return 0

        lax.fori_loop(0, 64, step, 0, unroll=4)

    by_core(core_ref, pack)


def input_kernel(place_ref, ins, outs, scratch, need, give):
    d_ref, w_ref, carried_ref = ins
    (out_ref,) = outs
    even_ref, odd_ref, third_ref = scratch
    need(*ins)

    def multiply(r, _):
        at = rows(r, 128)
        d = d_ref[at, :]
        even_ref[at, :] = dot(d, w_ref[:512, :], (1, 1))
        odd_ref[at, :] = dot(d, w_ref[512:1024, :], (1, 1))
        third_ref[at, :] = dot(d, w_ref[1024:, :], (1, 1))
        return 0

    lax.fori_loop(0, 4, multiply, 0)
    earlier = pltpu.roll(third_ref[384:512, :], 1, 0)
    first = lax.broadcasted_iota(jnp.int32, (128, CH), 0) == 0
    even_ref[:128, :] += jnp.where(first, carried_ref[...], earlier)
    even_ref[128:, :] += third_ref[:384, :]
    matrix = spread(True)
    for j in range(4):
        parts = []
        for r in range(4):
            at = slice(128 * r + 32 * j, 128 * r + 32 * j + 32)
            parts += [even_ref[at, :].astype(bf16), odd_ref[at, :].astype(bf16)]
        out_ref[256 * j : 256 * j + 256, :] = dot(matrix, jnp.concatenate(parts, 0)).astype(bf16)


def swap_cores(value):
    return lax.ppermute(value, "core", [(0, 1), (1, 0)])


def together(*values):
    return lax.optimization_barrier(values)


def around(value, axis, size, back):
    return lax.ppermute(value, axis, [(i, (i + back) % size) for i in range(size)])


def across_plane(value, *meanwhile):
    return together(lax.all_to_all(value, ("x", "y"), 0, 0, tiled=True), *meanwhile)


def sum_cores(give, send):
    return (give.astype(f32) + swap_cores(send).astype(f32)).astype(bf16)


def sum_plane(plane):
    return jnp.sum(plane.astype(f32), 0).astype(bf16)


def sum_line(value):
    count = value.shape[1]
    line = jnp.broadcast_to(value[:, None], (4, 4, count, HALF)).reshape(16, count, HALF)
    line = lax.all_to_all(line, ("zh", "zl", "core"), 0, 0, tiled=True)
    return jnp.sum(line.reshape(8, 2, count, HALF).astype(f32), 0)


def sum_line_by_permutes(value, core):
    zh = lax.axis_index("zh")
    pick = lambda k: lax.dynamic_index_in_dim(value, (zh + k) % 4, 0, False)
    parts = [pick(0)] + [around(pick(k), "zh", 4, k) for k in range(1, 4)]
    summed = sum(part.astype(f32) for part in parts)
    summed = summed + lax.ppermute(summed, "zl", [(0, 1), (1, 0)])
    other = swap_cores(summed)
    return jnp.stack([jnp.where(core == 0, summed, other), jnp.where(core == 0, other, summed)])


def proj_rows(halves):
    return halves.reshape(2, 4, 8, HALF).transpose(2, 0, 1, 3).reshape(8, 8 * HALF)[:, :WIDTH]


def shards(features, w_five, w_six, w_seven, channel_params, w_proj, proj_bias, out_cotangent):
    core = lax.axis_index("core")
    place_at = core.astype(jnp.int32).reshape(1)
    inputs, cotangent = features[0], out_cotangent[0]
    square, flat, stack = (512, CH), (512, 128), (64, 32, HALF)

    (packed,) = staged(
        pack_kernel,
        (place_at, w_five, w_six, w_seven, w_proj, channel_params, proj_bias.reshape(1, 30)),
        [((4, 96, HALF), bf16)],
        [((8, HALF), f32)],
        flops=0,
        moved=2**18,
    )
    line = lax.all_to_all(packed, "zh", 0, 0, tiled=True)
    spread_ab = jnp.broadcast_to(line[None, :, :64], (16, 4, 64, HALF))

    line, first_rows, late_cotangent = together(line, inputs[:16], cotangent)
    next_row = lax.ppermute(first_rows, ("zl", "core"), [(1, 0), (2, 1), (3, 2)])
    even, odd, third, spread_c = staged(
        split_kernel,
        (place_at, inputs, next_row, line),
        [(square, bf16)] * 3 + [((16, 4, 32, HALF), bf16)],
        [((128, CH), f32)],
        flops=2**28,
        moved=3 * 2**20,
    )
    grad_bias = jnp.sum(late_cotangent.astype(f32), 0).reshape(64, 1, 30)
    grad_bias = jnp.pad(grad_bias, [(0, 0), (0, 7), (0, 98)]).reshape(512, 128)

    mine_ab, spread_c, even, odd, third, grad_bias = across_plane(spread_ab, spread_c, even, odd, third, grad_bias)
    mine_ab = mine_ab.reshape(64, 64, HALF)
    other_ab = swap_cores(mine_ab)
    bias = jnp.where(core == 0, mine_ab[:, 24, 128:158], other_ab[:, 24, 128:158])
    bias = bias.reshape(4, 4, 4, 30).transpose(0, 2, 1, 3).reshape(1, WIDTH).astype(f32)

    saved = lambda n: [((n, CH), f32), ((n, CH), f32), ((n, 128), f32)]
    pair = lambda n: [((64, n, HALF), bf16)] * 2
    w_shapes = [((1536, CH), bf16), ((1024, CH), bf16), ((1024, CH), bf16)]
    cp, w5, act_five, *saved_five, w6, w7, act_six, u6, s6, r6, u7, s7, r7, normed, unit, scale, give_c, send_c = staged(
        forward_kernel,
        (place_at, mine_ab, other_ab, even, odd, third, cotangent),
        [((16, CH), f32), w_shapes[0], (square, bf16)]
        + saved(512)
        + w_shapes[1:]
        + [((256, CH), bf16)]
        + saved(256)
        + saved(128)
        + [((128, CH), bf16), ((128, CH), f32), ((128, 128), f32)]
        + pair(32),
        [((1536, CH), f32), (flat, f32), (square, f32), ((256, CH), f32), ((128, CH), f32), ((128, CH), bf16)]
        + [((CH, 8 * HALF), f32)],
        flops=2**31,
        moved=16 * 2**20,
    )

    mine_c, give_c, send_c = across_plane(spread_c, give_c, send_c)
    mine_c = mine_c.reshape(stack)
    other_c = swap_cores(mine_c)
    mine_c, cores_c = together(mine_c, sum_cores(give_c, send_c))
    projected, edge, d_five, give_ab, send_ab = staged(
        backward_kernel,
        (place_at, mine_c, other_c, cp, bias, cotangent, normed, unit, scale, u7, s7, r7, w7, act_six)
        + (u6, s6, r6, w6, act_five, *saved_five, w5, even, odd, third, grad_bias),
        [((128, WIDTH), bf16), ((8, CH), f32), (square, bf16)] + pair(64),
        [((CH, WIDTH), bf16), ((CH, 8 * HALF), f32), (square, f32), ((256, CH), f32), ((128, CH), f32)]
        + [((1536, CH), f32), ((1024, CH), f32), ((1024, CH), f32), ((256, CH), bf16), ((128, CH), bf16)]
        + [(flat, f32), ((128, CH), f32)],
        flops=2**31,
        moved=16 * 2**20,
    )

    plane_c, give_ab, send_ab = across_plane(cores_c.reshape(16, 4, 32, HALF), give_ab, send_ab)
    cores_ab, plane_c, d_five = together(sum_cores(give_ab, send_ab), plane_c, d_five)
    carried = lax.ppermute(edge[7:8], ("zl", "core"), [(0, 1), (1, 2), (2, 3)])
    (input_grad,) = staged(
        input_kernel,
        (place_at, d_five, w5, carried),
        [((1024, CH), bf16)],
        [(square, f32)] * 3,
        flops=2**30,
        moved=4 * 2**20,
    )
    sum_c = sum_line_by_permutes(sum_plane(plane_c), core)
    plane_ab, sum_c, input_grad = across_plane(cores_ab.reshape(16, 4, 64, HALF), sum_c, input_grad)
    sum_ab = sum_line(sum_plane(plane_ab))

    joined = lambda halves: jnp.concatenate([halves[0], halves[1]], 1)
    return (
        projected[None],
        input_grad[None],
        joined(sum_ab[:, :24]),
        joined(sum_ab[:, 32:48]),
        joined(sum_ab[:, 48:]),
        sum_ab[0, 24:32, :11],
        proj_rows(sum_c),
        sum_ab[0, 24, 128:158],
    )


def solution(mesh):
    fine = Mesh(mesh.devices.reshape(4, 4, 4, 2, 2), ("x", "zh", "y", "zl", "core"))
    dp, seq = ("x", "zh", "y"), ("zl", "core")
    placed = (
        P(dp, seq, None),
        P(dp, None),
        P(dp, None),
        P(dp, None),
        P(dp, None),
        P(dp, None),
        P(dp),
        P(dp, seq, None),
    )
    return jax.shard_map(
        shards,
        mesh=fine,
        in_specs=placed,
        out_specs=(
            P(dp, seq, None),
            P(dp, seq, None),
            P(dp, None),
            P(dp, None),
            P(dp, None),
            P(dp, None),
            P(dp, None),
            P(dp),
        ),
        check_vma=False,
    )
```

time: 224 us -> 182 us (0.81)
  blocking collectives: 40.7 us -> 17 us
  waiting for transfers between devices: 69.7 us -> 56.2 us
  local copies, waits for them, and re-layouts: 16.3 us -> 8.43 us
  Pallas kernels: 32.1 us -> 36 us
    all_to_all x6 -> x5, waiting for transfers between devices: 65.6 us -> 40.7 us  [the longest x4 24 us: across_plane(): lax.all_to_all(value, ('x', 'y'), 0, 0, tiled=True)]
    all_to_all x2 -> x1, blocking collectives: 40.7 us -> 17 us  [shards(): line = lax.all_to_all(packed, 'zh', 0, 0, tiled=True)]
    ppermute x1 -> x5, starting transfers between devices: 1.91 us -> 11.4 us  [the longest x3 5.28 us: around(): lax.ppermute(value, axis, [(i, (i + back) % size) for i in range(size)])]
    unnamed x35 -> x8, local copies, waits for them, and re-layouts: 9.01 us -> 1.19 us
    all_to_all x6 -> x5, starting transfers between devices: 33 us -> 25.8 us  [the longest x4 20.2 us: across_plane(): lax.all_to_all(value, ('x', 'y'), 0, 0, tiled=True)]
    ppermute x4 -> x5, waiting for transfers between devices: 2.29 us -> 7.96 us  [swap_cores(): return lax.ppermute(value, 'core', [(0, 1), (1, 0)])]
    ppermute x1 -> x5, waiting for transfers between devices: 1.79 us -> 6.89 us  [the longest x3 5.27 us: around(): lax.ppermute(value, axis, [(i, (i + back) % size) for i in range(size)])]
    pallas_call x5, Pallas kernels: 32.1 us -> 36 us  [staged(): pl.pallas_call(kernel, out_shape=[jax.ShapeDtypeStruct(shape, kind) for s...]
  transfers between devices with their start and end apart: 12 -> 16, of which waited for: 8 -> 10; matrix products, arithmetic and copies ran while one was open for 7% -> 5% of each run, Pallas kernels for 8% -> 19%
where the time goes in v1:
time: 182 us; the launch traced here: 181 us
  waiting for transfers between devices  56.2 us (31%)
  starting transfers between devices  50.5 us (28%)
  Pallas kernels  36 us (20%)
  blocking collectives  17 us (9%)
  other arithmetic  12.1 us (7%)
  local copies, waits for them, and re-layouts  8.43 us (5%)
    pallas_call x5, Pallas kernels, staged(): pl.pallas_call(kernel, out_shape=[jax.ShapeDtypeStruct(shape, kind) for s...  36 us
    all_to_all x4, waiting for transfers between devices, across_plane(): lax.all_to_all(value, ('x', 'y'), 0, 0, tiled=True)  24 us
    all_to_all x4, starting transfers between devices, across_plane(): lax.all_to_all(value, ('x', 'y'), 0, 0, tiled=True)  20.2 us
    all_to_all x1, blocking collectives, shards(): line = lax.all_to_all(packed, 'zh', 0, 0, tiled=True)  17 us
    all_to_all x1, waiting for transfers between devices, sum_line(): line = lax.all_to_all(line, ('zh', 'zl', 'core'), 0, 0, tiled=True)  16.7 us
    ppermute x5, starting transfers between devices, swap_cores(): return lax.ppermute(value, 'core', [(0, 1), (1, 0)])  9.11 us
    ppermute x5, waiting for transfers between devices, swap_cores(): return lax.ppermute(value, 'core', [(0, 1), (1, 0)])  7.96 us
    convert_element_type x2, other arithmetic, sum_cores(): return (give.astype(f32) + swap_cores(send).astype(f32)).astype(bf16)  6.3 us
  transfers between devices with their start and end apart: 16, of which 10 were waited for; matrix products, arithmetic and copies ran while one was open for 5% of the time, Pallas kernels for 19%

profile of v1, /device:TPU:1, one launch (start us, length us, event | category | flops | bytes accessed | tf_op | source)
XLA Modules:
  0.0 181.1 jit_solution(10796186185620371706)
XLA Ops:
  0.6 1.6 shard_map.143
  2.2 17.0 %all_to_all.30.refs_2_ = bf16[4,96,256]{2,1,0:T(8,128)(2,1)S(1)} all-to-all(bf16[4,96,256]{2,1,0:T(8,128)(2,1)} %shard_map.143), channel_id=1, replica_groups=mesh['x'=4,'zh'=4,'y'=4,'zl'=2,'core'=2] {'zh'}, dimensions={0} | all-to-all | bytes 393216 | tf_op jit(solution)/shard_map/all_to_all | solution.py:464
  19.2 1.6 broadcast_in_dim.8
  20.8 6.9 %all-to-all-start.1 = ((bf16[16,4,64,256]{3,2,1,0:T(8,128)(2,1)}), bf16[16,4,64,256]{3,2,1,0:T(8,128)(2,1)}, u32[]{:S(2)}, u32[]{:S(2)}) async-start(bf16[16,4,64,256]{3,2,1,0:T(8,128)(2,1)} %broadcast_in_dim.8), calls=%async_computation.1 | async-start | bytes 4194304 | tf_op jit(solution)/shard_map/all_to_all | solution.py:418
  28.7 5.0 %collective-permute-start = (bf16[16,512]{1,0:T(8,128)(2,1)S(1)}, bf16[16,512]{1,0:T(8,128)(2,1)S(1)}, u32[]{:S(2)}, u32[]{:S(2)}) collective-permute-start(bf16[16,512]{1,0:T(8,128)(2,1)S(1)} %slice_bitcast_fusion.6), channel_id=1, source_target_pairs={{1,0},{2,1},{3,2},{5,4},{6,5},{7,6},{9,8},{10,9},{11,10},{13,12},{... | collective-permute-start | bytes 49160 | tf_op jit(solution)/shard_map/ppermute | solution.py:468
  34.4 1.6 collective-permute-done.refs_1_
  36.7 3.2 %shard_map.144 = (bf16[512,512]{1,0:T(8,128)(2,1)}, bf16[512,512]{1,0:T(8,128)(2,1)}, bf16[512,512]{1,0:T(8,128)(2,1)}, bf16[16,4,32,256]{3,2,1,0:T(8,128)(2,1)}) custom-call(s32[1]{0:T(128)} %bitcast.place_ref, bf16[1024,512]{1,0:T(8,128)(2,1)} %bitcast.60, bf16[16,512]{1,0:T(8,128)(2,1)} %copy-done.2, bf16[4,96,256]{2,1,0:T(8,128)(2,1)} %copy-done.1), custom_call_target="tpu_custom_call" | custom-call | flops 268435456 | bytes 3145728 | tf_op jit(solution)/shard_map/pallas_call | solution.py:62
  39.9 13.1 %all-to-all-done.1 = bf16[16,4,64,256]{3,2,1,0:T(8,128)(2,1)} async-done(((bf16[16,4,64,256]{3,2,1,0:T(8,128)(2,1)}), bf16[16,4,64,256]{3,2,1,0:T(8,128)(2,1)}, u32[]{:S(2)}, u32[]{:S(2)}) %all-to-all-start.1) | async-done | bytes 2097184 | tf_op jit(solution)/shard_map/all_to_all | solution.py:418
  53.1 5.7 %collective-permute-start.1 = (bf16[64,64,256]{2,1,0:T(8,128)(2,1)}, bf16[64,64,256]{2,1,0:T(8,128)(2,1)}, u32[]{:S(2)}, u32[]{:S(2)}) collective-permute-start(bf16[64,64,256]{2,1,0:T(8,128)(2,1)} %bitcast.6.refs_0_), channel_id=1, source_target_pairs={{0,1},{1,0},{2,3},{3,2},{4,5},{5,4},{6,7},{7,6},{8,9},{9,8},{10,11... | collective-permute-start | bytes 6291464 | tf_op jit(solution)/shard_map/ppermute | solution.py:406
  58.7 4.3 %all-to-all-start.2 = ((bf16[16,4,32,256]{3,2,1,0:T(8,128)(2,1)}), bf16[16,4,32,256]{3,2,1,0:T(8,128)(2,1)}, u32[]{:S(2)}, u32[]{:S(2)}) async-start(bf16[16,4,32,256]{3,2,1,0:T(8,128)(2,1)} %get-tuple-element.67), calls=%async_computation.2 | async-start | bytes 2097152 | tf_op jit(solution)/shard_map/all_to_all | solution.py:418
  63.1 13.0 %shard_map.145 = (f32[16,512]{1,0:T(8,128)}, bf16[1536,512]{1,0:T(8,128)(2,1)}, bf16[512,512]{1,0:T(8,128)(2,1)}, f32[512,512]{1,0:T(8,128)}, f32[512,512]{1,0:T...) custom-call(s32[1]{0:T(128)} %bitcast.place_ref, ...), custom_call_target="tpu_custom_call" | custom-call | flops 2147483648 | bytes 16777216 | tf_op jit(solution)/shard_map/pallas_call | solution.py:62
  76.1 4.7 %all-to-all-done.2 = bf16[16,4,32,256]{3,2,1,0:T(8,128)(2,1)} async-done(((bf16[16,4,32,256]{3,2,1,0:T(8,128)(2,1)}), bf16[16,4,32,256]{3,2,1,0:T(8,128)(2,1)}, u32[]{:S(2)}, u32[]{:S(2)}) %all-to-all-start.2) | async-done | bytes 1048608 | tf_op jit(solution)/shard_map/all_to_all | solution.py:418
  80.8 1.2 collective-permute-start.2
  82.0 4.0 %collective-permute-done.2 = bf16[64,32,256]{2,1,0:T(8,128)(2,1)S(1)} collective-permute-done((bf16[64,32,256]{2,1,0:T(8,128)(2,1)}, bf16[64,32,256]{2,1,0:T(8,128)(2,1)S(1)}, u32[]{:S(2)}, u32[]{:S(2)}) %collective-permute-start.2) | collective-permute-done | bytes 1048608 | tf_op jit(solution)/shard_map/ppermute | solution.py:406
  85.9 2.6 %add_convert_fusion.1 = bf16[64,32,256]{2,1,0:T(8,128)(2,1)} fusion(bf16[64,32,256]{2,1,0:T(8,128)(2,1)S(1)} %collective-permute-done.2, bf16[64,32,256]{2,1,0:T(8,128)(2,1)} %get-tuple-element.75), kind=kLoop, calls=%fused_computation.1 | loop fusion | flops 2097152 | bytes 3145728 | tf_op jit(solution)/shard_map/convert_element_type | solution.py:422
  88.5 4.3 %all-to-all-start.3 = ((bf16[16,4,32,256]{3,2,1,0:T(8,128)(2,1)}), bf16[16,4,32,256]{3,2,1,0:T(8,128)(2,1)}, u32[]{:S(2)}, u32[]{:S(2)}) async-start(bf16[16,4,32,256]{3,2,1,0:T(8,128)(2,1)} %bitcast.11), calls=%async_computation.3 | async-start | bytes 2097152 | tf_op jit(solution)/shard_map/all_to_all | solution.py:418
  94.6 12.5 %shard_map.146 = (bf16[128,1920]{1,0:T(8,128)(2,1)}, f32[8,512]{1,0:T(8,128)}, bf16[512,512]{1,0:T(8,128)(2,1)}, bf16[64,64,256]{2,1,0:T(8,128)(2,1)}, bf16[64,64,256]{2,1,0:T(8,128)(2,1)}) custom-call(s32[1]{0:T(128)} %bitcast.place_ref, bf16[64,32,256]{2,1,0:T(8,128)(2,1)} %bitcast.7.refs_0_, bf16[64,32,256]{2,1,0:T(8,128)(2,1)} %collective-permute-done.3.refs_1_, ...), custom_call_target="tpu_custom_call" | custom-call | flops 2147483648 | bytes 16777216 | tf_op jit(solution)/shard_map/pallas_call | solution.py:62
  107.2 2.3 %all-to-all-done.3 = bf16[16,4,32,256]{3,2,1,0:T(8,128)(2,1)} async-done(((bf16[16,4,32,256]{3,2,1,0:T(8,128)(2,1)}), bf16[16,4,32,256]{3,2,1,0:T(8,128)(2,1)}, u32[]{:S(2)}, u32[]{:S(2)}) %all-to-all-start.3) | async-done | bytes 1048608 | tf_op jit(solution)/shard_map/all_to_all | solution.py:418
  109.4 2.2 %collective-permute-start.4 = (bf16[64,64,256]{2,1,0:T(8,128)(2,1)}, bf16[64,64,256]{2,1,0:T(8,128)(2,1)S(1)}, u32[]{:S(2)}, u32[]{:S(2)}) collective-permute-start(bf16[64,64,256]{2,1,0:T(8,128)(2,1)} %get-tuple-element.102), channel_id=1, source_target_pairs={{0,1},{1,0},{2,3},{3,2},{4,5},{5,4},{6,7},{7,6},{8,9},{9,8},{10,11... | collective-permute-start | bytes 6291464 | tf_op jit(solution)/shard_map/ppermute | solution.py:406
  111.6 4.0 %collective-permute-done.4 = bf16[64,64,256]{2,1,0:T(8,128)(2,1)S(1)} collective-permute-done((bf16[64,64,256]{2,1,0:T(8,128)(2,1)}, bf16[64,64,256]{2,1,0:T(8,128)(2,1)S(1)}, u32[]{:S(2)}, u32[]{:S(2)}) %collective-permute-start.4) | collective-permute-done | bytes 2097184 | tf_op jit(solution)/shard_map/ppermute | solution.py:406
  115.6 3.7 %add_convert_fusion = bf16[64,64,256]{2,1,0:T(8,128)(2,1)} fusion(bf16[64,64,256]{2,1,0:T(8,128)(2,1)S(1)} %collective-permute-done.4, bf16[64,64,256]{2,1,0:T(8,128)(2,1)} %get-tuple-element.101), kind=kLoop, calls=%fused_computation | loop fusion | flops 4194304 | bytes 6291456 | tf_op jit(solution)/shard_map/convert_element_type | solution.py:422
  119.3 4.6 %all-to-all-start.4 = ((bf16[16,4,64,256]{3,2,1,0:T(8,128)(2,1)}), bf16[16,4,64,256]{3,2,1,0:T(8,128)(2,1)}, u32[]{:S(2)}, u32[]{:S(2)}) async-start(bf16[16,4,64,256]{3,2,1,0:T(8,128)(2,1)} %bitcast.12), calls=%async_computation.4 | async-start | bytes 4194304 | tf_op jit(solution)/shard_map/all_to_all | solution.py:418
  124.0 1.4 reduce_sum.43
  125.7 3.4 %collective-permute-start.7 = (bf16[32,256]{1,0:T(8,128)(2,1)S(1)}, bf16[32,256]{1,0:T(8,128)(2,1)S(1)}, u32[]{:S(2)}, u32[]{:S(2)}) collective-permute-start(bf16[32,256]{1,0:T(8,128)(2,1)S(1)} %get-tuple-element.121), channel_id=1, source_target_pairs={{0,48},{16,0},{32,16},{48,32},{1,49},{17,1},{33,17},{49,33},{2,50}... | collective-permute-start | bytes 49160 | tf_op jit(solution)/shard_map/ppermute | solution.py:414
  129.1 1.6 collective-permute-start.6
  130.7 5.3 %collective-permute-done.6 = bf16[32,256]{1,0:T(8,128)(2,1)S(1)} collective-permute-done((bf16[32,256]{1,0:T(8,128)(2,1)S(1)}, bf16[32,256]{1,0:T(8,128)(2,1)S(1)}, u32[]{:S(2)}, u32[]{:S(2)}) %collective-permute-start.6) | collective-permute-done | bytes 16416 | tf_op jit(solution)/shard_map/ppermute | solution.py:414
  137.8 4.2 %collective-permute-start.10 = (f32[1,512]{1,0:T(1,128)S(1)}, f32[1,512]{1,0:T(1,128)S(1)}, u32[]{:S(2)}, u32[]{:S(2)}) collective-permute-start(f32[1,512]{1,0:T(1,128)S(1)} %slice.59), channel_id=1, source_target_pairs={{0,1},{1,2},{2,3},{4,5},{5,6},{6,7},{8,9},{9,10},{10,11},{12,13},{... | collective-permute-start | bytes 6152 | tf_op jit(solution)/shard_map/ppermute | solution.py:524
  143.3 5.6 %shard_map.147 = bf16[1024,512]{1,0:T(8,128)(2,1)} custom-call(s32[1]{0:T(128)} %bitcast.place_ref, bf16[512,512]{1,0:T(8,128)(2,1)} %get-tuple-element.107.refs_0_, bf16[1536,512]{1,0:T(8,128)(2,1)} %get-tuple-element.95.refs_21_.refs_1_, f32[1,512]{1,0:T(1,128)} %copy-done.3), custom_call_target="tpu_custom_call" | custom-call | flops 1073741824 | bytes 4194304 | tf_op jit(solution)/shard_map/pallas_call | solution.py:62
  149.0 3.9 %all-to-all-done.4 = bf16[16,4,64,256]{3,2,1,0:T(8,128)(2,1)} async-done(((bf16[16,4,64,256]{3,2,1,0:T(8,128)(2,1)}), bf16[16,4,64,256]{3,2,1,0:T(8,128)(2,1)}, u32[]{:S(2)}, u32[]{:S(2)}) %all-to-all-start.4) | async-done | bytes 2097184 | tf_op jit(solution)/shard_map/all_to_all | solution.py:418
  152.9 2.0 %reduce_sum.44 = bf16[4,64,256]{2,1,0:T(8,128)(2,1)S(1)} reduce(bf16[16,4,64,256]{3,2,1,0:T(8,128)(2,1)} %all-to-all-done.4, bf16[]{:T(256)} %constant.50.clone.1), dimensions={0}, to_apply=%region_2.3 | reduce | flops 983040 | bytes 2228226 | tf_op jit(solution)/shard_map/reduce_sum | solution.py:426
  155.8 5.6 %all-to-all-start.5 = ((bf16[16,64,256]{2,1,0:T(8,128)(2,1)}), bf16[16,64,256]{2,1,0:T(8,128)(2,1)S(1)}, u32[]{:S(2)}, u32[]{:S(2)}) async-start(bf16[16,64,256]{2,1,0:T(8,128)(2,1)} %bitcast.20), calls=%async_computation.5 | async-start | bytes 1048576 | tf_op jit(solution)/shard_map/all_to_all | solution.py:432
  161.9 16.7 %all-to-all-done.5 = bf16[16,64,256]{2,1,0:T(8,128)(2,1)S(1)} async-done(((bf16[16,64,256]{2,1,0:T(8,128)(2,1)}), bf16[16,64,256]{2,1,0:T(8,128)(2,1)S(1)}, u32[]{:S(2)}, u32[]{:S(2)}) %all-to-all-start.5) | async-done | bytes 524320 | tf_op jit(solution)/shard_map/all_to_all | solution.py:432
  (42 shorter events, 11.4 us)
Async XLA Ops:
  19.2 1.6 copy-start.1
  20.8 7.7 %copy-start = (bf16[1,128,1920]{2,1,0:T(8,128)(2,1)S(1)}, bf16[1,128,1920]{2,1,0:T(8,128)(2,1)}, u32[]{:S(2)}) copy-start(bf16[1,128,1920]{2,1,0:T(8,128)(2,1)} %param.15) | copy-start | bytes 1474564
  20.8 32.2 %all-to-all-start.1 = ((bf16[16,4,64,256]{3,2,1,0:T(8,128)(2,1)}), bf16[16,4,64,256]{3,2,1,0:T(8,128)(2,1)}, u32[]{:S(2)}, u32[]{:S(2)}) async-start(bf16[16,4,64,256]{3,2,1,0:T(8,128)(2,1)} %broadcast_in_dim.8), calls=%async_computation.1 | async-start | bytes 4194304 | tf_op jit(solution)/shard_map/all_to_all | solution.py:418
  28.7 7.4 %collective-permute-start = (bf16[16,512]{1,0:T(8,128)(2,1)S(1)}, bf16[16,512]{1,0:T(8,128)(2,1)S(1)}, u32[]{:S(2)}, u32[]{:S(2)}) collective-permute-start(bf16[16,512]{1,0:T(8,128)(2,1)S(1)} %slice_bitcast_fusion.6), channel_id=1, source_target_pairs={{1,0},{2,1},{3,2},{5,4},{6,5},{7,6},{9,8},{10,9},{11,10},{13,12},{... | collective-permute-start | bytes 49160 | tf_op jit(solution)/shard_map/ppermute | solution.py:468
  36.1 0.6 copy-start.2
  53.1 10.0 %collective-permute-start.1 = (bf16[64,64,256]{2,1,0:T(8,128)(2,1)}, bf16[64,64,256]{2,1,0:T(8,128)(2,1)}, u32[]{:S(2)}, u32[]{:S(2)}) collective-permute-start(bf16[64,64,256]{2,1,0:T(8,128)(2,1)} %bitcast.6.refs_0_), channel_id=1, source_target_pairs={{0,1},{1,0},{2,3},{3,2},{4,5},{5,4},{6,7},{7,6},{8,9},{9,8},{10,11... | collective-permute-start | bytes 6291464 | tf_op jit(solution)/shard_map/ppermute | solution.py:406
  58.7 22.1 %all-to-all-start.2 = ((bf16[16,4,32,256]{3,2,1,0:T(8,128)(2,1)}), bf16[16,4,32,256]{3,2,1,0:T(8,128)(2,1)}, u32[]{:S(2)}, u32[]{:S(2)}) async-start(bf16[16,4,32,256]{3,2,1,0:T(8,128)(2,1)} %get-tuple-element.67), calls=%async_computation.2 | async-start | bytes 2097152 | tf_op jit(solution)/shard_map/all_to_all | solution.py:418
  80.8 5.1 %collective-permute-start.2 = (bf16[64,32,256]{2,1,0:T(8,128)(2,1)}, bf16[64,32,256]{2,1,0:T(8,128)(2,1)S(1)}, u32[]{:S(2)}, u32[]{:S(2)}) collective-permute-start(bf16[64,32,256]{2,1,0:T(8,128)(2,1)} %get-tuple-element.76), channel_id=1, source_target_pairs={{0,1},{1,0},{2,3},{3,2},{4,5},{5,4},{6,7},{7,6},{8,9},{9,8},{10,11... | collective-permute-start | bytes 3145736 | tf_op jit(solution)/shard_map/ppermute | solution.py:406
  82.0 12.7 %collective-permute-start.3 = (bf16[64,32,256]{2,1,0:T(8,128)(2,1)}, bf16[64,32,256]{2,1,0:T(8,128)(2,1)}, u32[]{:S(2)}, u32[]{:S(2)}) collective-permute-start(bf16[64,32,256]{2,1,0:T(8,128)(2,1)} %bitcast.7.refs_0_), channel_id=1, source_target_pairs={{0,1},{1,0},{2,3},{3,2},{4,5},{5,4},{6,7},{7,6},{8,9},{9,8},{10,11... | collective-permute-start | bytes 3145736 | tf_op jit(solution)/shard_map/ppermute | solution.py:406
  88.5 20.9 %all-to-all-start.3 = ((bf16[16,4,32,256]{3,2,1,0:T(8,128)(2,1)}), bf16[16,4,32,256]{3,2,1,0:T(8,128)(2,1)}, u32[]{:S(2)}, u32[]{:S(2)}) async-start(bf16[16,4,32,256]{3,2,1,0:T(8,128)(2,1)} %bitcast.11), calls=%async_computation.3 | async-start | bytes 2097152 | tf_op jit(solution)/shard_map/all_to_all | solution.py:418
  109.4 6.2 %collective-permute-start.4 = (bf16[64,64,256]{2,1,0:T(8,128)(2,1)}, bf16[64,64,256]{2,1,0:T(8,128)(2,1)S(1)}, u32[]{:S(2)}, u32[]{:S(2)}) collective-permute-start(bf16[64,64,256]{2,1,0:T(8,128)(2,1)} %get-tuple-element.102), channel_id=1, source_target_pairs={{0,1},{1,0},{2,3},{3,2},{4,5},{5,4},{6,7},{7,6},{8,9},{9,8},{10,11... | collective-permute-start | bytes 6291464 | tf_op jit(solution)/shard_map/ppermute | solution.py:406
  119.3 33.6 %all-to-all-start.4 = ((bf16[16,4,64,256]{3,2,1,0:T(8,128)(2,1)}), bf16[16,4,64,256]{3,2,1,0:T(8,128)(2,1)}, u32[]{:S(2)}, u32[]{:S(2)}) async-start(bf16[16,4,64,256]{3,2,1,0:T(8,128)(2,1)} %bitcast.12), calls=%async_computation.4 | async-start | bytes 4194304 | tf_op jit(solution)/shard_map/all_to_all | solution.py:418
  125.4 5.3 %collective-permute-start.5 = (bf16[32,256]{1,0:T(8,128)(2,1)S(1)}, bf16[32,256]{1,0:T(8,128)(2,1)S(1)}, u32[]{:S(2)}, u32[]{:S(2)}) collective-permute-start(bf16[32,256]{1,0:T(8,128)(2,1)S(1)} %get-tuple-element.120), channel_id=1, source_target_pairs={{0,16},{16,32},{32,48},{48,0},{1,17},{17,33},{33,49},{49,1},{2,18}... | collective-permute-start | bytes 49160 | tf_op jit(solution)/shard_map/ppermute | solution.py:414
  125.7 5.0 %collective-permute-start.7 = (bf16[32,256]{1,0:T(8,128)(2,1)S(1)}, bf16[32,256]{1,0:T(8,128)(2,1)S(1)}, u32[]{:S(2)}, u32[]{:S(2)}) collective-permute-start(bf16[32,256]{1,0:T(8,128)(2,1)S(1)} %get-tuple-element.121), channel_id=1, source_target_pairs={{0,48},{16,0},{32,16},{48,32},{1,49},{17,1},{33,17},{49,33},{2,50}... | collective-permute-start | bytes 49160 | tf_op jit(solution)/shard_map/ppermute | solution.py:414
  129.1 6.9 %collective-permute-start.6 = (bf16[32,256]{1,0:T(8,128)(2,1)S(1)}, bf16[32,256]{1,0:T(8,128)(2,1)S(1)}, u32[]{:S(2)}, u32[]{:S(2)}) collective-permute-start(bf16[32,256]{1,0:T(8,128)(2,1)S(1)} %get-tuple-element.122), channel_id=1, source_target_pairs={{0,32},{16,48},{32,0},{48,16},{1,33},{17,49},{33,1},{49,17},{2,34}... | collective-permute-start | bytes 49160 | tf_op jit(solution)/shard_map/ppermute | solution.py:414
  136.0 6.0 %collective-permute-start.8 = (f32[32,256]{1,0:T(8,128)S(1)}, f32[32,256]{1,0:T(8,128)S(1)}, u32[]{:S(2)}, u32[]{:S(2)}) collective-permute-start(f32[32,256]{1,0:T(8,128)S(1)} %fusion.2), channel_id=1, source_target_pairs={{0,2},{2,0},{1,3},{3,1},{4,6},{6,4},{5,7},{7,5},{8,10},{10,8},{9,1... | collective-permute-start | bytes 98312 | tf_op jit(solution)/shard_map/ppermute | solution.py:441
  137.8 4.9 %collective-permute-start.10 = (f32[1,512]{1,0:T(1,128)S(1)}, f32[1,512]{1,0:T(1,128)S(1)}, u32[]{:S(2)}, u32[]{:S(2)}) collective-permute-start(f32[1,512]{1,0:T(1,128)S(1)} %slice.59), channel_id=1, source_target_pairs={{0,1},{1,2},{2,3},{4,5},{5,6},{6,7},{8,9},{9,10},{10,11},{12,13},{... | collective-permute-start | bytes 6152 | tf_op jit(solution)/shard_map/ppermute | solution.py:524
  142.0 6.9 %collective-permute-start.9 = (f32[32,256]{1,0:T(8,128)S(1)}, f32[32,256]{1,0:T(8,128)S(1)}, u32[]{:S(2)}, u32[]{:S(2)}) collective-permute-start(f32[32,256]{1,0:T(8,128)S(1)} %add.71), channel_id=1, source_target_pairs={{0,1},{1,0},{2,3},{3,2},{4,5},{5,4},{6,7},{7,6},{8,9},{9,8},{10,11... | collective-permute-start | bytes 98312 | tf_op jit(solution)/shard_map/ppermute | solution.py:406
  142.7 0.6 copy-start.3
  155.8 22.9 %all-to-all-start.5 = ((bf16[16,64,256]{2,1,0:T(8,128)(2,1)}), bf16[16,64,256]{2,1,0:T(8,128)(2,1)S(1)}, u32[]{:S(2)}, u32[]{:S(2)}) async-start(bf16[16,64,256]{2,1,0:T(8,128)(2,1)} %bitcast.20), calls=%async_computation.5 | async-start | bytes 1048576 | tf_op jit(solution)/shard_map/all_to_all | solution.py:432

commit v2 on v1

--- a/solution.py
+++ b/solution.py
@@ -402,6 +402,23 @@
         out_ref[256 * j : 256 * j + 256, :] = dot(matrix, jnp.concatenate(parts, 0)).astype(bf16)
 
 
+def finish_kernel(core_ref, ins, outs, scratch, need, give):
+    mine_ref, other_ref = ins
+    g5_ref, g6_ref, g7_ref, channel_ref, bias_ref = outs
+    need(*ins)
+
+    def body(mine_at, other_at):
+        for ref, at in ((mine_ref, mine_at), (other_ref, other_at)):
+            g5_ref[:, at : at + HALF] = ref[:24, :]
+            g6_ref[:, at : at + HALF] = ref[32:48, :]
+            g7_ref[:, at : at + HALF] = ref[48:, :]
+            if at == 0:
+                channel_ref[...] = ref[24:32, :11]
+                bias_ref[...] = ref[24:25, 128:158]
+
+    by_core(core_ref, body)
+
+
 def swap_cores(value):
     return lax.ppermute(value, "core", [(0, 1), (1, 0)])
 
@@ -418,19 +435,58 @@
     return together(lax.all_to_all(value, ("x", "y"), 0, 0, tiled=True), *meanwhile)
 
 
+def add_kernel(a_ref, b_ref, out_ref, a, b, both, a_sems, b_sems, out_sems):
+    size = a_ref.shape[0] // 4
+    parts = [pl.ds(size * k, size) for k in range(4)]
+    loads = []
+    for k, part in enumerate(parts):
+        loads.append(pltpu.make_async_copy(a_ref.at[part], a.at[part], a_sems.at[k]))
+        loads.append(pltpu.make_async_copy(b_ref.at[part], b.at[part], b_sems.at[k]))
+    stores = [pltpu.make_async_copy(both.at[part], out_ref.at[part], out_sems.at[k]) for k, part in enumerate(parts)]
+    for load in loads:
+        load.start()
+    for k, store in enumerate(stores):
+        loads[2 * k].wait()
+        loads[2 * k + 1].wait()
+
+        def step(i, _, k=k):
+            at = size * k + i
+            both[at] = (a[at].astype(f32) + b[at].astype(f32)).astype(bf16)
+            return 0
+
+        lax.fori_loop(0, size, step, 0, unroll=4)
+        store.start()
+    for store in stores:
+        store.wait()
+
+
 def sum_cores(give, send):
-    return (give.astype(f32) + swap_cores(send).astype(f32)).astype(bf16)
+    hbm = pl.BlockSpec(memory_space=pltpu.HBM)
+    return pl.pallas_call(
+        add_kernel,
+        out_shape=jax.ShapeDtypeStruct(give.shape, bf16),
+        in_specs=[hbm, hbm],
+        out_specs=hbm,
+        scratch_shapes=[pltpu.VMEM(give.shape, bf16)] * 3 + [pltpu.SemaphoreType.DMA((4,))] * 3,
+        compiler_params=pltpu.CompilerParams(vmem_limit_bytes=ALL_VMEM),
+        cost_estimate=pl.CostEstimate(flops=2**20, bytes_accessed=6 * 2**20, transcendentals=0),
+    )(give, swap_cores(send))
 
 
 def sum_plane(plane):
     return jnp.sum(plane.astype(f32), 0).astype(bf16)
 
 
+def both_halves(summed, core):
+    other = swap_cores(summed)
+    return jnp.stack([jnp.where(core == 0, summed, other), jnp.where(core == 0, other, summed)])
+
+
 def sum_line(value):
     count = value.shape[1]
-    line = jnp.broadcast_to(value[:, None], (4, 4, count, HALF)).reshape(16, count, HALF)
-    line = lax.all_to_all(line, ("zh", "zl", "core"), 0, 0, tiled=True)
-    return jnp.sum(line.reshape(8, 2, count, HALF).astype(f32), 0)
+    line = jnp.broadcast_to(value[:, None], (4, 2, count, HALF)).reshape(8, count, HALF)
+    line = lax.all_to_all(line, ("zh", "zl"), 0, 0, tiled=True)
+    return jnp.sum(line.astype(f32), 0)
 
 
 def sum_line_by_permutes(value, core):
@@ -439,8 +495,7 @@
     parts = [pick(0)] + [around(pick(k), "zh", 4, k) for k in range(1, 4)]
     summed = sum(part.astype(f32) for part in parts)
     summed = summed + lax.ppermute(summed, "zl", [(0, 1), (1, 0)])
-    other = swap_cores(summed)
-    return jnp.stack([jnp.where(core == 0, summed, other), jnp.where(core == 0, other, summed)])
+    return both_halves(summed, core)
 
 
 def proj_rows(halves):
@@ -503,7 +558,7 @@
         moved=16 * 2**20,
     )
 
-    mine_c, give_c, send_c = across_plane(spread_c, give_c, send_c)
+    (mine_c,) = across_plane(spread_c)
     mine_c = mine_c.reshape(stack)
     other_c = swap_cores(mine_c)
     mine_c, cores_c = together(mine_c, sum_cores(give_c, send_c))
@@ -531,19 +586,27 @@
         moved=4 * 2**20,
     )
     sum_c = sum_line_by_permutes(sum_plane(plane_c), core)
-    plane_ab, sum_c, input_grad = across_plane(cores_ab.reshape(16, 4, 64, HALF), sum_c, input_grad)
+    grad_proj = proj_rows(sum_c)
+    plane_ab, grad_proj, input_grad = across_plane(cores_ab.reshape(16, 4, 64, HALF), grad_proj, input_grad)
     sum_ab = sum_line(sum_plane(plane_ab))
-
-    joined = lambda halves: jnp.concatenate([halves[0], halves[1]], 1)
+    grad_five, grad_six, grad_seven, grad_channel, grad_bias = staged(
+        finish_kernel,
+        (place_at, sum_ab, swap_cores(sum_ab)),
+        [((24, CH), f32), ((16, CH), f32), ((16, CH), f32), ((8, 11), f32), ((1, 30), f32)],
+        [],
+        flops=0,
+        moved=2**18,
+    )
+
     return (
         projected[None],
         input_grad[None],
-        joined(sum_ab[:, :24]),
-        joined(sum_ab[:, 32:48]),
-        joined(sum_ab[:, 48:]),
-        sum_ab[0, 24:32, :11],
-        proj_rows(sum_c),
-        sum_ab[0, 24, 128:158],
+        grad_five,
+        grad_six,
+        grad_seven,
+        grad_channel,
+        grad_proj,
+        grad_bias.reshape(30),
     )
 
 

time: 182 us -> 171 us (0.940)
  waiting for transfers between devices: 56.2 us -> 36.1 us
  blocking collectives: 17 us -> 29.8 us
  other arithmetic: 12.1 us -> 4.56 us
  Pallas kernels: 36 us -> 43.1 us
  starting transfers between devices: 50.5 us -> 48.2 us
    all_to_all x1 -> x0, waiting for transfers between devices: 16.7 us -> none  [sum_line(): line = lax.all_to_all(line, ('zh', 'zl', 'core'), 0, 0, tiled=True)]
    all_to_all x0 -> x1, blocking collectives: none -> 12.8 us  [sum_line(): line = lax.all_to_all(line, ('zh', 'zl'), 0, 0, tiled=True)]
    convert_element_type x2 -> x0, other arithmetic: 6.3 us -> none  [sum_cores(): return (give.astype(f32) + swap_cores(send).astype(f32)).astype(bf16)]
    all_to_all x1 -> x0, starting transfers between devices: 5.56 us -> none  [sum_line(): line = lax.all_to_all(line, ('zh', 'zl', 'core'), 0, 0, tiled=True)]
    pallas_call x0 -> x2, Pallas kernels: none -> 5.55 us  [sum_cores(): pl.pallas_call(add_kernel, out_shape=jax.ShapeDtypeStruct(give.shape, bf1...]
    ppermute x5 -> x6, starting transfers between devices: 9.11 us -> 12.2 us  [swap_cores(): return lax.ppermute(value, 'core', [(0, 1), (1, 0)])]
    ppermute x5 -> x6, waiting for transfers between devices: 7.96 us -> 5.04 us  [swap_cores(): return lax.ppermute(value, 'core', [(0, 1), (1, 0)])]
    ppermute x3, waiting for transfers between devices: 5.27 us -> 2.85 us  [around(): lax.ppermute(value, axis, [(i, (i + back) % size) for i in range(size)])]
  transfers between devices with their start and end apart: 16 -> 16, of which waited for: 10 -> 10; matrix products, arithmetic and copies ran while one was open for 5% -> 4% of each run, Pallas kernels for 19% -> 22%
where the time goes in v2:
time: 171 us; the launch traced here: 170 us
  starting transfers between devices  48.2 us (28%)
  Pallas kernels  43.1 us (25%)
  waiting for transfers between devices  36.1 us (21%)
  blocking collectives  29.8 us (17%)
  local copies, waits for them, and re-layouts  7.12 us (4%)
  other arithmetic  4.56 us (3%)
    pallas_call x6, Pallas kernels, staged(): pl.pallas_call(kernel, out_shape=[jax.ShapeDtypeStruct(shape, kind) for s...  37.6 us
    all_to_all x4, waiting for transfers between devices, across_plane(): lax.all_to_all(value, ('x', 'y'), 0, 0, tiled=True)  26.3 us
    all_to_all x4, starting transfers between devices, across_plane(): lax.all_to_all(value, ('x', 'y'), 0, 0, tiled=True)  20.1 us
    all_to_all x1, blocking collectives, shards(): line = lax.all_to_all(packed, 'zh', 0, 0, tiled=True)  17 us
    all_to_all x1, blocking collectives, sum_line(): line = lax.all_to_all(line, ('zh', 'zl'), 0, 0, tiled=True)  12.8 us
    ppermute x6, starting transfers between devices, swap_cores(): return lax.ppermute(value, 'core', [(0, 1), (1, 0)])  12.2 us
    ppermute x3, starting transfers between devices, around(): lax.ppermute(value, axis, [(i, (i + back) % size) for i in range(size)])  5.69 us
    pallas_call x2, Pallas kernels, sum_cores(): pl.pallas_call(add_kernel, out_shape=jax.ShapeDtypeStruct(give.shape, bf1...  5.55 us
  transfers between devices with their start and end apart: 16, of which 10 were waited for; matrix products, arithmetic and copies ran while one was open for 4% of the time, Pallas kernels for 22%

profile of v2, /device:TPU:1, one launch (start us, length us, event | category | flops | bytes accessed | tf_op | source)
XLA Modules:
  0.0 170.0 jit_solution(666088410952162836)
XLA Ops:
  0.6 1.6 shard_map.143
  2.2 17.0 %all_to_all.30.refs_2_ = bf16[4,96,256]{2,1,0:T(8,128)(2,1)S(1)} all-to-all(bf16[4,96,256]{2,1,0:T(8,128)(2,1)} %shard_map.143), channel_id=1, replica_groups=mesh['x'=4,'zh'=4,'y'=4,'zl'=2,'core'=2] {'zh'}, dimensions={0} | all-to-all | bytes 393216 | tf_op jit(solution)/shard_map/all_to_all | solution.py:519
  19.2 1.6 broadcast_in_dim.8
  20.8 6.9 %all-to-all-start.1 = ((bf16[16,4,64,256]{3,2,1,0:T(8,128)(2,1)}), bf16[16,4,64,256]{3,2,1,0:T(8,128)(2,1)}, u32[]{:S(2)}, u32[]{:S(2)}) async-start(bf16[16,4,64,256]{3,2,1,0:T(8,128)(2,1)} %broadcast_in_dim.8), calls=%async_computation.1 | async-start | bytes 4194304 | tf_op jit(solution)/shard_map/all_to_all | solution.py:435
  28.5 5.0 %collective-permute-start = (bf16[16,512]{1,0:T(8,128)(2,1)S(1)}, bf16[16,512]{1,0:T(8,128)(2,1)S(1)}, u32[]{:S(2)}, u32[]{:S(2)}) collective-permute-start(bf16[16,512]{1,0:T(8,128)(2,1)S(1)} %slice_bitcast_fusion), channel_id=1, source_target_pairs={{1,0},{2,1},{3,2},{5,4},{6,5},{7,6},{9,8},{10,9},{11,10},{13,12},{... | collective-permute-start | bytes 49160 | tf_op jit(solution)/shard_map/ppermute | solution.py:523
  34.4 1.4 collective-permute-done.refs_1_
  36.4 3.2 %shard_map.144 = (bf16[512,512]{1,0:T(8,128)(2,1)}, bf16[512,512]{1,0:T(8,128)(2,1)}, bf16[512,512]{1,0:T(8,128)(2,1)}, bf16[16,4,32,256]{3,2,1,0:T(8,128)(2,1)}) custom-call(s32[1]{0:T(128)} %bitcast.place_ref, bf16[1024,512]{1,0:T(8,128)(2,1)} %bitcast.42, bf16[16,512]{1,0:T(8,128)(2,1)} %copy-done.4, bf16[4,96,256]{2,1,0:T(8,128)(2,1)} %copy-done.1), custom_call_target="tpu_custom_call" | custom-call | flops 268435456 | bytes 3145728 | tf_op jit(solution)/shard_map/pallas_call | solution.py:62
  39.7 13.4 %all-to-all-done.1 = bf16[16,4,64,256]{3,2,1,0:T(8,128)(2,1)} async-done(((bf16[16,4,64,256]{3,2,1,0:T(8,128)(2,1)}), bf16[16,4,64,256]{3,2,1,0:T(8,128)(2,1)}, u32[]{:S(2)}, u32[]{:S(2)}) %all-to-all-start.1) | async-done | bytes 2097184 | tf_op jit(solution)/shard_map/all_to_all | solution.py:435
  53.1 5.7 %collective-permute-start.1 = (bf16[64,64,256]{2,1,0:T(8,128)(2,1)}, bf16[64,64,256]{2,1,0:T(8,128)(2,1)}, u32[]{:S(2)}, u32[]{:S(2)}) collective-permute-start(bf16[64,64,256]{2,1,0:T(8,128)(2,1)} %bitcast.7.refs_0_), channel_id=1, source_target_pairs={{0,1},{1,0},{2,3},{3,2},{4,5},{5,4},{6,7},{7,6},{8,9},{9,8},{10,11... | collective-permute-start | bytes 6291464 | tf_op jit(solution)/shard_map/ppermute | solution.py:423
  58.7 4.3 %all-to-all-start.2 = ((bf16[16,4,32,256]{3,2,1,0:T(8,128)(2,1)}), bf16[16,4,32,256]{3,2,1,0:T(8,128)(2,1)}, u32[]{:S(2)}, u32[]{:S(2)}) async-start(bf16[16,4,32,256]{3,2,1,0:T(8,128)(2,1)} %get-tuple-element.69), calls=%async_computation.2 | async-start | bytes 2097152 | tf_op jit(solution)/shard_map/all_to_all | solution.py:435
  63.1 13.0 %shard_map.145 = (f32[16,512]{1,0:T(8,128)}, bf16[1536,512]{1,0:T(8,128)(2,1)}, bf16[512,512]{1,0:T(8,128)(2,1)}, f32[512,512]{1,0:T(8,128)}, f32[512,512]{1,0:T...) custom-call(s32[1]{0:T(128)} %bitcast.place_ref, ...), custom_call_target="tpu_custom_call" | custom-call | flops 2147483648 | bytes 16777216 | tf_op jit(solution)/shard_map/pallas_call | solution.py:62
  76.4 4.5 %all-to-all-done.2 = bf16[16,4,32,256]{3,2,1,0:T(8,128)(2,1)} async-done(((bf16[16,4,32,256]{3,2,1,0:T(8,128)(2,1)}), bf16[16,4,32,256]{3,2,1,0:T(8,128)(2,1)}, u32[]{:S(2)}, u32[]{:S(2)}) %all-to-all-start.2) | async-done | bytes 1048608 | tf_op jit(solution)/shard_map/all_to_all | solution.py:435
  82.0 2.4 %shard_map.146 = bf16[64,32,256]{2,1,0:T(8,128)(2,1)} custom-call(bf16[64,32,256]{2,1,0:T(8,128)(2,1)} %get-tuple-element.74.a_ref, bf16[64,32,256]{2,1,0:T(8,128)(2,1)} %collective-permute-done.2.b_ref), custom_call_target="tpu_custom_call" | custom-call | flops 1048576 | bytes 6291456 | tf_op jit(solution)/shard_map/pallas_call | solution.py:465
  84.4 4.4 %all-to-all-start.3 = ((bf16[16,4,32,256]{3,2,1,0:T(8,128)(2,1)}), bf16[16,4,32,256]{3,2,1,0:T(8,128)(2,1)}, u32[]{:S(2)}, u32[]{:S(2)}) async-start(bf16[16,4,32,256]{3,2,1,0:T(8,128)(2,1)} %bitcast.38), calls=%async_computation.3 | async-start | bytes 2097152 | tf_op jit(solution)/shard_map/all_to_all | solution.py:435
  90.5 12.5 %shard_map.147 = (bf16[128,1920]{1,0:T(8,128)(2,1)}, f32[8,512]{1,0:T(8,128)}, bf16[512,512]{1,0:T(8,128)(2,1)}, bf16[64,64,256]{2,1,0:T(8,128)(2,1)}, bf16[64,64,256]{2,1,0:T(8,128)(2,1)}) custom-call(s32[1]{0:T(128)} %bitcast.place_ref, bf16[64,32,256]{2,1,0:T(8,128)(2,1)} %bitcast.6.refs_0_, bf16[64,32,256]{2,1,0:T(8,128)(2,1)} %collective-permute-done.3.refs_1_, ...), custom_call_target="tpu_custom_call" | custom-call | flops 2147483648 | bytes 16777216 | tf_op jit(solution)/shard_map/pallas_call | solution.py:62
  103.0 2.9 %all-to-all-done.3 = bf16[16,4,32,256]{3,2,1,0:T(8,128)(2,1)} async-done(((bf16[16,4,32,256]{3,2,1,0:T(8,128)(2,1)}), bf16[16,4,32,256]{3,2,1,0:T(8,128)(2,1)}, u32[]{:S(2)}, u32[]{:S(2)}) %all-to-all-start.3) | async-done | bytes 1048608 | tf_op jit(solution)/shard_map/all_to_all | solution.py:435
  105.9 1.6 collective-permute-start.4
  107.5 4.1 %collective-permute-done.4.b_ref = bf16[64,64,256]{2,1,0:T(8,128)(2,1)} collective-permute-done((bf16[64,64,256]{2,1,0:T(8,128)(2,1)}, bf16[64,64,256]{2,1,0:T(8,128)(2,1)}, u32[]{:S(2)}, u32[]{:S(2)}) %collective-permute-start.4) | collective-permute-done | bytes 2097184 | tf_op jit(solution)/shard_map/ppermute | solution.py:423
  111.6 3.2 %shard_map.148 = bf16[64,64,256]{2,1,0:T(8,128)(2,1)} custom-call(bf16[64,64,256]{2,1,0:T(8,128)(2,1)} %get-tuple-element.100.a_ref, bf16[64,64,256]{2,1,0:T(8,128)(2,1)} %collective-permute-done.4.b_ref), custom_call_target="tpu_custom_call" | custom-call | flops 1048576 | bytes 6291456 | tf_op jit(solution)/shard_map/pallas_call | solution.py:465
  114.8 4.4 %all-to-all-start.4 = ((bf16[16,4,64,256]{3,2,1,0:T(8,128)(2,1)}), bf16[16,4,64,256]{3,2,1,0:T(8,128)(2,1)}, u32[]{:S(2)}, u32[]{:S(2)}) async-start(bf16[16,4,64,256]{3,2,1,0:T(8,128)(2,1)} %bitcast.37), calls=%async_computation.4 | async-start | bytes 4194304 | tf_op jit(solution)/shard_map/all_to_all | solution.py:435
  119.3 1.4 reduce_sum.43
  121.4 3.6 %collective-permute-start.6 = (bf16[32,256]{1,0:T(8,128)(2,1)S(1)}, bf16[32,256]{1,0:T(8,128)(2,1)S(1)}, u32[]{:S(2)}, u32[]{:S(2)}) collective-permute-start(bf16[32,256]{1,0:T(8,128)(2,1)S(1)} %get-tuple-element.120), channel_id=1, source_target_pairs={{0,32},{16,48},{32,0},{48,16},{1,33},{17,49},{33,1},{49,17},{2,34}... | collective-permute-start | bytes 49160 | tf_op jit(solution)/shard_map/ppermute | solution.py:431
  125.0 1.4 collective-permute-start.7
  126.4 1.5 collective-permute-done.6
  127.9 1.3 collective-permute-done.7
  131.0 4.2 %collective-permute-start.10 = (f32[1,512]{1,0:T(1,128)S(1)}, f32[1,512]{1,0:T(1,128)S(1)}, u32[]{:S(2)}, u32[]{:S(2)}) collective-permute-start(f32[1,512]{1,0:T(1,128)S(1)} %slice.27), channel_id=1, source_target_pairs={{0,1},{1,2},{2,3},{4,5},{5,6},{6,7},{8,9},{9,10},{10,11},{12,13},{... | collective-permute-start | bytes 6152 | tf_op jit(solution)/shard_map/ppermute | solution.py:579
  136.5 5.6 %shard_map.149 = bf16[1024,512]{1,0:T(8,128)(2,1)} custom-call(s32[1]{0:T(128)} %bitcast.place_ref, bf16[512,512]{1,0:T(8,128)(2,1)} %get-tuple-element.106.refs_0_, bf16[1536,512]{1,0:T(8,128)(2,1)} %get-tuple-element.94.refs_21_.refs_1_, f32[1,512]{1,0:T(1,128)} %copy-done.5), custom_call_target="tpu_custom_call" | custom-call | flops 1073741824 | bytes 4194304 | tf_op jit(solution)/shard_map/pallas_call | solution.py:62
  142.8 5.6 %all-to-all-done.4 = bf16[16,4,64,256]{3,2,1,0:T(8,128)(2,1)} async-done(((bf16[16,4,64,256]{3,2,1,0:T(8,128)(2,1)}), bf16[16,4,64,256]{3,2,1,0:T(8,128)(2,1)}, u32[]{:S(2)}, u32[]{:S(2)}) %all-to-all-start.4) | async-done | bytes 2097184 | tf_op jit(solution)/shard_map/all_to_all | solution.py:435
  148.4 2.0 %reduce_sum.44 = bf16[4,64,256]{2,1,0:T(8,128)(2,1)S(1)} reduce(bf16[16,4,64,256]{3,2,1,0:T(8,128)(2,1)} %all-to-all-done.4, bf16[]{:T(256)} %constant.50.clone.1), dimensions={0}, to_apply=%region_2.3 | reduce | flops 983040 | bytes 2228226 | tf_op jit(solution)/shard_map/reduce_sum | solution.py:477
  150.4 12.8 %all_to_all.31 = bf16[8,64,256]{2,1,0:T(8,128)(2,1)S(1)} all-to-all(bf16[8,64,256]{2,1,0:T(8,128)(2,1)S(1)} %bitcast.43), channel_id=1, replica_groups=mesh['x'=4,'zh'=4,'y'=4,'zl'=2,'core'=2] {'zh','zl'}, dimensions={0} | all-to-all | bytes 524288 | tf_op jit(solution)/shard_map/all_to_all | solution.py:488
  163.2 3.5 %collective-permute-start.11 = (f32[64,256]{1,0:T(8,128)S(1)}, f32[64,256]{1,0:T(8,128)S(1)}, u32[]{:S(2)}, u32[]{:S(2)}) collective-permute-start(f32[64,256]{1,0:T(8,128)S(1)} %convert_reduce_fusion.1.refs_0_), channel_id=1, source_target_pairs={{0,1},{1,0},{2,3},{3,2},{4,5},{5,4},{6,7},{7,6},{8,9},{9,8},{10,11... | collective-permute-start | bytes 196616 | tf_op jit(solution)/shard_map/ppermute | solution.py:423
  168.3 1.6 shard_map.150
  (42 shorter events, 11.4 us)
Async XLA Ops:
  19.2 1.6 copy-start.1
  20.8 12.7 %copy-start = (bf16[1,128,1920]{2,1,0:T(8,128)(2,1)S(1)}, bf16[1,128,1920]{2,1,0:T(8,128)(2,1)}, u32[]{:S(2)}) copy-start(bf16[1,128,1920]{2,1,0:T(8,128)(2,1)} %param.15) | copy-start | bytes 1474564
  20.8 32.2 %all-to-all-start.1 = ((bf16[16,4,64,256]{3,2,1,0:T(8,128)(2,1)}), bf16[16,4,64,256]{3,2,1,0:T(8,128)(2,1)}, u32[]{:S(2)}, u32[]{:S(2)}) async-start(bf16[16,4,64,256]{3,2,1,0:T(8,128)(2,1)} %broadcast_in_dim.8), calls=%async_computation.1 | async-start | bytes 4194304 | tf_op jit(solution)/shard_map/all_to_all | solution.py:435
  28.5 7.3 %collective-permute-start = (bf16[16,512]{1,0:T(8,128)(2,1)S(1)}, bf16[16,512]{1,0:T(8,128)(2,1)S(1)}, u32[]{:S(2)}, u32[]{:S(2)}) collective-permute-start(bf16[16,512]{1,0:T(8,128)(2,1)S(1)} %slice_bitcast_fusion), channel_id=1, source_target_pairs={{1,0},{2,1},{3,2},{5,4},{6,5},{7,6},{9,8},{10,9},{11,10},{13,12},{... | collective-permute-start | bytes 49160 | tf_op jit(solution)/shard_map/ppermute | solution.py:523
  35.8 0.6 copy-start.4
  53.1 10.0 %collective-permute-start.1 = (bf16[64,64,256]{2,1,0:T(8,128)(2,1)}, bf16[64,64,256]{2,1,0:T(8,128)(2,1)}, u32[]{:S(2)}, u32[]{:S(2)}) collective-permute-start(bf16[64,64,256]{2,1,0:T(8,128)(2,1)} %bitcast.7.refs_0_), channel_id=1, source_target_pairs={{0,1},{1,0},{2,3},{3,2},{4,5},{5,4},{6,7},{7,6},{8,9},{9,8},{10,11... | collective-permute-start | bytes 6291464 | tf_op jit(solution)/shard_map/ppermute | solution.py:423
  58.7 22.1 %all-to-all-start.2 = ((bf16[16,4,32,256]{3,2,1,0:T(8,128)(2,1)}), bf16[16,4,32,256]{3,2,1,0:T(8,128)(2,1)}, u32[]{:S(2)}, u32[]{:S(2)}) async-start(bf16[16,4,32,256]{3,2,1,0:T(8,128)(2,1)} %get-tuple-element.69), calls=%async_computation.2 | async-start | bytes 2097152 | tf_op jit(solution)/shard_map/all_to_all | solution.py:435
  76.1 5.8 %collective-permute-start.2 = (bf16[64,32,256]{2,1,0:T(8,128)(2,1)}, bf16[64,32,256]{2,1,0:T(8,128)(2,1)}, u32[]{:S(2)}, u32[]{:S(2)}) collective-permute-start(bf16[64,32,256]{2,1,0:T(8,128)(2,1)} %get-tuple-element.75), channel_id=1, source_target_pairs={{0,1},{1,0},{2,3},{3,2},{4,5},{5,4},{6,7},{7,6},{8,9},{9,8},{10,11... | collective-permute-start | bytes 3145736 | tf_op jit(solution)/shard_map/ppermute | solution.py:423
  80.8 9.7 %collective-permute-start.3 = (bf16[64,32,256]{2,1,0:T(8,128)(2,1)}, bf16[64,32,256]{2,1,0:T(8,128)(2,1)}, u32[]{:S(2)}, u32[]{:S(2)}) collective-permute-start(bf16[64,32,256]{2,1,0:T(8,128)(2,1)} %bitcast.6.refs_0_), channel_id=1, source_target_pairs={{0,1},{1,0},{2,3},{3,2},{4,5},{5,4},{6,7},{7,6},{8,9},{9,8},{10,11... | collective-permute-start | bytes 3145736 | tf_op jit(solution)/shard_map/ppermute | solution.py:423
  84.4 21.5 %all-to-all-start.3 = ((bf16[16,4,32,256]{3,2,1,0:T(8,128)(2,1)}), bf16[16,4,32,256]{3,2,1,0:T(8,128)(2,1)}, u32[]{:S(2)}, u32[]{:S(2)}) async-start(bf16[16,4,32,256]{3,2,1,0:T(8,128)(2,1)} %bitcast.38), calls=%async_computation.3 | async-start | bytes 2097152 | tf_op jit(solution)/shard_map/all_to_all | solution.py:435
  105.9 5.7 %collective-permute-start.4 = (bf16[64,64,256]{2,1,0:T(8,128)(2,1)}, bf16[64,64,256]{2,1,0:T(8,128)(2,1)}, u32[]{:S(2)}, u32[]{:S(2)}) collective-permute-start(bf16[64,64,256]{2,1,0:T(8,128)(2,1)} %get-tuple-element.101), channel_id=1, source_target_pairs={{0,1},{1,0},{2,3},{3,2},{4,5},{5,4},{6,7},{7,6},{8,9},{9,8},{10,11... | collective-permute-start | bytes 6291464 | tf_op jit(solution)/shard_map/ppermute | solution.py:423
  114.8 33.6 %all-to-all-start.4 = ((bf16[16,4,64,256]{3,2,1,0:T(8,128)(2,1)}), bf16[16,4,64,256]{3,2,1,0:T(8,128)(2,1)}, u32[]{:S(2)}, u32[]{:S(2)}) async-start(bf16[16,4,64,256]{3,2,1,0:T(8,128)(2,1)} %bitcast.37), calls=%async_computation.4 | async-start | bytes 4194304 | tf_op jit(solution)/shard_map/all_to_all | solution.py:435
  120.7 5.7 %collective-permute-start.5 = (bf16[32,256]{1,0:T(8,128)(2,1)S(1)}, bf16[32,256]{1,0:T(8,128)(2,1)S(1)}, u32[]{:S(2)}, u32[]{:S(2)}) collective-permute-start(bf16[32,256]{1,0:T(8,128)(2,1)S(1)} %get-tuple-element.118), channel_id=1, source_target_pairs={{0,16},{16,32},{32,48},{48,0},{1,17},{17,33},{33,49},{49,1},{2,18}... | collective-permute-start | bytes 49160 | tf_op jit(solution)/shard_map/ppermute | solution.py:431
  121.4 6.5 %collective-permute-start.6 = (bf16[32,256]{1,0:T(8,128)(2,1)S(1)}, bf16[32,256]{1,0:T(8,128)(2,1)S(1)}, u32[]{:S(2)}, u32[]{:S(2)}) collective-permute-start(bf16[32,256]{1,0:T(8,128)(2,1)S(1)} %get-tuple-element.120), channel_id=1, source_target_pairs={{0,32},{16,48},{32,0},{48,16},{1,33},{17,49},{33,1},{49,17},{2,34}... | collective-permute-start | bytes 49160 | tf_op jit(solution)/shard_map/ppermute | solution.py:431
  125.0 4.2 %collective-permute-start.7 = (bf16[32,256]{1,0:T(8,128)(2,1)S(1)}, bf16[32,256]{1,0:T(8,128)(2,1)S(1)}, u32[]{:S(2)}, u32[]{:S(2)}) collective-permute-start(bf16[32,256]{1,0:T(8,128)(2,1)S(1)} %get-tuple-element.119), channel_id=1, source_target_pairs={{0,48},{16,0},{32,16},{48,32},{1,49},{17,1},{33,17},{49,33},{2,50}... | collective-permute-start | bytes 49160 | tf_op jit(solution)/shard_map/ppermute | solution.py:431
  129.3 5.9 %collective-permute-start.8 = (f32[32,256]{1,0:T(8,128)S(1)}, f32[32,256]{1,0:T(8,128)S(1)}, u32[]{:S(2)}, u32[]{:S(2)}) collective-permute-start(f32[32,256]{1,0:T(8,128)S(1)} %fusion.2), channel_id=1, source_target_pairs={{0,2},{2,0},{1,3},{3,1},{4,6},{6,4},{5,7},{7,5},{8,10},{10,8},{9,1... | collective-permute-start | bytes 98312 | tf_op jit(solution)/shard_map/ppermute | solution.py:497
  131.0 4.9 %collective-permute-start.10 = (f32[1,512]{1,0:T(1,128)S(1)}, f32[1,512]{1,0:T(1,128)S(1)}, u32[]{:S(2)}, u32[]{:S(2)}) collective-permute-start(f32[1,512]{1,0:T(1,128)S(1)} %slice.27), channel_id=1, source_target_pairs={{0,1},{1,2},{2,3},{4,5},{5,6},{6,7},{8,9},{9,10},{10,11},{12,13},{... | collective-permute-start | bytes 6152 | tf_op jit(solution)/shard_map/ppermute | solution.py:579
  135.2 6.9 %collective-permute-start.9 = (f32[32,256]{1,0:T(8,128)S(1)}, f32[32,256]{1,0:T(8,128)S(1)}, u32[]{:S(2)}, u32[]{:S(2)}) collective-permute-start(f32[32,256]{1,0:T(8,128)S(1)} %add.63), channel_id=1, source_target_pairs={{0,1},{1,0},{2,3},{3,2},{4,5},{5,4},{6,7},{7,6},{8,9},{9,8},{10,11... | collective-permute-start | bytes 98312 | tf_op jit(solution)/shard_map/ppermute | solution.py:423
  135.9 0.6 copy-start.5
  163.2 4.4 %copy-start.2 = (f32[64,256]{1,0:T(8,128)}, f32[64,256]{1,0:T(8,128)S(1)}, u32[]{:S(2)}) copy-start(f32[64,256]{1,0:T(8,128)S(1)} %convert_reduce_fusion.1.refs_0_) | copy-start | bytes 196612
  163.2 4.4 %collective-permute-start.11 = (f32[64,256]{1,0:T(8,128)S(1)}, f32[64,256]{1,0:T(8,128)S(1)}, u32[]{:S(2)}, u32[]{:S(2)}) collective-permute-start(f32[64,256]{1,0:T(8,128)S(1)} %convert_reduce_fusion.1.refs_0_), channel_id=1, source_target_pairs={{0,1},{1,0},{2,3},{3,2},{4,5},{5,4},{6,7},{7,6},{8,9},{9,8},{10,11... | collective-permute-start | bytes 196616 | tf_op jit(solution)/shard_map/ppermute | solution.py:423
  167.6 0.6 copy-start.3

commit v3 on v2

--- a/solution.py
+++ b/solution.py
@@ -11,7 +11,7 @@
 CH = 512
 WIDTH = 1920
 HALF = 256
-STEP = 32
+STEP = 64
 ALL_VMEM = 2**26 - 2**18
 
 
@@ -179,7 +179,7 @@
 
 def split_kernel(place_ref, ins, outs, scratch, need, give):
     x_ref, next_ref, line_ref = ins
-    even_ref, odd_ref, third_ref, spread_c_ref = outs
+    unfold_ref, spread_c_ref = outs
     (first_ref,) = scratch
     need(*ins)
     for k in range(16):
@@ -192,21 +192,21 @@
         groups = groups.astype(bf16)
         for r in range(4):
             at = slice(128 * r + 32 * j, 128 * r + 32 * j + 32)
-            even_ref[at, :] = groups[64 * r : 64 * r + 32]
-            odd_ref[at, :] = groups[64 * r + 32 : 64 * r + 64]
+            unfold_ref[0, at, :] = groups[64 * r : 64 * r + 32]
+            unfold_ref[1, at, :] = groups[64 * r + 32 : 64 * r + 64]
             if r > 0:
-                third_ref[128 * r - 128 + 32 * j : 128 * r - 96 + 32 * j, :] = groups[64 * r : 64 * r + 32]
+                unfold_ref[2, 128 * r - 128 + 32 * j : 128 * r - 96 + 32 * j, :] = groups[64 * r : 64 * r + 32]
     later = pltpu.roll(first_ref[...], 127, 0)
     last = lax.broadcasted_iota(jnp.int32, (128, CH), 0) == 127
-    third_ref[384:512, :] = jnp.where(last, next_ref[:1, :].astype(f32), later).astype(bf16)
+    unfold_ref[2, 384:512, :] = jnp.where(last, next_ref[:1, :].astype(f32), later).astype(bf16)
 
 
 def forward_kernel(core_ref, ins, outs, scratch, need, give):
-    mine_ref, other_ref, even_ref, odd_ref, third_ref, cot_ref = ins
+    mine_ref, other_ref, unfold_ref, unfold_other_ref, cot_ref, cot_other_ref = ins
     (
         cp_ref, w5_ref, five_ref, unit5_ref, slope5_ref, scale5_ref,
         w6_ref, w7_ref, act6_ref, unit6_ref, slope6_ref, scale6_ref, unit7_ref, slope7_ref, scale7_ref,
-        normed_ref, unit_ref, scale_ref, give_ref, send_ref,
+        normed_ref, unit_ref, scale_ref, give_ref,
     ) = outs
     wide_ref, small_ref, pre5_ref, pre6_ref, pre7_ref, act7_ref, gp_ref = scratch
     need(mine_ref, other_ref)
@@ -234,61 +234,72 @@
 
     lax.fori_loop(0, 12, narrow, 0)
     give(cp_ref, w5_ref, w6_ref, w7_ref)
-    need(even_ref, odd_ref, third_ref)
-
-    def multiply(r, _):
-        at = rows(r, 128)
-        pre5_ref[at, :] = (
-            dot(even_ref[at, :], w5_ref[:512, :]) + dot(odd_ref[at, :], w5_ref[512:1024, :])
-        ) + dot(third_ref[at, :], w5_ref[1024:, :])
-        return 0
-
-    lax.fori_loop(0, 4, multiply, 0)
+    need(unfold_ref, unfold_other_ref)
+
+    for b, ref in enumerate((unfold_ref, unfold_other_ref)):
+
+        def multiply(r, _, b=b, ref=ref):
+            at = rows(r, 128)
+            pre5_ref[rows(r + 4 * b, 128), :] = (
+                dot(ref[0, at, :], w5_ref[:512, :]) + dot(ref[1, at, :], w5_ref[512:1024, :])
+            ) + dot(ref[2, at, :], w5_ref[1024:, :])
+            return 0
+
+        lax.fori_loop(0, 4, multiply, 0)
     block_forward(pre5_ref, cp_ref, 0, five_ref, unit5_ref, slope5_ref, scale5_ref)
     give(five_ref, unit5_ref, slope5_ref, scale5_ref)
-    for s in range(2):
+    for s in range(4):
         pre6_ref[128 * s : 128 * s + 128, :] = dot(five_ref[256 * s : 256 * s + 128, :], w6_ref[:512, :]) + dot(
             five_ref[256 * s + 128 : 256 * s + 256, :], w6_ref[512:, :]
         )
     block_forward(pre6_ref, cp_ref, 3, act6_ref, unit6_ref, slope6_ref, scale6_ref)
-    pre7_ref[...] = dot(act6_ref[:128, :], w7_ref[:512, :]) + dot(act6_ref[128:, :], w7_ref[512:, :])
+    give(act6_ref, unit6_ref, slope6_ref, scale6_ref)
+    for b in range(2):
+        pre7_ref[128 * b : 128 * b + 128, :] = dot(act6_ref[256 * b : 256 * b + 128, :], w7_ref[:512, :]) + dot(
+            act6_ref[256 * b + 128 : 256 * b + 256, :], w7_ref[512:, :]
+        )
     block_forward(pre7_ref, cp_ref, 6, act7_ref, unit7_ref, slope7_ref, scale7_ref)
+    give(unit7_ref, slope7_ref, scale7_ref)
 
     unit, scale = standard(act7_ref[...].astype(f32))
     normed = (unit * cp_ref[9:10] + cp_ref[10:11]).astype(bf16)
     unit_ref[...] = unit
-    scale_ref[...] = jnp.broadcast_to(scale, (128, 128))
+    scale_ref[...] = jnp.broadcast_to(scale, (256, 128))
     normed_ref[...] = normed
+    give(unit_ref, scale_ref, normed_ref)
     flipped = normed.astype(f32).T.astype(bf16)
-    give(act6_ref, unit6_ref, slope6_ref, scale6_ref, unit7_ref, slope7_ref, scale7_ref)
-    need(cot_ref)
-    for b in range(8):
-        cols = slice(HALF * b, min(HALF * (b + 1), WIDTH))
-        gp_ref[:, cols] = dot(flipped, cot_ref[:, cols])
-    gp_ref[:, WIDTH:] = jnp.zeros((CH, 8 * HALF - WIDTH), f32)
-
-    def pack(mine_at, other_at):
-        def step(i, _):
-            to = place(i)
-            for ref, at in ((give_ref, mine_at), (send_ref, other_at)):
-                block = gp_ref[rows(to, 8), 4 * at : 4 * at + 4 * HALF]
-                parts = [block[:, HALF * b : HALF * (b + 1)] for b in range(4)]
-                ref[i] = jnp.concatenate(parts, 0).astype(bf16)
-            return 0
-
-        lax.fori_loop(0, 64, step, 0, unroll=4)
-
-    by_core(core_ref, pack)
+    need(cot_ref, cot_other_ref)
+
+    def multiply_proj(mine_at, other_at):
+        for b in range(4):
+            start = 4 * mine_at + HALF * b
+            cols = slice(start, min(start + HALF, WIDTH))
+            both = jnp.concatenate([cot_ref[:, cols], cot_other_ref[:, cols]], 0)
+            gp_ref[:, HALF * b : HALF * b + both.shape[1]] = dot(flipped, both)
+            if both.shape[1] < HALF:
+                gp_ref[:, HALF * b + both.shape[1] : HALF * (b + 1)] = jnp.zeros((CH, HALF - both.shape[1]), f32)
+
+    by_core(core_ref, multiply_proj)
+
+    def pack(i, _):
+        block = gp_ref[rows(place(i), 8), :]
+        parts = [block[:, HALF * b : HALF * (b + 1)] for b in range(4)]
+        give_ref[i] = jnp.concatenate(parts, 0).astype(bf16)
+        return 0
+
+    lax.fori_loop(0, 64, pack, 0, unroll=4)
 
 
 def backward_kernel(core_ref, ins, outs, scratch, need, give):
     (
-        mine_ref, other_ref, cp_ref, bias_ref, cot_ref, normed_ref, unit_ref, scale_ref,
+        mine_ref, other_ref, cp_ref, bias_ref, cot_ref, cot_other_ref, normed_ref, unit_ref, scale_ref,
         unit7_ref, slope7_ref, scale7_ref, w7_ref, act6_ref, unit6_ref, slope6_ref, scale6_ref, w6_ref, five_ref,
-        unit5_ref, slope5_ref, scale5_ref, w5_ref, even_ref, odd_ref, third_ref, gb_ref,
+        unit5_ref, slope5_ref, scale5_ref, w5_ref, unfold_ref, unfold_other_ref, gb_ref,
     ) = ins
-    out_ref, edge_ref, d5_ref, give_ref, send_ref = outs
-    wp_ref, wide_ref, pre5_ref, pre6_ref, pre7_ref, g5_ref, g6_ref, g7_ref, d6_ref, d7_ref, small_ref, sums_ref = scratch
+    out_ref, edge_ref, d5_ref, give_ref = outs
+    (
+        wp_ref, wide_ref, pre5_ref, pre6_ref, pre7_ref, g5_ref, g6_ref, g7_ref, d6_ref, d7_ref, half_ref, small_ref, sums_ref,
+    ) = scratch
     need(mine_ref, other_ref)
 
     def unpack(mine_at, other_at):
@@ -309,13 +320,22 @@
         return 0
 
     lax.fori_loop(0, 8, narrow, 0)
-    need(cp_ref, bias_ref, cot_ref, normed_ref)
-
-    normed_grad = jnp.zeros((128, CH), f32)
+    need(cp_ref, bias_ref, cot_ref, cot_other_ref, normed_ref)
+
+    def keep(ref):
+        size = ref.shape[0]
+
+        def body(mine_at, other_at):
+            half_ref[:size, :] = ref[:, mine_at : mine_at + HALF]
+
+        by_core(core_ref, body)
+
+    normed_grad = jnp.zeros((256, CH), f32)
     for b in range(8):
         cols = slice(HALF * b, min(HALF * (b + 1), WIDTH))
-        out_ref[:, cols] = (dot(normed_ref[...], wp_ref[:, cols]) + bias_ref[:, cols]).astype(bf16)
-        normed_grad = normed_grad + dot(cot_ref[:, cols], wp_ref[:, cols], (1, 1))
+        out_ref[:, cols] = (dot(normed_ref[:128, :], wp_ref[:, cols]) + bias_ref[:, cols]).astype(bf16)
+        both = jnp.concatenate([cot_ref[:, cols], cot_other_ref[:, cols]], 0)
+        normed_grad = normed_grad + dot(both, wp_ref[:, cols], (1, 1))
 
     need(unit_ref, scale_ref, unit7_ref, slope7_ref, scale7_ref)
     give(out_ref)
@@ -329,44 +349,49 @@
     for i, part in enumerate(block_backward(pre7_ref, cp_ref, 6, unit7_ref, slope7_ref, scale7_ref, d7_ref)):
         sums_ref[6 + i : 7 + i, :] = total(part)
     need(w7_ref, act6_ref)
+    keep(d7_ref)
     for s in range(2):
         half = slice(512 * s, 512 * s + 512)
-        pre6_ref[128 * s : 128 * s + 128, :] = dot(d7_ref[...], w7_ref[half, :], (1, 1))
-        g7_ref[half, :] = dot(act6_ref[128 * s : 128 * s + 128, :], d7_ref[...], (0, 0))
+        left = [act6_ref[256 * b + 128 * s : 256 * b + 128 * s + 128, :] for b in range(2)]
+        g7_ref[half, :] = dot(jnp.concatenate(left, 0), half_ref[:256, :], (0, 0))
+        for b in range(2):
+            at = 256 * b + 128 * s
+            pre6_ref[at : at + 128, :] = dot(d7_ref[128 * b : 128 * b + 128, :], w7_ref[half, :], (1, 1))
     need(unit6_ref, slope6_ref, scale6_ref)
     for i, part in enumerate(block_backward(pre6_ref, cp_ref, 3, unit6_ref, slope6_ref, scale6_ref, d6_ref)):
         sums_ref[3 + i : 4 + i, :] = total(part)
     need(w6_ref, five_ref)
+    keep(d6_ref)
     for r in range(2):
         half = slice(512 * r, 512 * r + 512)
-        for s in range(2):
+        left = [five_ref[256 * s + 128 * r : 256 * s + 128 * r + 128, :] for s in range(4)]
+        g6_ref[half, :] = dot(jnp.concatenate(left, 0), half_ref[:512, :], (0, 0))
+        for s in range(4):
             at = 256 * s + 128 * r
             pre5_ref[at : at + 128, :] = dot(d6_ref[128 * s : 128 * s + 128, :], w6_ref[half, :], (1, 1))
-        g6_ref[half, :] = dot(five_ref[128 * r : 128 * r + 128, :], d6_ref[:128, :], (0, 0)) + dot(
-            five_ref[256 + 128 * r : 384 + 128 * r, :], d6_ref[128:, :], (0, 0)
-        )
     need(unit5_ref, slope5_ref, scale5_ref)
     for i, part in enumerate(block_backward(pre5_ref, cp_ref, 0, unit5_ref, slope5_ref, scale5_ref, d5_ref)):
         sums_ref[i : i + 1, :] = total(part)
     need(*ins)
     give(d5_ref)
     edge_ref[...] = dot(d5_ref[496:512, :], w5_ref[1024:, :], (1, 1))[8:]
-    for k, ref in enumerate((even_ref, odd_ref, third_ref)):
-        g5_ref[512 * k : 512 * k + 512, :] = dot(ref[...], d5_ref[...], (0, 0))
+    keep(d5_ref)
+    for k in range(3):
+        g5_ref[512 * k : 512 * k + 512, :] = dot(unfold_ref[k], half_ref[:512, :], (0, 0)) + dot(
+            unfold_other_ref[k], half_ref[512:, :], (0, 0)
+        )
     small_ref[...] = sums_ref[...].T
 
     def pack(mine_at, other_at):
         def step(i, _):
             to = place(i)
-            for ref, at in ((give_ref, mine_at), (send_ref, other_at)):
-                if at == 0:
-                    tail = jnp.concatenate([small_ref[rows(to, 8), :], gb_ref[rows(to, 8), :]], 1)
-                else:
-                    tail = jnp.zeros((8, HALF), f32)
-                block = jnp.concatenate([g5_ref[rows(to, 24), at : at + HALF], tail], 0)
-                ref[i, :32, :] = block.astype(bf16)
-                ref[i, 32:48, :] = g6_ref[rows(to, 16), at : at + HALF].astype(bf16)
-                ref[i, 48:, :] = g7_ref[rows(to, 16), at : at + HALF].astype(bf16)
+            if mine_at == 0:
+                tail = jnp.concatenate([small_ref[rows(to, 8), :], gb_ref[rows(to, 8), :]], 1)
+            else:
+                tail = jnp.zeros((8, HALF), f32)
+            give_ref[i, :32, :] = jnp.concatenate([g5_ref[rows(to, 24), :], tail], 0).astype(bf16)
+            give_ref[i, 32:48, :] = g6_ref[rows(to, 16), :].astype(bf16)
+            give_ref[i, 48:, :] = g7_ref[rows(to, 16), :].astype(bf16)
             return 0
 
         lax.fori_loop(0, 64, step, 0, unroll=4)
@@ -435,44 +460,6 @@
     return together(lax.all_to_all(value, ("x", "y"), 0, 0, tiled=True), *meanwhile)
 
 
-def add_kernel(a_ref, b_ref, out_ref, a, b, both, a_sems, b_sems, out_sems):
-    size = a_ref.shape[0] // 4
-    parts = [pl.ds(size * k, size) for k in range(4)]
-    loads = []
-    for k, part in enumerate(parts):
-        loads.append(pltpu.make_async_copy(a_ref.at[part], a.at[part], a_sems.at[k]))
-        loads.append(pltpu.make_async_copy(b_ref.at[part], b.at[part], b_sems.at[k]))
-    stores = [pltpu.make_async_copy(both.at[part], out_ref.at[part], out_sems.at[k]) for k, part in enumerate(parts)]
-    for load in loads:
-        load.start()
-    for k, store in enumerate(stores):
-        loads[2 * k].wait()
-        loads[2 * k + 1].wait()
-
-        def step(i, _, k=k):
-            at = size * k + i
-            both[at] = (a[at].astype(f32) + b[at].astype(f32)).astype(bf16)
-            return 0
-
-        lax.fori_loop(0, size, step, 0, unroll=4)
-        store.start()
-    for store in stores:
-        store.wait()
-
-
-def sum_cores(give, send):
-    hbm = pl.BlockSpec(memory_space=pltpu.HBM)
-    return pl.pallas_call(
-        add_kernel,
-        out_shape=jax.ShapeDtypeStruct(give.shape, bf16),
-        in_specs=[hbm, hbm],
-        out_specs=hbm,
-        scratch_shapes=[pltpu.VMEM(give.shape, bf16)] * 3 + [pltpu.SemaphoreType.DMA((4,))] * 3,
-        compiler_params=pltpu.CompilerParams(vmem_limit_bytes=ALL_VMEM),
-        cost_estimate=pl.CostEstimate(flops=2**20, bytes_accessed=6 * 2**20, transcendentals=0),
-    )(give, swap_cores(send))
-
-
 def sum_plane(plane):
     return jnp.sum(plane.astype(f32), 0).astype(bf16)
 
@@ -521,61 +508,63 @@
 
     line, first_rows, late_cotangent = together(line, inputs[:16], cotangent)
     next_row = lax.ppermute(first_rows, ("zl", "core"), [(1, 0), (2, 1), (3, 2)])
-    even, odd, third, spread_c = staged(
+    unfold, spread_c = staged(
         split_kernel,
         (place_at, inputs, next_row, line),
-        [(square, bf16)] * 3 + [((16, 4, 32, HALF), bf16)],
+        [((3, 512, CH), bf16), ((16, 4, 32, HALF), bf16)],
         [((128, CH), f32)],
         flops=2**28,
         moved=3 * 2**20,
     )
-    grad_bias = jnp.sum(late_cotangent.astype(f32), 0).reshape(64, 1, 30)
+    unfold_other = swap_cores(unfold)
+    cot_other = swap_cores(late_cotangent)
+    grad_bias = (jnp.sum(late_cotangent.astype(f32), 0) + jnp.sum(cot_other.astype(f32), 0)).reshape(64, 1, 30)
     grad_bias = jnp.pad(grad_bias, [(0, 0), (0, 7), (0, 98)]).reshape(512, 128)
 
-    mine_ab, spread_c, even, odd, third, grad_bias = across_plane(spread_ab, spread_c, even, odd, third, grad_bias)
+    mine_ab, spread_c, unfold, unfold_other, cot_other, grad_bias = across_plane(
+        spread_ab, spread_c, unfold, unfold_other, cot_other, grad_bias
+    )
     mine_ab = mine_ab.reshape(64, 64, HALF)
     other_ab = swap_cores(mine_ab)
     bias = jnp.where(core == 0, mine_ab[:, 24, 128:158], other_ab[:, 24, 128:158])
     bias = bias.reshape(4, 4, 4, 30).transpose(0, 2, 1, 3).reshape(1, WIDTH).astype(f32)
 
     saved = lambda n: [((n, CH), f32), ((n, CH), f32), ((n, 128), f32)]
-    pair = lambda n: [((64, n, HALF), bf16)] * 2
     w_shapes = [((1536, CH), bf16), ((1024, CH), bf16), ((1024, CH), bf16)]
-    cp, w5, act_five, *saved_five, w6, w7, act_six, u6, s6, r6, u7, s7, r7, normed, unit, scale, give_c, send_c = staged(
+    cp, w5, act_five, *saved_five, w6, w7, act_six, u6, s6, r6, u7, s7, r7, normed, unit, scale, give_c = staged(
         forward_kernel,
-        (place_at, mine_ab, other_ab, even, odd, third, cotangent),
-        [((16, CH), f32), w_shapes[0], (square, bf16)]
+        (place_at, mine_ab, other_ab, unfold, unfold_other, cotangent, cot_other),
+        [((16, CH), f32), w_shapes[0], ((1024, CH), bf16)]
+        + saved(1024)
+        + w_shapes[1:]
+        + [(square, bf16)]
         + saved(512)
-        + w_shapes[1:]
-        + [((256, CH), bf16)]
         + saved(256)
-        + saved(128)
-        + [((128, CH), bf16), ((128, CH), f32), ((128, 128), f32)]
-        + pair(32),
-        [((1536, CH), f32), (flat, f32), (square, f32), ((256, CH), f32), ((128, CH), f32), ((128, CH), bf16)]
-        + [((CH, 8 * HALF), f32)],
+        + [((256, CH), bf16), ((256, CH), f32), ((256, 128), f32)]
+        + [(stack, bf16)],
+        [((1536, CH), f32), (flat, f32), ((1024, CH), f32), (square, f32), ((256, CH), f32), ((256, CH), bf16)]
+        + [((CH, 4 * HALF), f32)],
         flops=2**31,
         moved=16 * 2**20,
     )
 
-    (mine_c,) = across_plane(spread_c)
+    mine_c, give_c = across_plane(spread_c, give_c)
     mine_c = mine_c.reshape(stack)
     other_c = swap_cores(mine_c)
-    mine_c, cores_c = together(mine_c, sum_cores(give_c, send_c))
-    projected, edge, d_five, give_ab, send_ab = staged(
+    projected, edge, d_five, give_ab = staged(
         backward_kernel,
-        (place_at, mine_c, other_c, cp, bias, cotangent, normed, unit, scale, u7, s7, r7, w7, act_six)
-        + (u6, s6, r6, w6, act_five, *saved_five, w5, even, odd, third, grad_bias),
-        [((128, WIDTH), bf16), ((8, CH), f32), (square, bf16)] + pair(64),
-        [((CH, WIDTH), bf16), ((CH, 8 * HALF), f32), (square, f32), ((256, CH), f32), ((128, CH), f32)]
-        + [((1536, CH), f32), ((1024, CH), f32), ((1024, CH), f32), ((256, CH), bf16), ((128, CH), bf16)]
-        + [(flat, f32), ((128, CH), f32)],
+        (place_at, mine_c, other_c, cp, bias, cotangent, cot_other, normed, unit, scale, u7, s7, r7, w7, act_six)
+        + (u6, s6, r6, w6, act_five, *saved_five, w5, unfold, unfold_other, grad_bias),
+        [((128, WIDTH), bf16), ((8, CH), f32), ((1024, CH), bf16), ((64, 64, HALF), bf16)],
+        [((CH, WIDTH), bf16), ((CH, 8 * HALF), f32), ((1024, CH), f32), (square, f32), ((256, CH), f32)]
+        + [((1536, HALF), f32), ((1024, HALF), f32), ((1024, HALF), f32), (square, bf16), ((256, CH), bf16)]
+        + [((1024, HALF), bf16), (flat, f32), ((128, CH), f32)],
         flops=2**31,
         moved=16 * 2**20,
     )
 
-    plane_c, give_ab, send_ab = across_plane(cores_c.reshape(16, 4, 32, HALF), give_ab, send_ab)
-    cores_ab, plane_c, d_five = together(sum_cores(give_ab, send_ab), plane_c, d_five)
+    plane_c, give_ab = across_plane(give_c.reshape(16, 4, 32, HALF), give_ab)
+    give_ab, plane_c, d_five = together(give_ab, plane_c, d_five)
     carried = lax.ppermute(edge[7:8], ("zl", "core"), [(0, 1), (1, 2), (2, 3)])
     (input_grad,) = staged(
         input_kernel,
@@ -587,7 +576,7 @@
     )
     sum_c = sum_line_by_permutes(sum_plane(plane_c), core)
     grad_proj = proj_rows(sum_c)
-    plane_ab, grad_proj, input_grad = across_plane(cores_ab.reshape(16, 4, 64, HALF), grad_proj, input_grad)
+    plane_ab, grad_proj, input_grad = across_plane(give_ab.reshape(16, 4, 64, HALF), grad_proj, input_grad)
     sum_ab = sum_line(sum_plane(plane_ab))
     grad_five, grad_six, grad_seven, grad_channel, grad_bias = staged(
         finish_kernel,

time: 171 us -> 160 us (0.936)
  waiting for transfers between devices: 36.1 us -> 25.1 us
    all_to_all x4, waiting for transfers between devices: 26.3 us -> 13.7 us  [across_plane(): lax.all_to_all(value, ('x', 'y'), 0, 0, tiled=True)]
    pallas_call x2 -> x0, Pallas kernels: 5.55 us -> none  [sum_cores(): pl.pallas_call(add_kernel, out_shape=jax.ShapeDtypeStruct(give.shape, bf1...]
    pallas_call x6, Pallas kernels: 37.6 us -> 41.4 us  [staged(): pl.pallas_call(kernel, out_shape=[jax.ShapeDtypeStruct(shape, kind) for s...]
    ppermute x3, waiting for transfers between devices: 2.85 us -> 5.25 us  [around(): lax.ppermute(value, axis, [(i, (i + back) % size) for i in range(size)])]
    ppermute x6, waiting for transfers between devices: 5.04 us -> 3.25 us  [swap_cores(): return lax.ppermute(value, 'core', [(0, 1), (1, 0)])]
  transfers between devices with their start and end apart: 16 -> 16, of which waited for: 10 -> 9; matrix products, arithmetic and copies ran while one was open for 4% -> 5% of each run, Pallas kernels for 22% -> 24%
where the time goes in v3:
time: 160 us; the launch traced here: 159 us
  starting transfers between devices  48.4 us (30%)
  Pallas kernels  41.4 us (26%)
  blocking collectives  29.7 us (19%)
  waiting for transfers between devices  25.1 us (16%)
  local copies, waits for them, and re-layouts  7.99 us (5%)
  other arithmetic  5.67 us (4%)
    pallas_call x6, Pallas kernels, staged(): pl.pallas_call(kernel, out_shape=[jax.ShapeDtypeStruct(shape, kind) for s...  41.4 us
    all_to_all x4, starting transfers between devices, across_plane(): lax.all_to_all(value, ('x', 'y'), 0, 0, tiled=True)  20 us
    all_to_all x1, blocking collectives, shards(): line = lax.all_to_all(packed, 'zh', 0, 0, tiled=True)  17 us
    all_to_all x4, waiting for transfers between devices, across_plane(): lax.all_to_all(value, ('x', 'y'), 0, 0, tiled=True)  13.7 us
    all_to_all x1, blocking collectives, sum_line(): line = lax.all_to_all(line, ('zh', 'zl'), 0, 0, tiled=True)  12.7 us
    ppermute x6, starting transfers between devices, swap_cores(): return lax.ppermute(value, 'core', [(0, 1), (1, 0)])  12.2 us
    ppermute x3, starting transfers between devices, around(): lax.ppermute(value, axis, [(i, (i + back) % size) for i in range(size)])  5.3 us
    ppermute x3, waiting for transfers between devices, around(): lax.ppermute(value, axis, [(i, (i + back) % size) for i in range(size)])  5.25 us
  transfers between devices with their start and end apart: 16, of which 9 were waited for; matrix products, arithmetic and copies ran while one was open for 5% of the time, Pallas kernels for 24%

profile of v3, /device:TPU:1, one launch (start us, length us, event | category | flops | bytes accessed | tf_op | source)
XLA Modules:
  0.0 159.4 jit_solution(16163783954373898817)
XLA Ops:
  0.6 1.6 shard_map.143
  2.2 17.0 %all_to_all.30.refs_2_ = bf16[4,96,256]{2,1,0:T(8,128)(2,1)S(1)} all-to-all(bf16[4,96,256]{2,1,0:T(8,128)(2,1)} %shard_map.143), channel_id=1, replica_groups=mesh['x'=4,'zh'=4,'y'=4,'zl'=2,'core'=2] {'zh'}, dimensions={0} | all-to-all | bytes 393216 | tf_op jit(solution)/shard_map/all_to_all | solution.py:506
  19.2 1.6 %broadcast_in_dim.8 = bf16[16,4,64,256]{3,2,1,0:T(8,128)(2,1)} broadcast(bf16[4,64,256]{2,1,0:T(8,128)(2,1)S(1)} %slice.28), dimensions={1,2,3} | broadcast | bytes 2228224 | tf_op jit(solution)/shard_map/broadcast_in_dim | solution.py:507
  20.8 6.8 %all-to-all-start.1 = ((bf16[16,4,64,256]{3,2,1,0:T(8,128)(2,1)}), bf16[16,4,64,256]{3,2,1,0:T(8,128)(2,1)}, u32[]{:S(2)}, u32[]{:S(2)}) async-start(bf16[16,4,64,256]{3,2,1,0:T(8,128)(2,1)} %broadcast_in_dim.8), calls=%async_computation.1 | async-start | bytes 4194304 | tf_op jit(solution)/shard_map/all_to_all | solution.py:460
  28.4 5.0 %collective-permute-start = (bf16[16,512]{1,0:T(8,128)(2,1)S(1)}, bf16[16,512]{1,0:T(8,128)(2,1)S(1)}, u32[]{:S(2)}, u32[]{:S(2)}) collective-permute-start(bf16[16,512]{1,0:T(8,128)(2,1)S(1)} %slice_bitcast_fusion), channel_id=1, source_target_pairs={{1,0},{2,1},{3,2},{5,4},{6,5},{7,6},{9,8},{10,9},{11,10},{13,12},{... | collective-permute-start | bytes 49160 | tf_op jit(solution)/shard_map/ppermute | solution.py:510
  33.4 2.4 %collective-permute-done.refs_1_ = bf16[16,512]{1,0:T(8,128)(2,1)S(1)} collective-permute-done((bf16[16,512]{1,0:T(8,128)(2,1)S(1)}, bf16[16,512]{1,0:T(8,128)(2,1)S(1)}, u32[]{:S(2)}, u32[]{:S(2)}) %collective-permute-start) | collective-permute-done | bytes 16416 | tf_op jit(solution)/shard_map/ppermute | solution.py:510
  36.3 3.2 %shard_map.144 = (bf16[3,512,512]{2,1,0:T(8,128)(2,1)}, bf16[16,4,32,256]{3,2,1,0:T(8,128)(2,1)}) custom-call(s32[1]{0:T(128)} %bitcast.place_ref, bf16[1024,512]{1,0:T(8,128)(2,1)} %bitcast.42, bf16[16,512]{1,0:T(8,128)(2,1)} %copy-done.4, bf16[4,96,256]{2,1,0:T(8,128)(2,1)} %copy-done.1), custom_call_target="tpu_custom_call" | custom-call | flops 268435456 | bytes 3145728 | tf_op jit(solution)/shard_map/pallas_call | solution.py:62
  40.2 1.1 convert_reduce_fusion.1
  41.3 2.3 %collective-permute-done.2.refs_5_ = bf16[128,1920]{1,0:T(8,128)(2,1)S(1)} collective-permute-done((bf16[128,1920]{1,0:T(8,128)(2,1)}, bf16[128,1920]{1,0:T(8,128)(2,1)S(1)}, u32[]{:S(2)}, u32[]{:S(2)}) %collective-permute-start.2) | collective-permute-done | bytes 491552 | tf_op jit(solution)/shard_map/ppermute | solution.py:448
  45.4 7.5 %all-to-all-done.1 = bf16[16,4,64,256]{3,2,1,0:T(8,128)(2,1)} async-done(((bf16[16,4,64,256]{3,2,1,0:T(8,128)(2,1)}), bf16[16,4,64,256]{3,2,1,0:T(8,128)(2,1)}, u32[]{:S(2)}, u32[]{:S(2)}) %all-to-all-start.1) | async-done | bytes 2097184 | tf_op jit(solution)/shard_map/all_to_all | solution.py:460
  53.0 5.7 %collective-permute-start.3 = (bf16[64,64,256]{2,1,0:T(8,128)(2,1)}, bf16[64,64,256]{2,1,0:T(8,128)(2,1)}, u32[]{:S(2)}, u32[]{:S(2)}) collective-permute-start(bf16[64,64,256]{2,1,0:T(8,128)(2,1)} %bitcast.6.refs_0_), channel_id=1, source_target_pairs={{0,1},{1,0},{2,3},{3,2},{4,5},{5,4},{6,7},{7,6},{8,9},{9,8},{10,11... | collective-permute-start | bytes 6291464 | tf_op jit(solution)/shard_map/ppermute | solution.py:448
  58.6 4.3 %all-to-all-start.2 = ((bf16[16,4,32,256]{3,2,1,0:T(8,128)(2,1)}), bf16[16,4,32,256]{3,2,1,0:T(8,128)(2,1)}, u32[]{:S(2)}, u32[]{:S(2)}) async-start(bf16[16,4,32,256]{3,2,1,0:T(8,128)(2,1)} %get-tuple-element.62), calls=%async_computation.2 | async-start | bytes 2097152 | tf_op jit(solution)/shard_map/all_to_all | solution.py:460
  63.0 15.2 %shard_map.145 = (f32[16,512]{1,0:T(8,128)}, bf16[1536,512]{1,0:T(8,128)(2,1)}, bf16[1024,512]{1,0:T(8,128)(2,1)}, f32[1024,512]{1,0:T(8,128)}, f32[1024,512]{1,...) custom-call(s32[1]{0:T(128)} %bitcast.place_ref, ...), custom_call_target="tpu_custom_call" | custom-call | flops 2147483648 | bytes 16777216 | tf_op jit(solution)/shard_map/pallas_call | solution.py:62
  78.2 2.5 %all-to-all-done.2 = bf16[16,4,32,256]{3,2,1,0:T(8,128)(2,1)} async-done(((bf16[16,4,32,256]{3,2,1,0:T(8,128)(2,1)}), bf16[16,4,32,256]{3,2,1,0:T(8,128)(2,1)}, u32[]{:S(2)}, u32[]{:S(2)}) %all-to-all-start.2) | async-done | bytes 1048608 | tf_op jit(solution)/shard_map/all_to_all | solution.py:460
  80.7 1.2 collective-permute-start.4
  81.8 4.3 %all-to-all-start.3 = ((bf16[16,4,32,256]{3,2,1,0:T(8,128)(2,1)}), bf16[16,4,32,256]{3,2,1,0:T(8,128)(2,1)}, u32[]{:S(2)}, u32[]{:S(2)}) async-start(bf16[16,4,32,256]{3,2,1,0:T(8,128)(2,1)} %bitcast.43), calls=%async_computation.3 | async-start | bytes 2097152 | tf_op jit(solution)/shard_map/all_to_all | solution.py:460
  86.2 1.0 fusion
  87.9 14.1 %shard_map.146 = (bf16[128,1920]{1,0:T(8,128)(2,1)}, f32[8,512]{1,0:T(8,128)}, bf16[1024,512]{1,0:T(8,128)(2,1)}, bf16[64,64,256]{2,1,0:T(8,128)(2,1)}) custom-call(s32[1]{0:T(128)} %bitcast.place_ref, bf16[64,32,256]{2,1,0:T(8,128)(2,1)} %bitcast.7.refs_0_, bf16[64,32,256]{2,1,0:T(8,128)(2,1)} %collective-permute-done.4.refs_1_, ...), custom_call_target="tpu_custom_call" | custom-call | flops 2147483648 | bytes 16777216 | tf_op jit(solution)/shard_map/pallas_call | solution.py:62
  102.0 2.1 %all-to-all-done.3 = bf16[16,4,32,256]{3,2,1,0:T(8,128)(2,1)} async-done(((bf16[16,4,32,256]{3,2,1,0:T(8,128)(2,1)}), bf16[16,4,32,256]{3,2,1,0:T(8,128)(2,1)}, u32[]{:S(2)}, u32[]{:S(2)}) %all-to-all-start.3) | async-done | bytes 1048608 | tf_op jit(solution)/shard_map/all_to_all | solution.py:460
  104.1 4.5 %all-to-all-start.4 = ((bf16[16,4,64,256]{3,2,1,0:T(8,128)(2,1)}), bf16[16,4,64,256]{3,2,1,0:T(8,128)(2,1)}, u32[]{:S(2)}, u32[]{:S(2)}) async-start(bf16[16,4,64,256]{3,2,1,0:T(8,128)(2,1)} %bitcast.41), calls=%async_computation.4 | async-start | bytes 4194304 | tf_op jit(solution)/shard_map/all_to_all | solution.py:460
  108.7 1.4 reduce_sum.53
  110.5 3.3 %collective-permute-start.7 = (bf16[32,256]{1,0:T(8,128)(2,1)S(1)}, bf16[32,256]{1,0:T(8,128)(2,1)S(1)}, u32[]{:S(2)}, u32[]{:S(2)}) collective-permute-start(bf16[32,256]{1,0:T(8,128)(2,1)S(1)} %get-tuple-element.109), channel_id=1, source_target_pairs={{0,48},{16,0},{32,16},{48,32},{1,49},{17,1},{33,17},{49,33},{2,50}... | collective-permute-start | bytes 49160 | tf_op jit(solution)/shard_map/ppermute | solution.py:456
  113.8 1.6 %collective-permute-start.6 = (bf16[32,256]{1,0:T(8,128)(2,1)S(1)}, bf16[32,256]{1,0:T(8,128)(2,1)S(1)}, u32[]{:S(2)}, u32[]{:S(2)}) collective-permute-start(bf16[32,256]{1,0:T(8,128)(2,1)S(1)} %get-tuple-element.110), channel_id=1, source_target_pairs={{0,32},{16,48},{32,0},{48,16},{1,33},{17,49},{33,1},{49,17},{2,34}... | collective-permute-start | bytes 49160 | tf_op jit(solution)/shard_map/ppermute | solution.py:456
  115.4 5.2 %collective-permute-done.6 = bf16[32,256]{1,0:T(8,128)(2,1)S(1)} collective-permute-done((bf16[32,256]{1,0:T(8,128)(2,1)S(1)}, bf16[32,256]{1,0:T(8,128)(2,1)S(1)}, u32[]{:S(2)}, u32[]{:S(2)}) %collective-permute-start.6) | collective-permute-done | bytes 16416 | tf_op jit(solution)/shard_map/ppermute | solution.py:456
  120.7 1.1 collective-permute-start.8
  122.5 4.8 %collective-permute-start.10 = (f32[1,512]{1,0:T(1,128)S(1)}, f32[1,512]{1,0:T(1,128)S(1)}, u32[]{:S(2)}, u32[]{:S(2)}) collective-permute-start(f32[1,512]{1,0:T(1,128)S(1)} %slice.27), channel_id=1, source_target_pairs={{0,1},{1,2},{2,3},{4,5},{5,6},{6,7},{8,9},{9,10},{10,11},{12,13},{... | collective-permute-start | bytes 6152 | tf_op jit(solution)/shard_map/ppermute | solution.py:568
  128.6 5.8 %shard_map.147 = bf16[1024,512]{1,0:T(8,128)(2,1)} custom-call(s32[1]{0:T(128)} %bitcast.place_ref, bf16[1024,512]{1,0:T(8,128)(2,1)} %get-tuple-element.96.refs_0_, bf16[1536,512]{1,0:T(8,128)(2,1)} %get-tuple-element.86.refs_22_.refs_1_, f32[1,512]{1,0:T(1,128)} %copy-done.5), custom_call_target="tpu_custom_call" | custom-call | flops 1073741824 | bytes 4194304 | tf_op jit(solution)/shard_map/pallas_call | solution.py:62
  135.1 1.7 %all-to-all-done.4 = bf16[16,4,64,256]{3,2,1,0:T(8,128)(2,1)} async-done(((bf16[16,4,64,256]{3,2,1,0:T(8,128)(2,1)}), bf16[16,4,64,256]{3,2,1,0:T(8,128)(2,1)}, u32[]{:S(2)}, u32[]{:S(2)}) %all-to-all-start.4) | async-done | bytes 2097184 | tf_op jit(solution)/shard_map/all_to_all | solution.py:460
  136.8 2.0 %reduce_sum.54 = bf16[4,64,256]{2,1,0:T(8,128)(2,1)S(1)} reduce(bf16[16,4,64,256]{3,2,1,0:T(8,128)(2,1)} %all-to-all-done.4, bf16[]{:T(256)} %constant.50.clone.1), dimensions={0}, to_apply=%region_3.4 | reduce | flops 983040 | bytes 2228226 | tf_op jit(solution)/shard_map/reduce_sum | solution.py:464
  138.8 12.7 %all_to_all.31 = bf16[8,64,256]{2,1,0:T(8,128)(2,1)S(1)} all-to-all(bf16[8,64,256]{2,1,0:T(8,128)(2,1)S(1)} %bitcast.44), channel_id=1, replica_groups=mesh['x'=4,'zh'=4,'y'=4,'zl'=2,'core'=2] {'zh','zl'}, dimensions={0} | all-to-all | bytes 524288 | tf_op jit(solution)/shard_map/all_to_all | solution.py:475
  151.5 4.7 %collective-permute-start.11 = (f32[64,256]{1,0:T(8,128)S(1)}, f32[64,256]{1,0:T(8,128)S(1)}, u32[]{:S(2)}, u32[]{:S(2)}) collective-permute-start(f32[64,256]{1,0:T(8,128)S(1)} %convert_reduce_fusion.2.refs_0_), channel_id=1, source_target_pairs={{0,1},{1,0},{2,3},{3,2},{4,5},{5,4},{6,7},{7,6},{8,9},{9,8},{10,11... | collective-permute-start | bytes 196616 | tf_op jit(solution)/shard_map/ppermute | solution.py:448
  157.7 1.6 shard_map.148
  (42 shorter events, 9.1 us)
Async XLA Ops:
  19.2 1.6 %copy-start.1 = (bf16[4,96,256]{2,1,0:T(8,128)(2,1)}, bf16[4,96,256]{2,1,0:T(8,128)(2,1)S(1)}, u32[]{:S(2)}) copy-start(bf16[4,96,256]{2,1,0:T(8,128)(2,1)S(1)} %all_to_all.30.refs_2_) | copy-start | bytes 589828
  20.8 32.1 %all-to-all-start.1 = ((bf16[16,4,64,256]{3,2,1,0:T(8,128)(2,1)}), bf16[16,4,64,256]{3,2,1,0:T(8,128)(2,1)}, u32[]{:S(2)}, u32[]{:S(2)}) async-start(bf16[16,4,64,256]{3,2,1,0:T(8,128)(2,1)} %broadcast_in_dim.8), calls=%async_computation.1 | async-start | bytes 4194304 | tf_op jit(solution)/shard_map/all_to_all | solution.py:460
  28.4 7.3 %collective-permute-start = (bf16[16,512]{1,0:T(8,128)(2,1)S(1)}, bf16[16,512]{1,0:T(8,128)(2,1)S(1)}, u32[]{:S(2)}, u32[]{:S(2)}) collective-permute-start(bf16[16,512]{1,0:T(8,128)(2,1)S(1)} %slice_bitcast_fusion), channel_id=1, source_target_pairs={{1,0},{2,1},{3,2},{5,4},{6,5},{7,6},{9,8},{10,9},{11,10},{13,12},{... | collective-permute-start | bytes 49160 | tf_op jit(solution)/shard_map/ppermute | solution.py:510
  35.7 0.6 copy-start.4
  39.6 5.9 %collective-permute-start.1 = (bf16[3,512,512]{2,1,0:T(8,128)(2,1)}, bf16[3,512,512]{2,1,0:T(8,128)(2,1)}, u32[]{:S(2)}, u32[]{:S(2)}) collective-permute-start(bf16[3,512,512]{2,1,0:T(8,128)(2,1)} %get-tuple-element.64.refs_2_.refs_23_), channel_id=1, source_target_pairs={{0,1},{1,0},{2,3},{3,2},{4,5},{5,4},{6,7},{7,6},{8,9},{9,8},{10,11... | collective-permute-start | bytes 4718600 | tf_op jit(solution)/shard_map/ppermute | solution.py:448
  39.7 3.9 %collective-permute-start.2 = (bf16[128,1920]{1,0:T(8,128)(2,1)}, bf16[128,1920]{1,0:T(8,128)(2,1)S(1)}, u32[]{:S(2)}, u32[]{:S(2)}) collective-permute-start(bf16[128,1920]{1,0:T(8,128)(2,1)} %bitcast.37), channel_id=1, source_target_pairs={{0,1},{1,0},{2,3},{3,2},{4,5},{5,4},{6,7},{7,6},{8,9},{9,8},{10,11... | collective-permute-start | bytes 1474568 | tf_op jit(solution)/shard_map/ppermute | solution.py:448
  43.6 0.8 copy-start
  53.0 10.0 %collective-permute-start.3 = (bf16[64,64,256]{2,1,0:T(8,128)(2,1)}, bf16[64,64,256]{2,1,0:T(8,128)(2,1)}, u32[]{:S(2)}, u32[]{:S(2)}) collective-permute-start(bf16[64,64,256]{2,1,0:T(8,128)(2,1)} %bitcast.6.refs_0_), channel_id=1, source_target_pairs={{0,1},{1,0},{2,3},{3,2},{4,5},{5,4},{6,7},{7,6},{8,9},{9,8},{10,11... | collective-permute-start | bytes 6291464 | tf_op jit(solution)/shard_map/ppermute | solution.py:448
  58.6 22.0 %all-to-all-start.2 = ((bf16[16,4,32,256]{3,2,1,0:T(8,128)(2,1)}), bf16[16,4,32,256]{3,2,1,0:T(8,128)(2,1)}, u32[]{:S(2)}, u32[]{:S(2)}) async-start(bf16[16,4,32,256]{3,2,1,0:T(8,128)(2,1)} %get-tuple-element.62), calls=%async_computation.2 | async-start | bytes 2097152 | tf_op jit(solution)/shard_map/all_to_all | solution.py:460
  80.7 7.3 %collective-permute-start.4 = (bf16[64,32,256]{2,1,0:T(8,128)(2,1)}, bf16[64,32,256]{2,1,0:T(8,128)(2,1)}, u32[]{:S(2)}, u32[]{:S(2)}) collective-permute-start(bf16[64,32,256]{2,1,0:T(8,128)(2,1)} %bitcast.7.refs_0_), channel_id=1, source_target_pairs={{0,1},{1,0},{2,3},{3,2},{4,5},{5,4},{6,7},{7,6},{8,9},{9,8},{10,11... | collective-permute-start | bytes 3145736 | tf_op jit(solution)/shard_map/ppermute | solution.py:448
  81.8 22.3 %all-to-all-start.3 = ((bf16[16,4,32,256]{3,2,1,0:T(8,128)(2,1)}), bf16[16,4,32,256]{3,2,1,0:T(8,128)(2,1)}, u32[]{:S(2)}, u32[]{:S(2)}) async-start(bf16[16,4,32,256]{3,2,1,0:T(8,128)(2,1)} %bitcast.43), calls=%async_computation.3 | async-start | bytes 2097152 | tf_op jit(solution)/shard_map/all_to_all | solution.py:460
  104.1 32.7 %all-to-all-start.4 = ((bf16[16,4,64,256]{3,2,1,0:T(8,128)(2,1)}), bf16[16,4,64,256]{3,2,1,0:T(8,128)(2,1)}, u32[]{:S(2)}, u32[]{:S(2)}) async-start(bf16[16,4,64,256]{3,2,1,0:T(8,128)(2,1)} %bitcast.41), calls=%async_computation.4 | async-start | bytes 4194304 | tf_op jit(solution)/shard_map/all_to_all | solution.py:460
  110.1 5.3 %collective-permute-start.5 = (bf16[32,256]{1,0:T(8,128)(2,1)S(1)}, bf16[32,256]{1,0:T(8,128)(2,1)S(1)}, u32[]{:S(2)}, u32[]{:S(2)}) collective-permute-start(bf16[32,256]{1,0:T(8,128)(2,1)S(1)} %get-tuple-element.108), channel_id=1, source_target_pairs={{0,16},{16,32},{32,48},{48,0},{1,17},{17,33},{33,49},{49,1},{2,18}... | collective-permute-start | bytes 49160 | tf_op jit(solution)/shard_map/ppermute | solution.py:456
  110.5 5.0 %collective-permute-start.7 = (bf16[32,256]{1,0:T(8,128)(2,1)S(1)}, bf16[32,256]{1,0:T(8,128)(2,1)S(1)}, u32[]{:S(2)}, u32[]{:S(2)}) collective-permute-start(bf16[32,256]{1,0:T(8,128)(2,1)S(1)} %get-tuple-element.109), channel_id=1, source_target_pairs={{0,48},{16,0},{32,16},{48,32},{1,49},{17,1},{33,17},{49,33},{2,50}... | collective-permute-start | bytes 49160 | tf_op jit(solution)/shard_map/ppermute | solution.py:456
  113.8 6.9 %collective-permute-start.6 = (bf16[32,256]{1,0:T(8,128)(2,1)S(1)}, bf16[32,256]{1,0:T(8,128)(2,1)S(1)}, u32[]{:S(2)}, u32[]{:S(2)}) collective-permute-start(bf16[32,256]{1,0:T(8,128)(2,1)S(1)} %get-tuple-element.110), channel_id=1, source_target_pairs={{0,32},{16,48},{32,0},{48,16},{1,33},{17,49},{33,1},{49,17},{2,34}... | collective-permute-start | bytes 49160 | tf_op jit(solution)/shard_map/ppermute | solution.py:456
  120.7 6.6 %collective-permute-start.8 = (f32[32,256]{1,0:T(8,128)S(1)}, f32[32,256]{1,0:T(8,128)S(1)}, u32[]{:S(2)}, u32[]{:S(2)}) collective-permute-start(f32[32,256]{1,0:T(8,128)S(1)} %fusion.2), channel_id=1, source_target_pairs={{0,2},{2,0},{1,3},{3,1},{4,6},{6,4},{5,7},{7,5},{8,10},{10,8},{9,1... | collective-permute-start | bytes 98312 | tf_op jit(solution)/shard_map/ppermute | solution.py:484
  122.5 5.5 %collective-permute-start.10 = (f32[1,512]{1,0:T(1,128)S(1)}, f32[1,512]{1,0:T(1,128)S(1)}, u32[]{:S(2)}, u32[]{:S(2)}) collective-permute-start(f32[1,512]{1,0:T(1,128)S(1)} %slice.27), channel_id=1, source_target_pairs={{0,1},{1,2},{2,3},{4,5},{5,6},{6,7},{8,9},{9,10},{10,11},{12,13},{... | collective-permute-start | bytes 6152 | tf_op jit(solution)/shard_map/ppermute | solution.py:568
  127.4 7.1 %collective-permute-start.9 = (f32[32,256]{1,0:T(8,128)S(1)}, f32[32,256]{1,0:T(8,128)S(1)}, u32[]{:S(2)}, u32[]{:S(2)}) collective-permute-start(f32[32,256]{1,0:T(8,128)S(1)} %add.78), channel_id=1, source_target_pairs={{0,1},{1,0},{2,3},{3,2},{4,5},{5,4},{6,7},{7,6},{8,9},{9,8},{10,11... | collective-permute-start | bytes 98312 | tf_op jit(solution)/shard_map/ppermute | solution.py:448
  128.0 0.6 copy-start.5
  151.5 5.6 %copy-start.2 = (f32[64,256]{1,0:T(8,128)}, f32[64,256]{1,0:T(8,128)S(1)}, u32[]{:S(2)}) copy-start(f32[64,256]{1,0:T(8,128)S(1)} %convert_reduce_fusion.2.refs_0_) | copy-start | bytes 196612
  151.5 5.6 %collective-permute-start.11 = (f32[64,256]{1,0:T(8,128)S(1)}, f32[64,256]{1,0:T(8,128)S(1)}, u32[]{:S(2)}, u32[]{:S(2)}) collective-permute-start(f32[64,256]{1,0:T(8,128)S(1)} %convert_reduce_fusion.2.refs_0_), channel_id=1, source_target_pairs={{0,1},{1,0},{2,3},{3,2},{4,5},{5,4},{6,7},{7,6},{8,9},{9,8},{10,11... | collective-permute-start | bytes 196616 | tf_op jit(solution)/shard_map/ppermute | solution.py:448
  157.1 0.6 copy-start.3

commit v4 on v3

--- a/solution.py
+++ b/solution.py
@@ -12,6 +12,8 @@
 WIDTH = 1920
 HALF = 256
 STEP = 64
+SEAT = 64
+BLOCK = 240
 ALL_VMEM = 2**26 - 2**18
 
 
@@ -77,6 +79,18 @@
     return (index // 16) * 16 + (index % 4) * 4 + (index // 4) % 4
 
 
+def seated(values, seat):
+    return pltpu.roll(values, SEAT * seat, 1) if seat else values
+
+
+def unseated(values, seat):
+    return pltpu.roll(values, HALF - SEAT * seat, 1) if seat else values
+
+
+def shard_of(plane, seat):
+    return (plane // 4) * 16 + seat * 4 + plane % 4
+
+
 def rows(index, size):
     return pl.ds(pl.multiple_of(index * size, size), size)
 
@@ -155,7 +169,7 @@
     need(*ins)
     small_ref[...] = jnp.zeros((8, HALF), f32)
     small_ref[:, :11] = cp_ref[...].astype(f32)
-    small_ref[:1, 128:158] = bias_ref[...].astype(f32)
+    small_ref[:1, 16:46] = bias_ref[...].astype(f32)
 
     def body(at, _):
         tail = small_ref[...] if at == 0 else jnp.zeros((8, HALF), f32)
@@ -213,17 +227,19 @@
 
     def unpack(mine_at, other_at):
         def step(i, _):
-            to = place(i)
             for ref, at in ((mine_ref, mine_at), (other_ref, other_at)):
-                block = ref[i, :32].astype(f32)
-                wide_ref[rows(to, 24), at : at + HALF] = block[:24]
-                if at == 0:
-                    small_ref[rows(to, 8), :] = block[24:, :128]
-                w6_ref[rows(to, 16), at : at + HALF] = ref[i, 32:48]
-                w7_ref[rows(to, 16), at : at + HALF] = ref[i, 48:]
+                block = ref[i, :112].astype(f32)
+                for seat in range(4):
+                    to = shard_of(i, seat)
+                    low = 112 + 32 * seat
+                    wide_ref[rows(to, 24), at : at + HALF] = block[24 * seat : 24 * seat + 24]
+                    if at == 0:
+                        small_ref[rows(to, 8), :] = unseated(block[96:104], seat)[:, :128]
+                    w6_ref[rows(to, 16), at : at + HALF] = ref[i, low : low + 16]
+                    w7_ref[rows(to, 16), at : at + HALF] = ref[i, low + 16 : low + 32]
             return 0
 
-        lax.fori_loop(0, 64, step, 0, unroll=4)
+        lax.fori_loop(0, 16, step, 0)
 
     by_core(core_ref, unpack)
     cp_ref[...] = small_ref[...].T[:16]
@@ -384,17 +400,21 @@
 
     def pack(mine_at, other_at):
         def step(i, _):
-            to = place(i)
-            if mine_at == 0:
-                tail = jnp.concatenate([small_ref[rows(to, 8), :], gb_ref[rows(to, 8), :]], 1)
-            else:
-                tail = jnp.zeros((8, HALF), f32)
-            give_ref[i, :32, :] = jnp.concatenate([g5_ref[rows(to, 24), :], tail], 0).astype(bf16)
-            give_ref[i, 32:48, :] = g6_ref[rows(to, 16), :].astype(bf16)
-            give_ref[i, 48:, :] = g7_ref[rows(to, 16), :].astype(bf16)
+            parts, tail = [], jnp.zeros((8, HALF), f32)
+            for seat in range(4):
+                to = shard_of(i, seat)
+                low = 112 + 32 * seat
+                parts.append(g5_ref[rows(to, 24), :])
+                if mine_at == 0:
+                    own = small_ref[rows(to, 8), :] + gb_ref[rows(to, 8), :]
+                    tail = tail + seated(jnp.concatenate([own, jnp.zeros((8, HALF - 128), f32)], 1), seat)
+                give_ref[i, low : low + 16, :] = g6_ref[rows(to, 16), :].astype(bf16)
+                give_ref[i, low + 16 : low + 32, :] = g7_ref[rows(to, 16), :].astype(bf16)
+            parts += [tail, jnp.zeros((8, HALF), f32)]
+            give_ref[i, :112, :] = jnp.concatenate(parts, 0).astype(bf16)
             return 0
 
-        lax.fori_loop(0, 64, step, 0, unroll=4)
+        lax.fori_loop(0, 16, step, 0)
 
     by_core(core_ref, pack)
 
@@ -427,10 +447,9 @@
         out_ref[256 * j : 256 * j + 256, :] = dot(matrix, jnp.concatenate(parts, 0)).astype(bf16)
 
 
-def finish_kernel(core_ref, ins, outs, scratch, need, give):
-    mine_ref, other_ref = ins
+def finish_kernel(place_ref, zh_ref, mine_ref, other_ref, *refs):
+    to_hbm, outs, sems = refs[:5], refs[5:10], refs[10]
     g5_ref, g6_ref, g7_ref, channel_ref, bias_ref = outs
-    need(*ins)
 
     def body(mine_at, other_at):
         for ref, at in ((mine_ref, mine_at), (other_ref, other_at)):
@@ -438,10 +457,55 @@
             g6_ref[:, at : at + HALF] = ref[32:48, :]
             g7_ref[:, at : at + HALF] = ref[48:, :]
             if at == 0:
-                channel_ref[...] = ref[24:32, :11]
-                bias_ref[...] = ref[24:25, 128:158]
-
-    by_core(core_ref, body)
+                small = sum(jnp.where(zh_ref[0] == seat, unseated(ref[24:32, :], seat), 0.0) for seat in range(4))
+                channel_ref[...] = small[:, :11]
+                bias_ref[...] = small[:1, 16:46]
+
+    by_core(place_ref, body)
+    stores = [pltpu.make_async_copy(a, b, sems.at[i]) for i, (a, b) in enumerate(zip(outs, to_hbm))]
+    for store in stores:
+        store.start()
+    for store in stores:
+        store.wait()
+
+
+def finish(place_at, zh_at, mine, other):
+    shapes = [(24, CH), (16, CH), (16, CH), (8, 11), (1, 30)]
+    vmem = pl.BlockSpec(memory_space=pltpu.VMEM)
+    return pl.pallas_call(
+        finish_kernel,
+        out_shape=[jax.ShapeDtypeStruct(shape, f32) for shape in shapes],
+        in_specs=[pl.BlockSpec(memory_space=pltpu.SMEM)] * 2 + [vmem, vmem],
+        out_specs=[pl.BlockSpec(memory_space=pltpu.HBM)] * 5,
+        scratch_shapes=[pltpu.VMEM(shape, f32) for shape in shapes] + [pltpu.SemaphoreType.DMA((5,))],
+        compiler_params=pltpu.CompilerParams(vmem_limit_bytes=2**23),
+        cost_estimate=pl.CostEstimate(flops=0, bytes_accessed=2**18, transcendentals=0),
+    )(place_at, zh_at, mine, other)
+
+
+def copies_kernel(line, out_ref, block, out_sems):
+    small = sum(seated(line[seat, 16:32, :].astype(f32)[8:], seat) for seat in range(4))
+    parts = [line[seat, :32, :].astype(f32)[:24] for seat in range(4)] + [small, jnp.zeros((8, HALF), f32)]
+    block[:112, :] = jnp.concatenate(parts, 0).astype(bf16)
+    for seat in range(4):
+        block[112 + 32 * seat : 144 + 32 * seat, :] = line[seat, 32:64, :]
+    stores = [pltpu.make_async_copy(block, out_ref.at[k], out_sems.at[k]) for k in range(16)]
+    for store in stores:
+        store.start()
+    for store in stores:
+        store.wait()
+
+
+def copies(line):
+    return pl.pallas_call(
+        copies_kernel,
+        out_shape=jax.ShapeDtypeStruct((16, BLOCK, HALF), bf16),
+        in_specs=[pl.BlockSpec(memory_space=pltpu.VMEM)],
+        out_specs=pl.BlockSpec(memory_space=pltpu.HBM),
+        scratch_shapes=[pltpu.VMEM((BLOCK, HALF), bf16), pltpu.SemaphoreType.DMA((16,))],
+        compiler_params=pltpu.CompilerParams(vmem_limit_bytes=2**23),
+        cost_estimate=pl.CostEstimate(flops=0, bytes_accessed=2**21, transcendentals=0),
+    )(line)
 
 
 def swap_cores(value):
@@ -467,6 +531,11 @@
 def both_halves(summed, core):
     other = swap_cores(summed)
     return jnp.stack([jnp.where(core == 0, summed, other), jnp.where(core == 0, other, summed)])
+
+
+def by_shard(value):
+    parts = [[value[24 * z : 24 * z + 24], value[96:104], value[112 + 32 * z : 144 + 32 * z]] for z in range(4)]
+    return jnp.concatenate(sum(parts, []), 0).reshape(4, 64, HALF)
 
 
 def sum_line(value):
@@ -492,6 +561,7 @@
 def shards(features, w_five, w_six, w_seven, channel_params, w_proj, proj_bias, out_cotangent):
     core = lax.axis_index("core")
     place_at = core.astype(jnp.int32).reshape(1)
+    zh_at = lax.axis_index("zh").astype(jnp.int32).reshape(1)
     inputs, cotangent = features[0], out_cotangent[0]
     square, flat, stack = (512, CH), (512, 128), (64, 32, HALF)
 
@@ -504,7 +574,7 @@
         moved=2**18,
     )
     line = lax.all_to_all(packed, "zh", 0, 0, tiled=True)
-    spread_ab = jnp.broadcast_to(line[None, :, :64], (16, 4, 64, HALF))
+    spread_ab = copies(line)
 
     line, first_rows, late_cotangent = together(line, inputs[:16], cotangent)
     next_row = lax.ppermute(first_rows, ("zl", "core"), [(1, 0), (2, 1), (3, 2)])
@@ -519,15 +589,14 @@
     unfold_other = swap_cores(unfold)
     cot_other = swap_cores(late_cotangent)
     grad_bias = (jnp.sum(late_cotangent.astype(f32), 0) + jnp.sum(cot_other.astype(f32), 0)).reshape(64, 1, 30)
-    grad_bias = jnp.pad(grad_bias, [(0, 0), (0, 7), (0, 98)]).reshape(512, 128)
+    grad_bias = jnp.pad(grad_bias, [(0, 0), (0, 7), (16, 82)]).reshape(512, 128)
 
     mine_ab, spread_c, unfold, unfold_other, cot_other, grad_bias = across_plane(
         spread_ab, spread_c, unfold, unfold_other, cot_other, grad_bias
     )
-    mine_ab = mine_ab.reshape(64, 64, HALF)
     other_ab = swap_cores(mine_ab)
-    bias = jnp.where(core == 0, mine_ab[:, 24, 128:158], other_ab[:, 24, 128:158])
-    bias = bias.reshape(4, 4, 4, 30).transpose(0, 2, 1, 3).reshape(1, WIDTH).astype(f32)
+    bias = jnp.where(core == 0, mine_ab[:, 96, :], other_ab[:, 96, :])
+    bias = bias.reshape(4, 4, 4, SEAT)[..., 16:46].transpose(0, 2, 1, 3).reshape(1, WIDTH).astype(f32)
 
     saved = lambda n: [((n, CH), f32), ((n, CH), f32), ((n, 128), f32)]
     w_shapes = [((1536, CH), bf16), ((1024, CH), bf16), ((1024, CH), bf16)]
@@ -555,7 +624,7 @@
         backward_kernel,
         (place_at, mine_c, other_c, cp, bias, cotangent, cot_other, normed, unit, scale, u7, s7, r7, w7, act_six)
         + (u6, s6, r6, w6, act_five, *saved_five, w5, unfold, unfold_other, grad_bias),
-        [((128, WIDTH), bf16), ((8, CH), f32), ((1024, CH), bf16), ((64, 64, HALF), bf16)],
+        [((128, WIDTH), bf16), ((8, CH), f32), ((1024, CH), bf16), ((16, BLOCK, HALF), bf16)],
         [((CH, WIDTH), bf16), ((CH, 8 * HALF), f32), ((1024, CH), f32), (square, f32), ((256, CH), f32)]
         + [((1536, HALF), f32), ((1024, HALF), f32), ((1024, HALF), f32), (square, bf16), ((256, CH), bf16)]
         + [((1024, HALF), bf16), (flat, f32), ((128, CH), f32)],
@@ -576,17 +645,9 @@
     )
     sum_c = sum_line_by_permutes(sum_plane(plane_c), core)
     grad_proj = proj_rows(sum_c)
-    plane_ab, grad_proj, input_grad = across_plane(give_ab.reshape(16, 4, 64, HALF), grad_proj, input_grad)
-    sum_ab = sum_line(sum_plane(plane_ab))
-    grad_five, grad_six, grad_seven, grad_channel, grad_bias = staged(
-        finish_kernel,
-        (place_at, sum_ab, swap_cores(sum_ab)),
-        [((24, CH), f32), ((16, CH), f32), ((16, CH), f32), ((8, 11), f32), ((1, 30), f32)],
-        [],
-        flops=0,
-        moved=2**18,
-    )
-
+    plane_ab, grad_proj, input_grad = across_plane(give_ab, grad_proj, input_grad)
+    sum_ab = sum_line(by_shard(sum_plane(plane_ab)))
+    grad_five, grad_six, grad_seven, grad_channel, grad_bias = finish(place_at, zh_at, sum_ab, swap_cores(sum_ab))
     return (
         projected[None],
         input_grad[None],

time: 160 us -> 155 us (0.969)
  waiting for transfers between devices: 25.1 us -> 23.1 us
  local copies, waits for them, and re-layouts: 7.99 us -> 6 us
    pallas_call x0 -> x2, Pallas kernels: none -> 2.34 us  [the longest x1 1.51 us: copies(): pl.pallas_call(copies_kernel, out_shape=jax.ShapeDtypeStruct((16, BLOCK,...]
    pallas_call x6 -> x5, Pallas kernels: 41.4 us -> 39.2 us  [staged(): pl.pallas_call(kernel, out_shape=[jax.ShapeDtypeStruct(shape, kind) for s...]
    all_to_all x4, waiting for transfers between devices: 13.7 us -> 11.5 us  [across_plane(): lax.all_to_all(value, ('x', 'y'), 0, 0, tiled=True)]
  transfers between devices with their start and end apart: 16 -> 16, of which waited for: 9 -> 8; matrix products, arithmetic and copies ran while one was open for 5% -> 5% of each run, Pallas kernels for 24% -> 24%
where the time goes in v4:
time: 155 us
  starting transfers between devices  48.2 us (31%)
  Pallas kernels  41.5 us (27%)
  blocking collectives  29.1 us (19%)
  waiting for transfers between devices  23.1 us (15%)
  local copies, waits for them, and re-layouts  6 us (4%)
  other arithmetic  5.53 us (4%)
    pallas_call x5, Pallas kernels, staged(): pl.pallas_call(kernel, out_shape=[jax.ShapeDtypeStruct(shape, kind) for s...  39.2 us
    all_to_all x4, starting transfers between devices, across_plane(): lax.all_to_all(value, ('x', 'y'), 0, 0, tiled=True)  19.9 us
    all_to_all x1, blocking collectives, shards(): line = lax.all_to_all(packed, 'zh', 0, 0, tiled=True)  17 us
    ppermute x6, starting transfers between devices, swap_cores(): return lax.ppermute(value, 'core', [(0, 1), (1, 0)])  12.1 us
    all_to_all x1, blocking collectives, sum_line(): line = lax.all_to_all(line, ('zh', 'zl'), 0, 0, tiled=True)  12.1 us
    all_to_all x4, waiting for transfers between devices, across_plane(): lax.all_to_all(value, ('x', 'y'), 0, 0, tiled=True)  11.5 us
    ppermute x3, waiting for transfers between devices, around(): lax.ppermute(value, axis, [(i, (i + back) % size) for i in range(size)])  5.38 us
    ppermute x1, starting transfers between devices, shards(): carried = lax.ppermute(edge[7:8], ('zl', 'core'), [(0, 1), (1, 2), (2, 3)])  5.2 us
  transfers between devices with their start and end apart: 16, of which 8 were waited for; matrix products, arithmetic and copies ran while one was open for 5% of the time, Pallas kernels for 24%

profile of v4, /device:TPU:1, one launch (start us, length us, event | category | flops | bytes accessed | tf_op | source)
XLA Modules:
  0.0 154.6 jit_solution(187774151563862816)
XLA Ops:
  0.6 1.6 %shard_map.143 = bf16[4,96,256]{2,1,0:T(8,128)(2,1)} custom-call(s32[1]{0:T(128)} %bitcast.place_ref, bf16[24,512]{1,0:T(8,128)(2,1)} %refs_0_.1, bf16[16,512]{1,0:T(8,128)(2,1)} %refs_1_.1, bf16[16,512]{1,0:T(8,128)(2,1)} %refs_2_.1, bf16[8,1920]{1,0:T(8,128)(2,1)} %refs_3_.1, bf16[8,11]{1,0:T(8,128)(2,1)} %refs_4_.1, bf16[1,30]{1,0:T(2,128)(2,1)} %bitcast.45), custom_call_target="tpu_custom_call" | custom-call | bytes 262144 | tf_op jit(solution)/shard_map/pallas_call | solution.py:64
  2.3 17.0 %all_to_all.30.line.refs_2_ = bf16[4,96,256]{2,1,0:T(8,128)(2,1)S(1)} all-to-all(bf16[4,96,256]{2,1,0:T(8,128)(2,1)} %shard_map.143), channel_id=1, replica_groups=mesh['x'=4,'zh'=4,'y'=4,'zl'=2,'core'=2] {'zh'}, dimensions={0} | all-to-all | bytes 393216 | tf_op jit(solution)/shard_map/all_to_all | solution.py:576
  19.3 1.5 shard_map.144
  20.8 6.8 %all-to-all-start.1 = ((bf16[16,240,256]{2,1,0:T(8,128)(2,1)}), bf16[16,240,256]{2,1,0:T(8,128)(2,1)}, u32[]{:S(2)}, u32[]{:S(2)}) async-start(bf16[16,240,256]{2,1,0:T(8,128)(2,1)} %shard_map.144), calls=%async_computation.1 | async-start | bytes 3932160 | tf_op jit(solution)/shard_map/all_to_all | solution.py:524
  28.4 5.0 %collective-permute-start = (bf16[16,512]{1,0:T(8,128)(2,1)S(1)}, bf16[16,512]{1,0:T(8,128)(2,1)S(1)}, u32[]{:S(2)}, u32[]{:S(2)}) collective-permute-start(bf16[16,512]{1,0:T(8,128)(2,1)S(1)} %slice_bitcast_fusion), channel_id=1, source_target_pairs={{1,0},{2,1},{3,2},{5,4},{6,5},{7,6},{9,8},{10,9},{11,10},{13,12},{... | collective-permute-start | bytes 49160 | tf_op jit(solution)/shard_map/ppermute | solution.py:580
  33.4 2.4 %collective-permute-done.refs_1_ = bf16[16,512]{1,0:T(8,128)(2,1)S(1)} collective-permute-done((bf16[16,512]{1,0:T(8,128)(2,1)S(1)}, bf16[16,512]{1,0:T(8,128)(2,1)S(1)}, u32[]{:S(2)}, u32[]{:S(2)}) %collective-permute-start) | collective-permute-done | bytes 16416 | tf_op jit(solution)/shard_map/ppermute | solution.py:580
  36.3 3.2 %shard_map.145 = (bf16[3,512,512]{2,1,0:T(8,128)(2,1)}, bf16[16,4,32,256]{3,2,1,0:T(8,128)(2,1)}) custom-call(s32[1]{0:T(128)} %bitcast.place_ref, bf16[1024,512]{1,0:T(8,128)(2,1)} %bitcast.39, bf16[16,512]{1,0:T(8,128)(2,1)} %copy-done.2, bf16[4,96,256]{2,1,0:T(8,128)(2,1)} %copy-done), custom_call_target="tpu_custom_call" | custom-call | flops 268435456 | bytes 3145728 | tf_op jit(solution)/shard_map/pallas_call | solution.py:64
  40.1 1.1 convert_reduce_fusion.1
  41.3 2.3 %collective-permute-done.2.refs_5_ = bf16[128,1920]{1,0:T(8,128)(2,1)S(1)} collective-permute-done((bf16[128,1920]{1,0:T(8,128)(2,1)}, bf16[128,1920]{1,0:T(8,128)(2,1)S(1)}, u32[]{:S(2)}, u32[]{:S(2)}) %collective-permute-start.2) | collective-permute-done | bytes 491552 | tf_op jit(solution)/shard_map/ppermute | solution.py:512
  43.6 0.8 copy-done.1
  44.7 0.9 pad_bitcast_fusion.refs_25_
  45.5 6.1 %all-to-all-done.1.refs_0_ = bf16[16,240,256]{2,1,0:T(8,128)(2,1)} async-done(((bf16[16,240,256]{2,1,0:T(8,128)(2,1)}), bf16[16,240,256]{2,1,0:T(8,128)(2,1)}, u32[]{:S(2)}, u32[]{:S(2)}) %all-to-all-start.1) | async-done | bytes 1966112 | tf_op jit(solution)/shard_map/all_to_all | solution.py:524
  51.6 5.5 %collective-permute-start.3 = (bf16[16,240,256]{2,1,0:T(8,128)(2,1)}, bf16[16,240,256]{2,1,0:T(8,128)(2,1)}, u32[]{:S(2)}, u32[]{:S(2)}) collective-permute-start(bf16[16,240,256]{2,1,0:T(8,128)(2,1)} %all-to-all-done.1.refs_0_), channel_id=1, source_target_pairs={{0,1},{1,0},{2,3},{3,2},{4,5},{5,4},{6,7},{7,6},{8,9},{9,8},{10,11... | collective-permute-start | bytes 5898248 | tf_op jit(solution)/shard_map/ppermute | solution.py:512
  57.1 4.4 %all-to-all-start.2 = ((bf16[16,4,32,256]{3,2,1,0:T(8,128)(2,1)}), bf16[16,4,32,256]{3,2,1,0:T(8,128)(2,1)}, u32[]{:S(2)}, u32[]{:S(2)}) async-start(bf16[16,4,32,256]{3,2,1,0:T(8,128)(2,1)} %get-tuple-element.62), calls=%async_computation.2 | async-start | bytes 2097152 | tf_op jit(solution)/shard_map/all_to_all | solution.py:524
  61.5 15.1 %shard_map.146 = (f32[16,512]{1,0:T(8,128)}, bf16[1536,512]{1,0:T(8,128)(2,1)}, bf16[1024,512]{1,0:T(8,128)(2,1)}, f32[1024,512]{1,0:T(8,128)}, f32[1024,512]{1,...) custom-call(s32[1]{0:T(128)} %bitcast.place_ref, ...), custom_call_target="tpu_custom_call" | custom-call | flops 2147483648 | bytes 16777216 | tf_op jit(solution)/shard_map/pallas_call | solution.py:64
  76.6 2.8 %all-to-all-done.2 = bf16[16,4,32,256]{3,2,1,0:T(8,128)(2,1)} async-done(((bf16[16,4,32,256]{3,2,1,0:T(8,128)(2,1)}), bf16[16,4,32,256]{3,2,1,0:T(8,128)(2,1)}, u32[]{:S(2)}, u32[]{:S(2)}) %all-to-all-start.2) | async-done | bytes 1048608 | tf_op jit(solution)/shard_map/all_to_all | solution.py:524
  79.4 1.1 collective-permute-start.4
  80.5 4.4 %all-to-all-start.3 = ((bf16[16,4,32,256]{3,2,1,0:T(8,128)(2,1)}), bf16[16,4,32,256]{3,2,1,0:T(8,128)(2,1)}, u32[]{:S(2)}, u32[]{:S(2)}) async-start(bf16[16,4,32,256]{3,2,1,0:T(8,128)(2,1)} %bitcast.40), calls=%async_computation.3 | async-start | bytes 2097152 | tf_op jit(solution)/shard_map/all_to_all | solution.py:524
  84.8 0.9 fusion.2
  86.7 13.4 %shard_map.147 = (bf16[128,1920]{1,0:T(8,128)(2,1)}, f32[8,512]{1,0:T(8,128)}, bf16[1024,512]{1,0:T(8,128)(2,1)}, bf16[16,240,256]{2,1,0:T(8,128)(2,1)}) custom-call(s32[1]{0:T(128)} %bitcast.place_ref, bf16[64,32,256]{2,1,0:T(8,128)(2,1)} %bitcast.6.refs_0_, bf16[64,32,256]{2,1,0:T(8,128)(2,1)} %collective-permute-done.4.refs_1_, ...), custom_call_target="tpu_custom_call" | custom-call | flops 2147483648 | bytes 16777216 | tf_op jit(solution)/shard_map/pallas_call | solution.py:64
  100.1 2.6 %all-to-all-done.3 = bf16[16,4,32,256]{3,2,1,0:T(8,128)(2,1)} async-done(((bf16[16,4,32,256]{3,2,1,0:T(8,128)(2,1)}), bf16[16,4,32,256]{3,2,1,0:T(8,128)(2,1)}, u32[]{:S(2)}, u32[]{:S(2)}) %all-to-all-start.3) | async-done | bytes 1048608 | tf_op jit(solution)/shard_map/all_to_all | solution.py:524
  102.8 4.4 %all-to-all-start.4 = ((bf16[16,240,256]{2,1,0:T(8,128)(2,1)}), bf16[16,240,256]{2,1,0:T(8,128)(2,1)}, u32[]{:S(2)}, u32[]{:S(2)}) async-start(bf16[16,240,256]{2,1,0:T(8,128)(2,1)} %get-tuple-element.94), calls=%async_computation.4 | async-start | bytes 3932160 | tf_op jit(solution)/shard_map/all_to_all | solution.py:524
  107.2 1.4 reduce_sum.53
  108.8 3.6 %collective-permute-start.7 = (bf16[32,256]{1,0:T(8,128)(2,1)S(1)}, bf16[32,256]{1,0:T(8,128)(2,1)S(1)}, u32[]{:S(2)}, u32[]{:S(2)}) collective-permute-start(bf16[32,256]{1,0:T(8,128)(2,1)S(1)} %get-tuple-element.109), channel_id=1, source_target_pairs={{0,48},{16,0},{32,16},{48,32},{1,49},{17,1},{33,17},{49,33},{2,50}... | collective-permute-start | bytes 49160 | tf_op jit(solution)/shard_map/ppermute | solution.py:520
  112.3 1.5 collective-permute-start.6
  113.9 5.4 %collective-permute-done.6 = bf16[32,256]{1,0:T(8,128)(2,1)S(1)} collective-permute-done((bf16[32,256]{1,0:T(8,128)(2,1)S(1)}, bf16[32,256]{1,0:T(8,128)(2,1)S(1)}, u32[]{:S(2)}, u32[]{:S(2)}) %collective-permute-start.6) | collective-permute-done | bytes 16416 | tf_op jit(solution)/shard_map/ppermute | solution.py:520
  120.8 5.2 %collective-permute-start.10 = (f32[1,512]{1,0:T(1,128)S(1)}, f32[1,512]{1,0:T(1,128)S(1)}, u32[]{:S(2)}, u32[]{:S(2)}) collective-permute-start(f32[1,512]{1,0:T(1,128)S(1)} %slice.58), channel_id=1, source_target_pairs={{0,1},{1,2},{2,3},{4,5},{5,6},{6,7},{8,9},{9,10},{10,11},{12,13},{... | collective-permute-start | bytes 6152 | tf_op jit(solution)/shard_map/ppermute | solution.py:637
  127.3 5.8 %shard_map.148 = bf16[1024,512]{1,0:T(8,128)(2,1)} custom-call(s32[1]{0:T(128)} %bitcast.place_ref, bf16[1024,512]{1,0:T(8,128)(2,1)} %get-tuple-element.96.refs_0_, bf16[1536,512]{1,0:T(8,128)(2,1)} %get-tuple-element.86.refs_22_.refs_1_, f32[1,512]{1,0:T(1,128)} %copy-done.3), custom_call_target="tpu_custom_call" | custom-call | flops 1073741824 | bytes 4194304 | tf_op jit(solution)/shard_map/pallas_call | solution.py:64
  133.7 1.8 %reduce_sum.54 = bf16[240,256]{1,0:T(8,128)(2,1)S(1)} reduce(bf16[16,240,256]{2,1,0:T(8,128)(2,1)} %all-to-all-done.4, bf16[]{:T(256)} %constant.50.clone.1), dimensions={0}, to_apply=%region_3.4 | reduce | flops 921600 | bytes 2088962 | tf_op jit(solution)/shard_map/reduce_sum | solution.py:528
  135.7 12.1 %all_to_all.31 = bf16[8,64,256]{2,1,0:T(8,128)(2,1)S(1)} all-to-all(bf16[8,64,256]{2,1,0:T(8,128)(2,1)S(1)} %bitcast.41), channel_id=1, replica_groups=mesh['x'=4,'zh'=4,'y'=4,'zl'=2,'core'=2] {'zh','zl'}, dimensions={0} | all-to-all | bytes 524288 | tf_op jit(solution)/shard_map/all_to_all | solution.py:544
  147.8 4.8 %collective-permute-start.11 = (f32[64,256]{1,0:T(8,128)S(1)}, f32[64,256]{1,0:T(8,128)S(1)}, u32[]{:S(2)}, u32[]{:S(2)}) collective-permute-start(f32[64,256]{1,0:T(8,128)S(1)} %convert_reduce_fusion.2.mine_ref), channel_id=1, source_target_pairs={{0,1},{1,0},{2,3},{3,2},{4,5},{5,4},{6,7},{7,6},{8,9},{9,8},{10,11... | collective-permute-start | bytes 196616 | tf_op jit(solution)/shard_map/ppermute | solution.py:512
  152.7 0.9 collective-permute-done.11.other_ref
  (50 shorter events, 7.6 us)
Async XLA Ops:
  19.3 1.5 copy-start
  20.8 30.8 %all-to-all-start.1 = ((bf16[16,240,256]{2,1,0:T(8,128)(2,1)}), bf16[16,240,256]{2,1,0:T(8,128)(2,1)}, u32[]{:S(2)}, u32[]{:S(2)}) async-start(bf16[16,240,256]{2,1,0:T(8,128)(2,1)} %shard_map.144), calls=%async_computation.1 | async-start | bytes 3932160 | tf_op jit(solution)/shard_map/all_to_all | solution.py:524
  28.4 7.3 %collective-permute-start = (bf16[16,512]{1,0:T(8,128)(2,1)S(1)}, bf16[16,512]{1,0:T(8,128)(2,1)S(1)}, u32[]{:S(2)}, u32[]{:S(2)}) collective-permute-start(bf16[16,512]{1,0:T(8,128)(2,1)S(1)} %slice_bitcast_fusion), channel_id=1, source_target_pairs={{1,0},{2,1},{3,2},{5,4},{6,5},{7,6},{9,8},{10,9},{11,10},{13,12},{... | collective-permute-start | bytes 49160 | tf_op jit(solution)/shard_map/ppermute | solution.py:580
  35.7 0.6 copy-start.2
  39.5 6.0 %collective-permute-start.1 = (bf16[3,512,512]{2,1,0:T(8,128)(2,1)}, bf16[3,512,512]{2,1,0:T(8,128)(2,1)}, u32[]{:S(2)}, u32[]{:S(2)}) collective-permute-start(bf16[3,512,512]{2,1,0:T(8,128)(2,1)} %get-tuple-element.64.refs_2_.refs_23_), channel_id=1, source_target_pairs={{0,1},{1,0},{2,3},{3,2},{4,5},{5,4},{6,7},{7,6},{8,9},{9,8},{10,11... | collective-permute-start | bytes 4718600 | tf_op jit(solution)/shard_map/ppermute | solution.py:512
  39.6 3.9 %collective-permute-start.2 = (bf16[128,1920]{1,0:T(8,128)(2,1)}, bf16[128,1920]{1,0:T(8,128)(2,1)S(1)}, u32[]{:S(2)}, u32[]{:S(2)}) collective-permute-start(bf16[128,1920]{1,0:T(8,128)(2,1)} %bitcast.35), channel_id=1, source_target_pairs={{0,1},{1,0},{2,3},{3,2},{4,5},{5,4},{6,7},{7,6},{8,9},{9,8},{10,11... | collective-permute-start | bytes 1474568 | tf_op jit(solution)/shard_map/ppermute | solution.py:512
  43.6 0.8 copy-start.1
  51.6 9.9 %collective-permute-start.3 = (bf16[16,240,256]{2,1,0:T(8,128)(2,1)}, bf16[16,240,256]{2,1,0:T(8,128)(2,1)}, u32[]{:S(2)}, u32[]{:S(2)}) collective-permute-start(bf16[16,240,256]{2,1,0:T(8,128)(2,1)} %all-to-all-done.1.refs_0_), channel_id=1, source_target_pairs={{0,1},{1,0},{2,3},{3,2},{4,5},{5,4},{6,7},{7,6},{8,9},{9,8},{10,11... | collective-permute-start | bytes 5898248 | tf_op jit(solution)/shard_map/ppermute | solution.py:512
  57.1 22.3 %all-to-all-start.2 = ((bf16[16,4,32,256]{3,2,1,0:T(8,128)(2,1)}), bf16[16,4,32,256]{3,2,1,0:T(8,128)(2,1)}, u32[]{:S(2)}, u32[]{:S(2)}) async-start(bf16[16,4,32,256]{3,2,1,0:T(8,128)(2,1)} %get-tuple-element.62), calls=%async_computation.2 | async-start | bytes 2097152 | tf_op jit(solution)/shard_map/all_to_all | solution.py:524
  79.4 7.3 %collective-permute-start.4 = (bf16[64,32,256]{2,1,0:T(8,128)(2,1)}, bf16[64,32,256]{2,1,0:T(8,128)(2,1)}, u32[]{:S(2)}, u32[]{:S(2)}) collective-permute-start(bf16[64,32,256]{2,1,0:T(8,128)(2,1)} %bitcast.6.refs_0_), channel_id=1, source_target_pairs={{0,1},{1,0},{2,3},{3,2},{4,5},{5,4},{6,7},{7,6},{8,9},{9,8},{10,11... | collective-permute-start | bytes 3145736 | tf_op jit(solution)/shard_map/ppermute | solution.py:512
  80.5 22.3 %all-to-all-start.3 = ((bf16[16,4,32,256]{3,2,1,0:T(8,128)(2,1)}), bf16[16,4,32,256]{3,2,1,0:T(8,128)(2,1)}, u32[]{:S(2)}, u32[]{:S(2)}) async-start(bf16[16,4,32,256]{3,2,1,0:T(8,128)(2,1)} %bitcast.40), calls=%async_computation.3 | async-start | bytes 2097152 | tf_op jit(solution)/shard_map/all_to_all | solution.py:524
  102.8 31.0 %all-to-all-start.4 = ((bf16[16,240,256]{2,1,0:T(8,128)(2,1)}), bf16[16,240,256]{2,1,0:T(8,128)(2,1)}, u32[]{:S(2)}, u32[]{:S(2)}) async-start(bf16[16,240,256]{2,1,0:T(8,128)(2,1)} %get-tuple-element.94), calls=%async_computation.4 | async-start | bytes 3932160 | tf_op jit(solution)/shard_map/all_to_all | solution.py:524
  108.7 5.2 %collective-permute-start.5 = (bf16[32,256]{1,0:T(8,128)(2,1)S(1)}, bf16[32,256]{1,0:T(8,128)(2,1)S(1)}, u32[]{:S(2)}, u32[]{:S(2)}) collective-permute-start(bf16[32,256]{1,0:T(8,128)(2,1)S(1)} %get-tuple-element.108), channel_id=1, source_target_pairs={{0,16},{16,32},{32,48},{48,0},{1,17},{17,33},{33,49},{49,1},{2,18}... | collective-permute-start | bytes 49160 | tf_op jit(solution)/shard_map/ppermute | solution.py:520
  108.8 5.1 %collective-permute-start.7 = (bf16[32,256]{1,0:T(8,128)(2,1)S(1)}, bf16[32,256]{1,0:T(8,128)(2,1)S(1)}, u32[]{:S(2)}, u32[]{:S(2)}) collective-permute-start(bf16[32,256]{1,0:T(8,128)(2,1)S(1)} %get-tuple-element.109), channel_id=1, source_target_pairs={{0,48},{16,0},{32,16},{48,32},{1,49},{17,1},{33,17},{49,33},{2,50}... | collective-permute-start | bytes 49160 | tf_op jit(solution)/shard_map/ppermute | solution.py:520
  112.3 6.9 %collective-permute-start.6 = (bf16[32,256]{1,0:T(8,128)(2,1)S(1)}, bf16[32,256]{1,0:T(8,128)(2,1)S(1)}, u32[]{:S(2)}, u32[]{:S(2)}) collective-permute-start(bf16[32,256]{1,0:T(8,128)(2,1)S(1)} %get-tuple-element.110), channel_id=1, source_target_pairs={{0,32},{16,48},{32,0},{48,16},{1,33},{17,49},{33,1},{49,17},{2,34}... | collective-permute-start | bytes 49160 | tf_op jit(solution)/shard_map/ppermute | solution.py:520
  119.2 6.7 %collective-permute-start.8 = (f32[32,256]{1,0:T(8,128)S(1)}, f32[32,256]{1,0:T(8,128)S(1)}, u32[]{:S(2)}, u32[]{:S(2)}) collective-permute-start(f32[32,256]{1,0:T(8,128)S(1)} %fusion.1), channel_id=1, source_target_pairs={{0,2},{2,0},{1,3},{3,1},{4,6},{6,4},{5,7},{7,5},{8,10},{10,8},{9,1... | collective-permute-start | bytes 98312 | tf_op jit(solution)/shard_map/ppermute | solution.py:553
  120.8 5.9 %collective-permute-start.10 = (f32[1,512]{1,0:T(1,128)S(1)}, f32[1,512]{1,0:T(1,128)S(1)}, u32[]{:S(2)}, u32[]{:S(2)}) collective-permute-start(f32[1,512]{1,0:T(1,128)S(1)} %slice.58), channel_id=1, source_target_pairs={{0,1},{1,2},{2,3},{4,5},{5,6},{6,7},{8,9},{9,10},{10,11},{12,13},{... | collective-permute-start | bytes 6152 | tf_op jit(solution)/shard_map/ppermute | solution.py:637
  126.0 7.1 %collective-permute-start.9 = (f32[32,256]{1,0:T(8,128)S(1)}, f32[32,256]{1,0:T(8,128)S(1)}, u32[]{:S(2)}, u32[]{:S(2)}) collective-permute-start(f32[32,256]{1,0:T(8,128)S(1)} %add.78), channel_id=1, source_target_pairs={{0,1},{1,0},{2,3},{3,2},{4,5},{5,4},{6,7},{7,6},{8,9},{9,8},{10,11... | collective-permute-start | bytes 98312 | tf_op jit(solution)/shard_map/ppermute | solution.py:512
  126.7 0.6 copy-start.3
  147.8 5.7 %collective-permute-start.11 = (f32[64,256]{1,0:T(8,128)S(1)}, f32[64,256]{1,0:T(8,128)S(1)}, u32[]{:S(2)}, u32[]{:S(2)}) collective-permute-start(f32[64,256]{1,0:T(8,128)S(1)} %convert_reduce_fusion.2.mine_ref), channel_id=1, source_target_pairs={{0,1},{1,0},{2,3},{3,2},{4,5},{5,4},{6,7},{7,6},{8,9},{9,8},{10,11... | collective-permute-start | bytes 196616 | tf_op jit(solution)/shard_map/ppermute | solution.py:512

commit v5 on v4

--- a/solution.py
+++ b/solution.py
@@ -11,7 +11,7 @@
 CH = 512
 WIDTH = 1920
 HALF = 256
-STEP = 64
+STEP = 128
 SEAT = 64
 BLOCK = 240
 ALL_VMEM = 2**26 - 2**18
@@ -538,11 +538,11 @@
     return jnp.concatenate(sum(parts, []), 0).reshape(4, 64, HALF)
 
 
-def sum_line(value):
+def sum_line(value, meanwhile):
     count = value.shape[1]
     line = jnp.broadcast_to(value[:, None], (4, 2, count, HALF)).reshape(8, count, HALF)
-    line = lax.all_to_all(line, ("zh", "zl"), 0, 0, tiled=True)
-    return jnp.sum(line.astype(f32), 0)
+    line, meanwhile = together(lax.all_to_all(line, ("zh", "zl"), 0, 0, tiled=True), meanwhile)
+    return jnp.sum(line.astype(f32), 0), meanwhile
 
 
 def sum_line_by_permutes(value, core):
@@ -633,8 +633,12 @@
     )
 
     plane_c, give_ab = across_plane(give_c.reshape(16, 4, 32, HALF), give_ab)
-    give_ab, plane_c, d_five = together(give_ab, plane_c, d_five)
+    give_ab, plane_c = together(give_ab, plane_c)
     carried = lax.ppermute(edge[7:8], ("zl", "core"), [(0, 1), (1, 2), (2, 3)])
+    sum_c = sum_line_by_permutes(sum_plane(plane_c), core)
+    grad_proj = proj_rows(sum_c)
+    plane_ab, grad_proj, carried = across_plane(give_ab, grad_proj, carried)
+    part_ab, d_five = together(by_shard(sum_plane(plane_ab)), d_five)
     (input_grad,) = staged(
         input_kernel,
         (place_at, d_five, w5, carried),
@@ -643,10 +647,7 @@
         flops=2**30,
         moved=4 * 2**20,
     )
-    sum_c = sum_line_by_permutes(sum_plane(plane_c), core)
-    grad_proj = proj_rows(sum_c)
-    plane_ab, grad_proj, input_grad = across_plane(give_ab, grad_proj, input_grad)
-    sum_ab = sum_line(by_shard(sum_plane(plane_ab)))
+    sum_ab, input_grad = sum_line(part_ab, input_grad)
     grad_five, grad_six, grad_seven, grad_channel, grad_bias = finish(place_at, zh_at, sum_ab, swap_cores(sum_ab))
     return (
         projected[None],

time: 155 us -> 155 us (level)
  blocking collectives: 29.1 us -> 17 us
  waiting for transfers between devices: 23.1 us -> 31.7 us
  starting transfers between devices: 48.2 us -> 53.5 us
  Pallas kernels: 41.5 us -> 39.8 us
    all_to_all x1 -> x0, blocking collectives: 12.1 us -> none  [sum_line(): line = lax.all_to_all(line, ('zh', 'zl'), 0, 0, tiled=True)]
    ppermute x6, starting transfers between devices: 12.1 us -> 16.9 us  [swap_cores(): return lax.ppermute(value, 'core', [(0, 1), (1, 0)])]
    all_to_all x0 -> x1, starting transfers between devices: none -> 4.05 us  [sum_line(): lax.all_to_all(line, ('zh', 'zl'), 0, 0, tiled=True)]
    all_to_all x0 -> x1, waiting for transfers between devices: none -> 3.54 us  [sum_line(): lax.all_to_all(line, ('zh', 'zl'), 0, 0, tiled=True)]
    all_to_all x4, waiting for transfers between devices: 11.5 us -> 14.9 us  [across_plane(): lax.all_to_all(value, ('x', 'y'), 0, 0, tiled=True)]
    ppermute x1, starting transfers between devices: 5.2 us -> 2.41 us  [shards(): carried = lax.ppermute(edge[7:8], ('zl', 'core'), [(0, 1), (1, 2), (2, 3)])]
    ppermute x1, waiting for transfers between devices: 0.01 us -> 2.35 us  [sum_line_by_permutes(): summed = summed + lax.ppermute(summed, 'zl', [(0, 1), (1, 0)])]
    pallas_call x5, Pallas kernels: 39.2 us -> 37.5 us  [staged(): pl.pallas_call(kernel, out_shape=[jax.ShapeDtypeStruct(shape, kind) for s...]
  transfers between devices with their start and end apart: 16 -> 17, of which waited for: 8 -> 10; matrix products, arithmetic and copies ran while one was open for 5% -> 5% of each run, Pallas kernels for 24% -> 23%
where the time goes in v5:
time: 155 us; the launch traced here: 154 us
  starting transfers between devices  53.5 us (35%)
  Pallas kernels  39.8 us (26%)
  waiting for transfers between devices  31.7 us (20%)
  blocking collectives  17 us (11%)
  local copies, waits for them, and re-layouts  6.15 us (4%)
  other arithmetic  4.93 us (3%)
    pallas_call x5, Pallas kernels, staged(): pl.pallas_call(kernel, out_shape=[jax.ShapeDtypeStruct(shape, kind) for s...  37.5 us
    all_to_all x4, starting transfers between devices, across_plane(): lax.all_to_all(value, ('x', 'y'), 0, 0, tiled=True)  19.2 us
    all_to_all x1, blocking collectives, shards(): line = lax.all_to_all(packed, 'zh', 0, 0, tiled=True)  17 us
    ppermute x6, starting transfers between devices, swap_cores(): return lax.ppermute(value, 'core', [(0, 1), (1, 0)])  16.9 us
    all_to_all x4, waiting for transfers between devices, across_plane(): lax.all_to_all(value, ('x', 'y'), 0, 0, tiled=True)  14.9 us
    ppermute x3, waiting for transfers between devices, around(): lax.ppermute(value, axis, [(i, (i + back) % size) for i in range(size)])  5.28 us
    ppermute x3, starting transfers between devices, around(): lax.ppermute(value, axis, [(i, (i + back) % size) for i in range(size)])  5.17 us
    ppermute x1, starting transfers between devices, shards(): lax.ppermute(first_rows, ('zl', 'core'), [(1, 0), (2, 1), (3, 2)])  4.97 us
  transfers between devices with their start and end apart: 17, of which 10 were waited for; matrix products, arithmetic and copies ran while one was open for 5% of the time, Pallas kernels for 23%

profile of v5, /device:TPU:1, one launch (start us, length us, event | category | flops | bytes accessed | tf_op | source)
XLA Modules:
  0.0 154.3 jit_solution(5213054205206586932)
XLA Ops:
  0.6 1.6 %shard_map.143 = bf16[4,96,256]{2,1,0:T(8,128)(2,1)} custom-call(s32[1]{0:T(128)} %bitcast.place_ref, bf16[24,512]{1,0:T(8,128)(2,1)} %refs_0_.1, bf16[16,512]{1,0:T(8,128)(2,1)} %refs_1_.1, bf16[16,512]{1,0:T(8,128)(2,1)} %refs_2_.1, bf16[8,1920]{1,0:T(8,128)(2,1)} %refs_3_.1, bf16[8,11]{1,0:T(8,128)(2,1)} %refs_4_.1, bf16[1,30]{1,0:T(2,128)(2,1)} %bitcast.44), custom_call_target="tpu_custom_call" | custom-call | bytes 262144 | tf_op jit(solution)/shard_map/pallas_call | solution.py:64
  2.3 17.0 %all_to_all.30.line.refs_2_ = bf16[4,96,256]{2,1,0:T(8,128)(2,1)S(1)} all-to-all(bf16[4,96,256]{2,1,0:T(8,128)(2,1)} %shard_map.143), channel_id=1, replica_groups=mesh['x'=4,'zh'=4,'y'=4,'zl'=2,'core'=2] {'zh'}, dimensions={0} | all-to-all | bytes 393216 | tf_op jit(solution)/shard_map/all_to_all | solution.py:576
  19.3 1.5 shard_map.144
  20.9 6.8 %all-to-all-start.1 = ((bf16[16,240,256]{2,1,0:T(8,128)(2,1)}), bf16[16,240,256]{2,1,0:T(8,128)(2,1)}, u32[]{:S(2)}, u32[]{:S(2)}) async-start(bf16[16,240,256]{2,1,0:T(8,128)(2,1)} %shard_map.144), calls=%async_computation.1 | async-start | bytes 3932160 | tf_op jit(solution)/shard_map/all_to_all | solution.py:524
  28.4 5.0 %collective-permute-start = (bf16[16,512]{1,0:T(8,128)(2,1)S(1)}, bf16[16,512]{1,0:T(8,128)(2,1)S(1)}, u32[]{:S(2)}, u32[]{:S(2)}) collective-permute-start(bf16[16,512]{1,0:T(8,128)(2,1)S(1)} %slice_bitcast_fusion), channel_id=1, source_target_pairs={{1,0},{2,1},{3,2},{5,4},{6,5},{7,6},{9,8},{10,9},{11,10},{13,12},{... | collective-permute-start | bytes 49160 | tf_op jit(solution)/shard_map/ppermute | solution.py:580
  33.4 2.4 %collective-permute-done.refs_1_ = bf16[16,512]{1,0:T(8,128)(2,1)S(1)} collective-permute-done((bf16[16,512]{1,0:T(8,128)(2,1)S(1)}, bf16[16,512]{1,0:T(8,128)(2,1)S(1)}, u32[]{:S(2)}, u32[]{:S(2)}) %collective-permute-start) | collective-permute-done | bytes 16416 | tf_op jit(solution)/shard_map/ppermute | solution.py:580
  36.3 3.2 %shard_map.145 = (bf16[3,512,512]{2,1,0:T(8,128)(2,1)}, bf16[16,4,32,256]{3,2,1,0:T(8,128)(2,1)}) custom-call(s32[1]{0:T(128)} %bitcast.place_ref, bf16[1024,512]{1,0:T(8,128)(2,1)} %bitcast.39, bf16[16,512]{1,0:T(8,128)(2,1)} %copy-done.2, bf16[4,96,256]{2,1,0:T(8,128)(2,1)} %copy-done), custom_call_target="tpu_custom_call" | custom-call | flops 268435456 | bytes 3145728 | tf_op jit(solution)/shard_map/pallas_call | solution.py:64
  40.2 1.1 convert_reduce_fusion.1
  41.3 2.3 %collective-permute-done.2.refs_5_ = bf16[128,1920]{1,0:T(8,128)(2,1)S(1)} collective-permute-done((bf16[128,1920]{1,0:T(8,128)(2,1)}, bf16[128,1920]{1,0:T(8,128)(2,1)S(1)}, u32[]{:S(2)}, u32[]{:S(2)}) %collective-permute-start.2) | collective-permute-done | bytes 491552 | tf_op jit(solution)/shard_map/ppermute | solution.py:512
  45.6 6.0 %all-to-all-done.1.refs_0_ = bf16[16,240,256]{2,1,0:T(8,128)(2,1)} async-done(((bf16[16,240,256]{2,1,0:T(8,128)(2,1)}), bf16[16,240,256]{2,1,0:T(8,128)(2,1)}, u32[]{:S(2)}, u32[]{:S(2)}) %all-to-all-start.1) | async-done | bytes 1966112 | tf_op jit(solution)/shard_map/all_to_all | solution.py:524
  51.6 5.5 %collective-permute-start.3 = (bf16[16,240,256]{2,1,0:T(8,128)(2,1)}, bf16[16,240,256]{2,1,0:T(8,128)(2,1)}, u32[]{:S(2)}, u32[]{:S(2)}) collective-permute-start(bf16[16,240,256]{2,1,0:T(8,128)(2,1)} %all-to-all-done.1.refs_0_), channel_id=1, source_target_pairs={{0,1},{1,0},{2,3},{3,2},{4,5},{5,4},{6,7},{7,6},{8,9},{9,8},{10,11... | collective-permute-start | bytes 5898248 | tf_op jit(solution)/shard_map/ppermute | solution.py:512
  57.1 4.4 %all-to-all-start.2 = ((bf16[16,4,32,256]{3,2,1,0:T(8,128)(2,1)}), bf16[16,4,32,256]{3,2,1,0:T(8,128)(2,1)}, u32[]{:S(2)}, u32[]{:S(2)}) async-start(bf16[16,4,32,256]{3,2,1,0:T(8,128)(2,1)} %get-tuple-element.65), calls=%async_computation.2 | async-start | bytes 2097152 | tf_op jit(solution)/shard_map/all_to_all | solution.py:524
  61.5 13.8 %shard_map.146 = (f32[16,512]{1,0:T(8,128)}, bf16[1536,512]{1,0:T(8,128)(2,1)}, bf16[1024,512]{1,0:T(8,128)(2,1)}, f32[1024,512]{1,0:T(8,128)}, f32[1024,512]{1,...) custom-call(s32[1]{0:T(128)} %bitcast.place_ref, ...), custom_call_target="tpu_custom_call" | custom-call | flops 2147483648 | bytes 16777216 | tf_op jit(solution)/shard_map/pallas_call | solution.py:64
  75.3 4.1 %all-to-all-done.2 = bf16[16,4,32,256]{3,2,1,0:T(8,128)(2,1)} async-done(((bf16[16,4,32,256]{3,2,1,0:T(8,128)(2,1)}), bf16[16,4,32,256]{3,2,1,0:T(8,128)(2,1)}, u32[]{:S(2)}, u32[]{:S(2)}) %all-to-all-start.2) | async-done | bytes 1048608 | tf_op jit(solution)/shard_map/all_to_all | solution.py:524
  79.4 1.1 collective-permute-start.4
  80.5 4.3 %all-to-all-start.3 = ((bf16[16,4,32,256]{3,2,1,0:T(8,128)(2,1)}), bf16[16,4,32,256]{3,2,1,0:T(8,128)(2,1)}, u32[]{:S(2)}, u32[]{:S(2)}) async-start(bf16[16,4,32,256]{3,2,1,0:T(8,128)(2,1)} %bitcast.40), calls=%async_computation.3 | async-start | bytes 2097152 | tf_op jit(solution)/shard_map/all_to_all | solution.py:524
  86.7 13.1 %shard_map.147 = (bf16[128,1920]{1,0:T(8,128)(2,1)}, f32[8,512]{1,0:T(8,128)}, bf16[1024,512]{1,0:T(8,128)(2,1)}, bf16[16,240,256]{2,1,0:T(8,128)(2,1)}) custom-call(s32[1]{0:T(128)} %bitcast.place_ref, bf16[64,32,256]{2,1,0:T(8,128)(2,1)} %bitcast.6.refs_0_, bf16[64,32,256]{2,1,0:T(8,128)(2,1)} %collective-permute-done.4.refs_1_, ...), custom_call_target="tpu_custom_call" | custom-call | flops 2147483648 | bytes 16777216 | tf_op jit(solution)/shard_map/pallas_call | solution.py:64
  99.8 3.0 %all-to-all-done.3 = bf16[16,4,32,256]{3,2,1,0:T(8,128)(2,1)} async-done(((bf16[16,4,32,256]{3,2,1,0:T(8,128)(2,1)}), bf16[16,4,32,256]{3,2,1,0:T(8,128)(2,1)}, u32[]{:S(2)}, u32[]{:S(2)}) %all-to-all-start.3) | async-done | bytes 1048608 | tf_op jit(solution)/shard_map/all_to_all | solution.py:524
  102.8 3.7 %all-to-all-start.4 = ((bf16[16,240,256]{2,1,0:T(8,128)(2,1)}), bf16[16,240,256]{2,1,0:T(8,128)(2,1)S(1)}, u32[]{:S(2)}, u32[]{:S(2)}) async-start(bf16[16,240,256]{2,1,0:T(8,128)(2,1)} %get-tuple-element.96), calls=%async_computation.4 | async-start | bytes 3932160 | tf_op jit(solution)/shard_map/all_to_all | solution.py:524
  106.5 1.4 reduce_sum.53
  108.1 3.6 %collective-permute-start.7 = (bf16[32,256]{1,0:T(8,128)(2,1)S(1)}, bf16[32,256]{1,0:T(8,128)(2,1)S(1)}, u32[]{:S(2)}, u32[]{:S(2)}) collective-permute-start(bf16[32,256]{1,0:T(8,128)(2,1)S(1)} %get-tuple-element.115), channel_id=1, source_target_pairs={{0,48},{16,0},{32,16},{48,32},{1,49},{17,1},{33,17},{49,33},{2,50}... | collective-permute-start | bytes 49160 | tf_op jit(solution)/shard_map/ppermute | solution.py:520
  111.6 1.5 collective-permute-start.6
  113.2 5.3 %collective-permute-done.6 = bf16[32,256]{1,0:T(8,128)(2,1)S(1)} collective-permute-done((bf16[32,256]{1,0:T(8,128)(2,1)S(1)}, bf16[32,256]{1,0:T(8,128)(2,1)S(1)}, u32[]{:S(2)}, u32[]{:S(2)}) %collective-permute-start.6) | collective-permute-done | bytes 16416 | tf_op jit(solution)/shard_map/ppermute | solution.py:520
  119.3 2.3 %collective-permute-done.8 = f32[32,256]{1,0:T(8,128)S(1)} collective-permute-done((f32[32,256]{1,0:T(8,128)S(1)}, f32[32,256]{1,0:T(8,128)S(1)}, u32[]{:S(2)}, u32[]{:S(2)}) %collective-permute-start.8) | collective-permute-done | bytes 32800 | tf_op jit(solution)/shard_map/ppermute | solution.py:553
  121.6 3.6 %collective-permute-start.9 = (f32[32,256]{1,0:T(8,128)S(1)}, f32[32,256]{1,0:T(8,128)S(1)}, u32[]{:S(2)}, u32[]{:S(2)}) collective-permute-start(f32[32,256]{1,0:T(8,128)S(1)} %add.78), channel_id=1, source_target_pairs={{0,1},{1,0},{2,3},{3,2},{4,5},{5,4},{6,7},{7,6},{8,9},{9,8},{10,11... | collective-permute-start | bytes 98312 | tf_op jit(solution)/shard_map/ppermute | solution.py:512
  126.0 2.4 %collective-permute-start.10 = (f32[1,512]{1,0:T(1,128)S(1)}, f32[1,512]{1,0:T(1,128)S(1)}, u32[]{:S(2)}, u32[]{:S(2)}) collective-permute-start(f32[1,512]{1,0:T(1,128)S(1)} %slice.58), channel_id=1, source_target_pairs={{0,1},{1,2},{2,3},{4,5},{5,6},{6,7},{8,9},{9,10},{10,11},{12,13},{... | collective-permute-start | bytes 6152 | tf_op jit(solution)/shard_map/ppermute | solution.py:637
  129.1 1.8 %all-to-all-done.4 = bf16[16,240,256]{2,1,0:T(8,128)(2,1)S(1)} async-done(((bf16[16,240,256]{2,1,0:T(8,128)(2,1)}), bf16[16,240,256]{2,1,0:T(8,128)(2,1)S(1)}, u32[]{:S(2)}, u32[]{:S(2)}) %all-to-all-start.4) | async-done | bytes 1966112 | tf_op jit(solution)/shard_map/all_to_all | solution.py:524
  132.0 4.0 %all-to-all-start.5 = ((bf16[8,64,256]{2,1,0:T(8,128)(2,1)}), bf16[8,64,256]{2,1,0:T(8,128)(2,1)}, u32[]{:S(2)}, u32[]{:S(2)}) async-start(bf16[8,64,256]{2,1,0:T(8,128)(2,1)} %bitcast.19), calls=%async_computation.5 | async-start | bytes 524288 | tf_op jit(solution)/shard_map/all_to_all | solution.py:544
  136.0 5.8 %shard_map.148 = bf16[1024,512]{1,0:T(8,128)(2,1)} custom-call(s32[1]{0:T(128)} %bitcast.place_ref, bf16[1024,512]{1,0:T(8,128)(2,1)} %get-tuple-element.102.refs_0_, bf16[1536,512]{1,0:T(8,128)(2,1)} %get-tuple-element.89.refs_22_.refs_1_, f32[1,512]{1,0:T(1,128)} %copy-done.3), custom_call_target="tpu_custom_call" | custom-call | flops 1073741824 | bytes 4194304 | tf_op jit(solution)/shard_map/pallas_call | solution.py:64
  141.8 3.5 %all-to-all-done.5 = bf16[8,64,256]{2,1,0:T(8,128)(2,1)} async-done(((bf16[8,64,256]{2,1,0:T(8,128)(2,1)}), bf16[8,64,256]{2,1,0:T(8,128)(2,1)}, u32[]{:S(2)}, u32[]{:S(2)}) %all-to-all-start.5) | async-done | bytes 262176 | tf_op jit(solution)/shard_map/all_to_all | solution.py:544
  145.4 1.0 convert_reduce_fusion.2.mine_ref
  146.4 6.1 %collective-permute-start.11 = (f32[64,256]{1,0:T(8,128)S(1)}, f32[64,256]{1,0:T(8,128)S(1)}, u32[]{:S(2)}, u32[]{:S(2)}) collective-permute-start(f32[64,256]{1,0:T(8,128)S(1)} %convert_reduce_fusion.2.mine_ref), channel_id=1, source_target_pairs={{0,1},{1,0},{2,3},{3,2},{4,5},{5,4},{6,7},{7,6},{8,9},{9,8},{10,11... | collective-permute-start | bytes 196616 | tf_op jit(solution)/shard_map/ppermute | solution.py:512
  (51 shorter events, 10.8 us)
Async XLA Ops:
  19.3 1.5 %copy-start = (bf16[4,96,256]{2,1,0:T(8,128)(2,1)}, bf16[4,96,256]{2,1,0:T(8,128)(2,1)S(1)}, u32[]{:S(2)}) copy-start(bf16[4,96,256]{2,1,0:T(8,128)(2,1)S(1)} %all_to_all.30.line.refs_2_) | copy-start | bytes 589828
  20.9 30.8 %all-to-all-start.1 = ((bf16[16,240,256]{2,1,0:T(8,128)(2,1)}), bf16[16,240,256]{2,1,0:T(8,128)(2,1)}, u32[]{:S(2)}, u32[]{:S(2)}) async-start(bf16[16,240,256]{2,1,0:T(8,128)(2,1)} %shard_map.144), calls=%async_computation.1 | async-start | bytes 3932160 | tf_op jit(solution)/shard_map/all_to_all | solution.py:524
  28.4 7.3 %collective-permute-start = (bf16[16,512]{1,0:T(8,128)(2,1)S(1)}, bf16[16,512]{1,0:T(8,128)(2,1)S(1)}, u32[]{:S(2)}, u32[]{:S(2)}) collective-permute-start(bf16[16,512]{1,0:T(8,128)(2,1)S(1)} %slice_bitcast_fusion), channel_id=1, source_target_pairs={{1,0},{2,1},{3,2},{5,4},{6,5},{7,6},{9,8},{10,9},{11,10},{13,12},{... | collective-permute-start | bytes 49160 | tf_op jit(solution)/shard_map/ppermute | solution.py:580
  35.7 0.6 copy-start.2
  39.6 6.0 %collective-permute-start.1 = (bf16[3,512,512]{2,1,0:T(8,128)(2,1)}, bf16[3,512,512]{2,1,0:T(8,128)(2,1)}, u32[]{:S(2)}, u32[]{:S(2)}) collective-permute-start(bf16[3,512,512]{2,1,0:T(8,128)(2,1)} %get-tuple-element.67.refs_2_.refs_23_), channel_id=1, source_target_pairs={{0,1},{1,0},{2,3},{3,2},{4,5},{5,4},{6,7},{7,6},{8,9},{9,8},{10,11... | collective-permute-start | bytes 4718600 | tf_op jit(solution)/shard_map/ppermute | solution.py:512
  39.7 3.9 %collective-permute-start.2 = (bf16[128,1920]{1,0:T(8,128)(2,1)}, bf16[128,1920]{1,0:T(8,128)(2,1)S(1)}, u32[]{:S(2)}, u32[]{:S(2)}) collective-permute-start(bf16[128,1920]{1,0:T(8,128)(2,1)} %bitcast.35), channel_id=1, source_target_pairs={{0,1},{1,0},{2,3},{3,2},{4,5},{5,4},{6,7},{7,6},{8,9},{9,8},{10,11... | collective-permute-start | bytes 1474568 | tf_op jit(solution)/shard_map/ppermute | solution.py:512
  43.6 0.9 copy-start.1
  51.6 9.9 %collective-permute-start.3 = (bf16[16,240,256]{2,1,0:T(8,128)(2,1)}, bf16[16,240,256]{2,1,0:T(8,128)(2,1)}, u32[]{:S(2)}, u32[]{:S(2)}) collective-permute-start(bf16[16,240,256]{2,1,0:T(8,128)(2,1)} %all-to-all-done.1.refs_0_), channel_id=1, source_target_pairs={{0,1},{1,0},{2,3},{3,2},{4,5},{5,4},{6,7},{7,6},{8,9},{9,8},{10,11... | collective-permute-start | bytes 5898248 | tf_op jit(solution)/shard_map/ppermute | solution.py:512
  57.1 22.3 %all-to-all-start.2 = ((bf16[16,4,32,256]{3,2,1,0:T(8,128)(2,1)}), bf16[16,4,32,256]{3,2,1,0:T(8,128)(2,1)}, u32[]{:S(2)}, u32[]{:S(2)}) async-start(bf16[16,4,32,256]{3,2,1,0:T(8,128)(2,1)} %get-tuple-element.65), calls=%async_computation.2 | async-start | bytes 2097152 | tf_op jit(solution)/shard_map/all_to_all | solution.py:524
  79.4 7.3 %collective-permute-start.4 = (bf16[64,32,256]{2,1,0:T(8,128)(2,1)}, bf16[64,32,256]{2,1,0:T(8,128)(2,1)}, u32[]{:S(2)}, u32[]{:S(2)}) collective-permute-start(bf16[64,32,256]{2,1,0:T(8,128)(2,1)} %bitcast.6.refs_0_), channel_id=1, source_target_pairs={{0,1},{1,0},{2,3},{3,2},{4,5},{5,4},{6,7},{7,6},{8,9},{9,8},{10,11... | collective-permute-start | bytes 3145736 | tf_op jit(solution)/shard_map/ppermute | solution.py:512
  80.5 22.3 %all-to-all-start.3 = ((bf16[16,4,32,256]{3,2,1,0:T(8,128)(2,1)}), bf16[16,4,32,256]{3,2,1,0:T(8,128)(2,1)}, u32[]{:S(2)}, u32[]{:S(2)}) async-start(bf16[16,4,32,256]{3,2,1,0:T(8,128)(2,1)} %bitcast.40), calls=%async_computation.3 | async-start | bytes 2097152 | tf_op jit(solution)/shard_map/all_to_all | solution.py:524
  102.8 28.1 %all-to-all-start.4 = ((bf16[16,240,256]{2,1,0:T(8,128)(2,1)}), bf16[16,240,256]{2,1,0:T(8,128)(2,1)S(1)}, u32[]{:S(2)}, u32[]{:S(2)}) async-start(bf16[16,240,256]{2,1,0:T(8,128)(2,1)} %get-tuple-element.96), calls=%async_computation.4 | async-start | bytes 3932160 | tf_op jit(solution)/shard_map/all_to_all | solution.py:524
  108.0 5.2 %collective-permute-start.5 = (bf16[32,256]{1,0:T(8,128)(2,1)S(1)}, bf16[32,256]{1,0:T(8,128)(2,1)S(1)}, u32[]{:S(2)}, u32[]{:S(2)}) collective-permute-start(bf16[32,256]{1,0:T(8,128)(2,1)S(1)} %get-tuple-element.114), channel_id=1, source_target_pairs={{0,16},{16,32},{32,48},{48,0},{1,17},{17,33},{33,49},{49,1},{2,18}... | collective-permute-start | bytes 49160 | tf_op jit(solution)/shard_map/ppermute | solution.py:520
  108.1 5.1 %collective-permute-start.7 = (bf16[32,256]{1,0:T(8,128)(2,1)S(1)}, bf16[32,256]{1,0:T(8,128)(2,1)S(1)}, u32[]{:S(2)}, u32[]{:S(2)}) collective-permute-start(bf16[32,256]{1,0:T(8,128)(2,1)S(1)} %get-tuple-element.115), channel_id=1, source_target_pairs={{0,48},{16,0},{32,16},{48,32},{1,49},{17,1},{33,17},{49,33},{2,50}... | collective-permute-start | bytes 49160 | tf_op jit(solution)/shard_map/ppermute | solution.py:520
  111.6 6.8 %collective-permute-start.6 = (bf16[32,256]{1,0:T(8,128)(2,1)S(1)}, bf16[32,256]{1,0:T(8,128)(2,1)S(1)}, u32[]{:S(2)}, u32[]{:S(2)}) collective-permute-start(bf16[32,256]{1,0:T(8,128)(2,1)S(1)} %get-tuple-element.116), channel_id=1, source_target_pairs={{0,32},{16,48},{32,0},{48,16},{1,33},{17,49},{33,1},{49,17},{2,34}... | collective-permute-start | bytes 49160 | tf_op jit(solution)/shard_map/ppermute | solution.py:520
  118.5 3.1 %collective-permute-start.8 = (f32[32,256]{1,0:T(8,128)S(1)}, f32[32,256]{1,0:T(8,128)S(1)}, u32[]{:S(2)}, u32[]{:S(2)}) collective-permute-start(f32[32,256]{1,0:T(8,128)S(1)} %fusion.1), channel_id=1, source_target_pairs={{0,2},{2,0},{1,3},{3,1},{4,6},{6,4},{5,7},{7,5},{8,10},{10,8},{9,1... | collective-permute-start | bytes 98312 | tf_op jit(solution)/shard_map/ppermute | solution.py:553
  121.6 6.8 %collective-permute-start.9 = (f32[32,256]{1,0:T(8,128)S(1)}, f32[32,256]{1,0:T(8,128)S(1)}, u32[]{:S(2)}, u32[]{:S(2)}) collective-permute-start(f32[32,256]{1,0:T(8,128)S(1)} %add.78), channel_id=1, source_target_pairs={{0,1},{1,0},{2,3},{3,2},{4,5},{5,4},{6,7},{7,6},{8,9},{9,8},{10,11... | collective-permute-start | bytes 98312 | tf_op jit(solution)/shard_map/ppermute | solution.py:512
  126.0 3.1 %collective-permute-start.10 = (f32[1,512]{1,0:T(1,128)S(1)}, f32[1,512]{1,0:T(1,128)S(1)}, u32[]{:S(2)}, u32[]{:S(2)}) collective-permute-start(f32[1,512]{1,0:T(1,128)S(1)} %slice.58), channel_id=1, source_target_pairs={{0,1},{1,2},{2,3},{4,5},{5,6},{6,7},{8,9},{9,10},{10,11},{12,13},{... | collective-permute-start | bytes 6152 | tf_op jit(solution)/shard_map/ppermute | solution.py:637
  129.1 6.9 %copy-start.3 = (f32[1,512]{1,0:T(1,128)}, f32[1,512]{1,0:T(1,128)S(1)}, u32[]{:S(2)}) copy-start(f32[1,512]{1,0:T(1,128)S(1)} %collective-permute-done.10.refs_2_) | copy-start | bytes 6148
  132.0 13.4 %all-to-all-start.5 = ((bf16[8,64,256]{2,1,0:T(8,128)(2,1)}), bf16[8,64,256]{2,1,0:T(8,128)(2,1)}, u32[]{:S(2)}, u32[]{:S(2)}) async-start(bf16[8,64,256]{2,1,0:T(8,128)(2,1)} %bitcast.19), calls=%async_computation.5 | async-start | bytes 524288 | tf_op jit(solution)/shard_map/all_to_all | solution.py:544
  146.4 7.0 %collective-permute-start.11 = (f32[64,256]{1,0:T(8,128)S(1)}, f32[64,256]{1,0:T(8,128)S(1)}, u32[]{:S(2)}, u32[]{:S(2)}) collective-permute-start(f32[64,256]{1,0:T(8,128)S(1)} %convert_reduce_fusion.2.mine_ref), channel_id=1, source_target_pairs={{0,1},{1,0},{2,3},{3,2},{4,5},{5,4},{6,7},{7,6},{8,9},{9,8},{10,11... | collective-permute-start | bytes 196616 | tf_op jit(solution)/shard_map/ppermute | solution.py:512

commit v6 on v5

--- a/solution.py
+++ b/solution.py
@@ -162,18 +162,16 @@
     return (position == 8 * (group % 32) + group // 32).astype(bf16)
 
 
-def pack_kernel(place_ref, ins, outs, scratch, need, give):
-    w5_ref, w6_ref, w7_ref, wp_ref, cp_ref, bias_ref = ins
-    (out_ref,) = outs
-    (small_ref,) = scratch
-    need(*ins)
-    small_ref[...] = jnp.zeros((8, HALF), f32)
-    small_ref[:, :11] = cp_ref[...].astype(f32)
-    small_ref[:1, 16:46] = bias_ref[...].astype(f32)
+def pack_kernel(place_ref, w5_ref, wp_ref, small_ref, w6_hbm, w7_hbm, out_hbm, w6_ref, w7_ref, out_ref, sems):
+    loads = [pltpu.make_async_copy(w6_hbm, w6_ref, sems.at[0]), pltpu.make_async_copy(w7_hbm, w7_ref, sems.at[1])]
+    for load in loads:
+        load.start()
+    for load in loads:
+        load.wait()
 
     def body(at, _):
-        tail = small_ref[...] if at == 0 else jnp.zeros((8, HALF), f32)
-        first = jnp.concatenate([w5_ref[:, at : at + HALF].astype(f32), tail], 0).astype(bf16)
+        both = [w5_ref[:, at : at + HALF].astype(f32), small_ref[:, at : at + HALF].astype(f32)]
+        first = jnp.concatenate(both, 0).astype(bf16)
         parts = []
         for b in range(4):
             start = 4 * at + HALF * b
@@ -189,6 +187,23 @@
             out_ref[k, 64:, :] = last
 
     by_core(place_ref, body)
+    store = pltpu.make_async_copy(out_ref, out_hbm, sems.at[2])
+    store.start()
+    store.wait()
+
+
+def pack(place_at, w_five, w_proj, small, w_six, w_seven):
+    vmem, hbm = pl.BlockSpec(memory_space=pltpu.VMEM), pl.BlockSpec(memory_space=pltpu.HBM)
+    return pl.pallas_call(
+        pack_kernel,
+        out_shape=jax.ShapeDtypeStruct((4, 96, HALF), bf16),
+        in_specs=[pl.BlockSpec(memory_space=pltpu.SMEM), vmem, vmem, vmem, hbm, hbm],
+        out_specs=hbm,
+        scratch_shapes=[pltpu.VMEM((16, CH), bf16), pltpu.VMEM((16, CH), bf16), pltpu.VMEM((4, 96, HALF), bf16)]
+        + [pltpu.SemaphoreType.DMA((3,))],
+        compiler_params=pltpu.CompilerParams(vmem_limit_bytes=2**23),
+        cost_estimate=pl.CostEstimate(flops=0, bytes_accessed=2**18, transcendentals=0),
+    )(place_at, w_five, w_proj, small, w_six, w_seven)
 
 
 def split_kernel(place_ref, ins, outs, scratch, need, give):
@@ -565,14 +580,8 @@
     inputs, cotangent = features[0], out_cotangent[0]
     square, flat, stack = (512, CH), (512, 128), (64, 32, HALF)
 
-    (packed,) = staged(
-        pack_kernel,
-        (place_at, w_five, w_six, w_seven, w_proj, channel_params, proj_bias.reshape(1, 30)),
-        [((4, 96, HALF), bf16)],
-        [((8, HALF), f32)],
-        flops=0,
-        moved=2**18,
-    )
+    small = jnp.pad(channel_params, [(0, 0), (0, 501)]) + jnp.pad(proj_bias[None], [(0, 7), (16, 466)])
+    packed = pack(place_at, w_five, w_proj, small, w_six, w_seven)
     line = lax.all_to_all(packed, "zh", 0, 0, tiled=True)
     spread_ab = copies(line)
 

time: 155 us -> 158 us (1.019)
  local copies, waits for them, and re-layouts: 6.15 us -> 9.06 us
    unnamed x18 -> x26, local copies, waits for them, and re-layouts: 1.5 us -> 4.41 us
    pallas_call x5 -> x4, Pallas kernels: 37.5 us -> 35.8 us  [staged(): pl.pallas_call(kernel, out_shape=[jax.ShapeDtypeStruct(shape, kind) for s...]
where the time goes in v6:
time: 158 us; the launch traced here: 156 us
  starting transfers between devices  53.6 us (34%)
  Pallas kernels  38.5 us (24%)
  waiting for transfers between devices  31.7 us (20%)
  blocking collectives  16.8 us (11%)
  local copies, waits for them, and re-layouts  9.06 us (6%)
  other arithmetic  5.7 us (4%)
    pallas_call x4, Pallas kernels, staged(): pl.pallas_call(kernel, out_shape=[jax.ShapeDtypeStruct(shape, kind) for s...  35.8 us
    all_to_all x4, starting transfers between devices, across_plane(): lax.all_to_all(value, ('x', 'y'), 0, 0, tiled=True)  19.2 us
    ppermute x6, starting transfers between devices, swap_cores(): return lax.ppermute(value, 'core', [(0, 1), (1, 0)])  16.9 us
    all_to_all x1, blocking collectives, shards(): line = lax.all_to_all(packed, 'zh', 0, 0, tiled=True)  16.8 us
    all_to_all x4, waiting for transfers between devices, across_plane(): lax.all_to_all(value, ('x', 'y'), 0, 0, tiled=True)  14.9 us
    ppermute x3, waiting for transfers between devices, around(): lax.ppermute(value, axis, [(i, (i + back) % size) for i in range(size)])  5.24 us
    ppermute x3, starting transfers between devices, around(): lax.ppermute(value, axis, [(i, (i + back) % size) for i in range(size)])  5.19 us
    ppermute x1, starting transfers between devices, shards(): lax.ppermute(first_rows, ('zl', 'core'), [(1, 0), (2, 1), (3, 2)])  4.98 us
  transfers between devices with their start and end apart: 17, of which 10 were waited for; matrix products, arithmetic and copies ran while one was open for 5% of the time, Pallas kernels for 23%

profile of v6, /device:TPU:1, one launch (start us, length us, event | category | flops | bytes accessed | tf_op | source)
XLA Modules:
  0.0 156.5 jit_solution(12963269434360043764)
XLA Ops:
  4.7 16.8 %all_to_all.30.line.refs_2_ = bf16[4,96,256]{2,1,0:T(8,128)(2,1)S(1)} all-to-all(bf16[4,96,256]{2,1,0:T(8,128)(2,1)S(1)} %shard_map.143), channel_id=1, replica_groups=mesh['x'=4,'zh'=4,'y'=4,'zl'=2,'core'=2] {'zh'}, dimensions={0} | all-to-all | bytes 393216 | tf_op jit(solution)/shard_map/all_to_all | solution.py:585
  21.5 1.5 shard_map.144
  23.0 6.8 %all-to-all-start.1 = ((bf16[16,240,256]{2,1,0:T(8,128)(2,1)}), bf16[16,240,256]{2,1,0:T(8,128)(2,1)}, u32[]{:S(2)}, u32[]{:S(2)}) async-start(bf16[16,240,256]{2,1,0:T(8,128)(2,1)} %shard_map.144), calls=%async_computation.1 | async-start | bytes 3932160 | tf_op jit(solution)/shard_map/all_to_all | solution.py:539
  30.6 5.0 %collective-permute-start = (bf16[16,512]{1,0:T(8,128)(2,1)S(1)}, bf16[16,512]{1,0:T(8,128)(2,1)S(1)}, u32[]{:S(2)}, u32[]{:S(2)}) collective-permute-start(bf16[16,512]{1,0:T(8,128)(2,1)S(1)} %slice_bitcast_fusion), channel_id=1, source_target_pairs={{1,0},{2,1},{3,2},{5,4},{6,5},{7,6},{9,8},{10,9},{11,10},{13,12},{... | collective-permute-start | bytes 49160 | tf_op jit(solution)/shard_map/ppermute | solution.py:589
  35.5 2.4 %collective-permute-done.refs_1_ = bf16[16,512]{1,0:T(8,128)(2,1)S(1)} collective-permute-done((bf16[16,512]{1,0:T(8,128)(2,1)S(1)}, bf16[16,512]{1,0:T(8,128)(2,1)S(1)}, u32[]{:S(2)}, u32[]{:S(2)}) %collective-permute-start) | collective-permute-done | bytes 16416 | tf_op jit(solution)/shard_map/ppermute | solution.py:589
  38.5 3.2 %shard_map.145 = (bf16[3,512,512]{2,1,0:T(8,128)(2,1)}, bf16[16,4,32,256]{3,2,1,0:T(8,128)(2,1)}) custom-call(s32[1]{0:T(128)} %bitcast.place_ref, bf16[1024,512]{1,0:T(8,128)(2,1)} %bitcast.39, bf16[16,512]{1,0:T(8,128)(2,1)} %copy-done.6, bf16[4,96,256]{2,1,0:T(8,128)(2,1)} %copy-done), custom_call_target="tpu_custom_call" | custom-call | flops 268435456 | bytes 3145728 | tf_op jit(solution)/shard_map/pallas_call | solution.py:64
  42.3 1.1 convert_reduce_fusion.1
  43.5 2.3 %collective-permute-done.2.refs_5_ = bf16[128,1920]{1,0:T(8,128)(2,1)S(1)} collective-permute-done((bf16[128,1920]{1,0:T(8,128)(2,1)}, bf16[128,1920]{1,0:T(8,128)(2,1)S(1)}, u32[]{:S(2)}, u32[]{:S(2)}) %collective-permute-start.2) | collective-permute-done | bytes 491552 | tf_op jit(solution)/shard_map/ppermute | solution.py:527
  47.7 6.1 %all-to-all-done.1.refs_0_ = bf16[16,240,256]{2,1,0:T(8,128)(2,1)} async-done(((bf16[16,240,256]{2,1,0:T(8,128)(2,1)}), bf16[16,240,256]{2,1,0:T(8,128)(2,1)}, u32[]{:S(2)}, u32[]{:S(2)}) %all-to-all-start.1) | async-done | bytes 1966112 | tf_op jit(solution)/shard_map/all_to_all | solution.py:539
  53.8 5.5 %collective-permute-start.3 = (bf16[16,240,256]{2,1,0:T(8,128)(2,1)}, bf16[16,240,256]{2,1,0:T(8,128)(2,1)}, u32[]{:S(2)}, u32[]{:S(2)}) collective-permute-start(bf16[16,240,256]{2,1,0:T(8,128)(2,1)} %all-to-all-done.1.refs_0_), channel_id=1, source_target_pairs={{0,1},{1,0},{2,3},{3,2},{4,5},{5,4},{6,7},{7,6},{8,9},{9,8},{10,11... | collective-permute-start | bytes 5898248 | tf_op jit(solution)/shard_map/ppermute | solution.py:527
  59.3 4.3 %all-to-all-start.2 = ((bf16[16,4,32,256]{3,2,1,0:T(8,128)(2,1)}), bf16[16,4,32,256]{3,2,1,0:T(8,128)(2,1)}, u32[]{:S(2)}, u32[]{:S(2)}) async-start(bf16[16,4,32,256]{3,2,1,0:T(8,128)(2,1)} %get-tuple-element.65), calls=%async_computation.2 | async-start | bytes 2097152 | tf_op jit(solution)/shard_map/all_to_all | solution.py:539
  63.6 13.8 %shard_map.146 = (f32[16,512]{1,0:T(8,128)}, bf16[1536,512]{1,0:T(8,128)(2,1)}, bf16[1024,512]{1,0:T(8,128)(2,1)}, f32[1024,512]{1,0:T(8,128)}, f32[1024,512]{1,...) custom-call(s32[1]{0:T(128)} %bitcast.place_ref, ...), custom_call_target="tpu_custom_call" | custom-call | flops 2147483648 | bytes 16777216 | tf_op jit(solution)/shard_map/pallas_call | solution.py:64
  77.4 4.1 %all-to-all-done.2 = bf16[16,4,32,256]{3,2,1,0:T(8,128)(2,1)} async-done(((bf16[16,4,32,256]{3,2,1,0:T(8,128)(2,1)}), bf16[16,4,32,256]{3,2,1,0:T(8,128)(2,1)}, u32[]{:S(2)}, u32[]{:S(2)}) %all-to-all-start.2) | async-done | bytes 1048608 | tf_op jit(solution)/shard_map/all_to_all | solution.py:539
  81.6 1.1 collective-permute-start.4
  82.6 4.4 %all-to-all-start.3 = ((bf16[16,4,32,256]{3,2,1,0:T(8,128)(2,1)}), bf16[16,4,32,256]{3,2,1,0:T(8,128)(2,1)}, u32[]{:S(2)}, u32[]{:S(2)}) async-start(bf16[16,4,32,256]{3,2,1,0:T(8,128)(2,1)} %bitcast.40), calls=%async_computation.3 | async-start | bytes 2097152 | tf_op jit(solution)/shard_map/all_to_all | solution.py:539
  87.0 0.9 fusion.2
  88.9 13.1 %shard_map.147 = (bf16[128,1920]{1,0:T(8,128)(2,1)}, f32[8,512]{1,0:T(8,128)}, bf16[1024,512]{1,0:T(8,128)(2,1)}, bf16[16,240,256]{2,1,0:T(8,128)(2,1)}) custom-call(s32[1]{0:T(128)} %bitcast.place_ref, bf16[64,32,256]{2,1,0:T(8,128)(2,1)} %bitcast.6.refs_0_, bf16[64,32,256]{2,1,0:T(8,128)(2,1)} %collective-permute-done.4.refs_1_, ...), custom_call_target="tpu_custom_call" | custom-call | flops 2147483648 | bytes 16777216 | tf_op jit(solution)/shard_map/pallas_call | solution.py:64
  102.0 3.0 %all-to-all-done.3 = bf16[16,4,32,256]{3,2,1,0:T(8,128)(2,1)} async-done(((bf16[16,4,32,256]{3,2,1,0:T(8,128)(2,1)}), bf16[16,4,32,256]{3,2,1,0:T(8,128)(2,1)}, u32[]{:S(2)}, u32[]{:S(2)}) %all-to-all-start.3) | async-done | bytes 1048608 | tf_op jit(solution)/shard_map/all_to_all | solution.py:539
  104.9 3.7 %all-to-all-start.4 = ((bf16[16,240,256]{2,1,0:T(8,128)(2,1)}), bf16[16,240,256]{2,1,0:T(8,128)(2,1)S(1)}, u32[]{:S(2)}, u32[]{:S(2)}) async-start(bf16[16,240,256]{2,1,0:T(8,128)(2,1)} %get-tuple-element.96), calls=%async_computation.4 | async-start | bytes 3932160 | tf_op jit(solution)/shard_map/all_to_all | solution.py:539
  108.7 1.4 reduce_sum.53
  110.2 3.6 %collective-permute-start.7 = (bf16[32,256]{1,0:T(8,128)(2,1)S(1)}, bf16[32,256]{1,0:T(8,128)(2,1)S(1)}, u32[]{:S(2)}, u32[]{:S(2)}) collective-permute-start(bf16[32,256]{1,0:T(8,128)(2,1)S(1)} %get-tuple-element.115), channel_id=1, source_target_pairs={{0,48},{16,0},{32,16},{48,32},{1,49},{17,1},{33,17},{49,33},{2,50}... | collective-permute-start | bytes 49160 | tf_op jit(solution)/shard_map/ppermute | solution.py:535
  113.8 1.5 collective-permute-start.6
  115.3 5.2 %collective-permute-done.6 = bf16[32,256]{1,0:T(8,128)(2,1)S(1)} collective-permute-done((bf16[32,256]{1,0:T(8,128)(2,1)S(1)}, bf16[32,256]{1,0:T(8,128)(2,1)S(1)}, u32[]{:S(2)}, u32[]{:S(2)}) %collective-permute-start.6) | collective-permute-done | bytes 16416 | tf_op jit(solution)/shard_map/ppermute | solution.py:535
  121.4 2.3 %collective-permute-done.8 = f32[32,256]{1,0:T(8,128)S(1)} collective-permute-done((f32[32,256]{1,0:T(8,128)S(1)}, f32[32,256]{1,0:T(8,128)S(1)}, u32[]{:S(2)}, u32[]{:S(2)}) %collective-permute-start.8) | collective-permute-done | bytes 32800 | tf_op jit(solution)/shard_map/ppermute | solution.py:568
  123.7 3.7 %collective-permute-start.9 = (f32[32,256]{1,0:T(8,128)S(1)}, f32[32,256]{1,0:T(8,128)S(1)}, u32[]{:S(2)}, u32[]{:S(2)}) collective-permute-start(f32[32,256]{1,0:T(8,128)S(1)} %add.86), channel_id=1, source_target_pairs={{0,1},{1,0},{2,3},{3,2},{4,5},{5,4},{6,7},{7,6},{8,9},{9,8},{10,11... | collective-permute-start | bytes 98312 | tf_op jit(solution)/shard_map/ppermute | solution.py:527
  128.1 2.4 %collective-permute-start.10 = (f32[1,512]{1,0:T(1,128)S(1)}, f32[1,512]{1,0:T(1,128)S(1)}, u32[]{:S(2)}, u32[]{:S(2)}) collective-permute-start(f32[1,512]{1,0:T(1,128)S(1)} %slice.58), channel_id=1, source_target_pairs={{0,1},{1,2},{2,3},{4,5},{5,6},{6,7},{8,9},{9,10},{10,11},{12,13},{... | collective-permute-start | bytes 6152 | tf_op jit(solution)/shard_map/ppermute | solution.py:646
  131.3 1.7 %all-to-all-done.4 = bf16[16,240,256]{2,1,0:T(8,128)(2,1)S(1)} async-done(((bf16[16,240,256]{2,1,0:T(8,128)(2,1)}), bf16[16,240,256]{2,1,0:T(8,128)(2,1)S(1)}, u32[]{:S(2)}, u32[]{:S(2)}) %all-to-all-start.4) | async-done | bytes 1966112 | tf_op jit(solution)/shard_map/all_to_all | solution.py:539
  134.1 4.1 %all-to-all-start.5 = ((bf16[8,64,256]{2,1,0:T(8,128)(2,1)}), bf16[8,64,256]{2,1,0:T(8,128)(2,1)}, u32[]{:S(2)}, u32[]{:S(2)}) async-start(bf16[8,64,256]{2,1,0:T(8,128)(2,1)} %bitcast.19), calls=%async_computation.5 | async-start | bytes 524288 | tf_op jit(solution)/shard_map/all_to_all | solution.py:559
  138.2 5.8 %shard_map.148 = bf16[1024,512]{1,0:T(8,128)(2,1)} custom-call(s32[1]{0:T(128)} %bitcast.place_ref, bf16[1024,512]{1,0:T(8,128)(2,1)} %get-tuple-element.102.refs_0_, bf16[1536,512]{1,0:T(8,128)(2,1)} %get-tuple-element.89.refs_22_.refs_1_, f32[1,512]{1,0:T(1,128)} %copy-done.7), custom_call_target="tpu_custom_call" | custom-call | flops 1073741824 | bytes 4194304 | tf_op jit(solution)/shard_map/pallas_call | solution.py:64
  144.0 3.6 %all-to-all-done.5 = bf16[8,64,256]{2,1,0:T(8,128)(2,1)} async-done(((bf16[8,64,256]{2,1,0:T(8,128)(2,1)}), bf16[8,64,256]{2,1,0:T(8,128)(2,1)}, u32[]{:S(2)}, u32[]{:S(2)}) %all-to-all-start.5) | async-done | bytes 262176 | tf_op jit(solution)/shard_map/all_to_all | solution.py:559
  147.5 1.0 convert_reduce_fusion.2.mine_ref
  148.5 6.1 %collective-permute-start.11 = (f32[64,256]{1,0:T(8,128)S(1)}, f32[64,256]{1,0:T(8,128)S(1)}, u32[]{:S(2)}, u32[]{:S(2)}) collective-permute-start(f32[64,256]{1,0:T(8,128)S(1)} %convert_reduce_fusion.2.mine_ref), channel_id=1, source_target_pairs={{0,1},{1,0},{2,3},{3,2},{4,5},{5,4},{6,7},{7,6},{8,9},{9,8},{10,11... | collective-permute-start | bytes 196616 | tf_op jit(solution)/shard_map/ppermute | solution.py:527
  (60 shorter events, 13.9 us)
Async XLA Ops:
  1.4 0.8 copy-start.1
  2.2 0.7 copy-start.2
  2.9 0.7 copy-start.3
  3.6 0.7 copy-start.4
  21.5 1.5 copy-start
  23.0 30.8 %all-to-all-start.1 = ((bf16[16,240,256]{2,1,0:T(8,128)(2,1)}), bf16[16,240,256]{2,1,0:T(8,128)(2,1)}, u32[]{:S(2)}, u32[]{:S(2)}) async-start(bf16[16,240,256]{2,1,0:T(8,128)(2,1)} %shard_map.144), calls=%async_computation.1 | async-start | bytes 3932160 | tf_op jit(solution)/shard_map/all_to_all | solution.py:539
  30.6 7.3 %collective-permute-start = (bf16[16,512]{1,0:T(8,128)(2,1)S(1)}, bf16[16,512]{1,0:T(8,128)(2,1)S(1)}, u32[]{:S(2)}, u32[]{:S(2)}) collective-permute-start(bf16[16,512]{1,0:T(8,128)(2,1)S(1)} %slice_bitcast_fusion), channel_id=1, source_target_pairs={{1,0},{2,1},{3,2},{5,4},{6,5},{7,6},{9,8},{10,9},{11,10},{13,12},{... | collective-permute-start | bytes 49160 | tf_op jit(solution)/shard_map/ppermute | solution.py:589
  37.9 0.6 copy-start.6
  41.7 6.0 %collective-permute-start.1 = (bf16[3,512,512]{2,1,0:T(8,128)(2,1)}, bf16[3,512,512]{2,1,0:T(8,128)(2,1)}, u32[]{:S(2)}, u32[]{:S(2)}) collective-permute-start(bf16[3,512,512]{2,1,0:T(8,128)(2,1)} %get-tuple-element.67.refs_2_.refs_23_), channel_id=1, source_target_pairs={{0,1},{1,0},{2,3},{3,2},{4,5},{5,4},{6,7},{7,6},{8,9},{9,8},{10,11... | collective-permute-start | bytes 4718600 | tf_op jit(solution)/shard_map/ppermute | solution.py:527
  41.8 3.9 %collective-permute-start.2 = (bf16[128,1920]{1,0:T(8,128)(2,1)}, bf16[128,1920]{1,0:T(8,128)(2,1)S(1)}, u32[]{:S(2)}, u32[]{:S(2)}) collective-permute-start(bf16[128,1920]{1,0:T(8,128)(2,1)} %bitcast.35), channel_id=1, source_target_pairs={{0,1},{1,0},{2,3},{3,2},{4,5},{5,4},{6,7},{7,6},{8,9},{9,8},{10,11... | collective-permute-start | bytes 1474568 | tf_op jit(solution)/shard_map/ppermute | solution.py:527
  45.8 0.8 copy-start.5
  53.8 9.9 %collective-permute-start.3 = (bf16[16,240,256]{2,1,0:T(8,128)(2,1)}, bf16[16,240,256]{2,1,0:T(8,128)(2,1)}, u32[]{:S(2)}, u32[]{:S(2)}) collective-permute-start(bf16[16,240,256]{2,1,0:T(8,128)(2,1)} %all-to-all-done.1.refs_0_), channel_id=1, source_target_pairs={{0,1},{1,0},{2,3},{3,2},{4,5},{5,4},{6,7},{7,6},{8,9},{9,8},{10,11... | collective-permute-start | bytes 5898248 | tf_op jit(solution)/shard_map/ppermute | solution.py:527
  59.3 22.3 %all-to-all-start.2 = ((bf16[16,4,32,256]{3,2,1,0:T(8,128)(2,1)}), bf16[16,4,32,256]{3,2,1,0:T(8,128)(2,1)}, u32[]{:S(2)}, u32[]{:S(2)}) async-start(bf16[16,4,32,256]{3,2,1,0:T(8,128)(2,1)} %get-tuple-element.65), calls=%async_computation.2 | async-start | bytes 2097152 | tf_op jit(solution)/shard_map/all_to_all | solution.py:539
  81.6 7.3 %collective-permute-start.4 = (bf16[64,32,256]{2,1,0:T(8,128)(2,1)}, bf16[64,32,256]{2,1,0:T(8,128)(2,1)}, u32[]{:S(2)}, u32[]{:S(2)}) collective-permute-start(bf16[64,32,256]{2,1,0:T(8,128)(2,1)} %bitcast.6.refs_0_), channel_id=1, source_target_pairs={{0,1},{1,0},{2,3},{3,2},{4,5},{5,4},{6,7},{7,6},{8,9},{9,8},{10,11... | collective-permute-start | bytes 3145736 | tf_op jit(solution)/shard_map/ppermute | solution.py:527
  82.6 22.3 %all-to-all-start.3 = ((bf16[16,4,32,256]{3,2,1,0:T(8,128)(2,1)}), bf16[16,4,32,256]{3,2,1,0:T(8,128)(2,1)}, u32[]{:S(2)}, u32[]{:S(2)}) async-start(bf16[16,4,32,256]{3,2,1,0:T(8,128)(2,1)} %bitcast.40), calls=%async_computation.3 | async-start | bytes 2097152 | tf_op jit(solution)/shard_map/all_to_all | solution.py:539
  104.9 28.1 %all-to-all-start.4 = ((bf16[16,240,256]{2,1,0:T(8,128)(2,1)}), bf16[16,240,256]{2,1,0:T(8,128)(2,1)S(1)}, u32[]{:S(2)}, u32[]{:S(2)}) async-start(bf16[16,240,256]{2,1,0:T(8,128)(2,1)} %get-tuple-element.96), calls=%async_computation.4 | async-start | bytes 3932160 | tf_op jit(solution)/shard_map/all_to_all | solution.py:539
  110.1 5.2 %collective-permute-start.5 = (bf16[32,256]{1,0:T(8,128)(2,1)S(1)}, bf16[32,256]{1,0:T(8,128)(2,1)S(1)}, u32[]{:S(2)}, u32[]{:S(2)}) collective-permute-start(bf16[32,256]{1,0:T(8,128)(2,1)S(1)} %get-tuple-element.114), channel_id=1, source_target_pairs={{0,16},{16,32},{32,48},{48,0},{1,17},{17,33},{33,49},{49,1},{2,18}... | collective-permute-start | bytes 49160 | tf_op jit(solution)/shard_map/ppermute | solution.py:535
  110.2 5.1 %collective-permute-start.7 = (bf16[32,256]{1,0:T(8,128)(2,1)S(1)}, bf16[32,256]{1,0:T(8,128)(2,1)S(1)}, u32[]{:S(2)}, u32[]{:S(2)}) collective-permute-start(bf16[32,256]{1,0:T(8,128)(2,1)S(1)} %get-tuple-element.115), channel_id=1, source_target_pairs={{0,48},{16,0},{32,16},{48,32},{1,49},{17,1},{33,17},{49,33},{2,50}... | collective-permute-start | bytes 49160 | tf_op jit(solution)/shard_map/ppermute | solution.py:535
  113.8 6.8 %collective-permute-start.6 = (bf16[32,256]{1,0:T(8,128)(2,1)S(1)}, bf16[32,256]{1,0:T(8,128)(2,1)S(1)}, u32[]{:S(2)}, u32[]{:S(2)}) collective-permute-start(bf16[32,256]{1,0:T(8,128)(2,1)S(1)} %get-tuple-element.116), channel_id=1, source_target_pairs={{0,32},{16,48},{32,0},{48,16},{1,33},{17,49},{33,1},{49,17},{2,34}... | collective-permute-start | bytes 49160 | tf_op jit(solution)/shard_map/ppermute | solution.py:535
  120.6 3.1 %collective-permute-start.8 = (f32[32,256]{1,0:T(8,128)S(1)}, f32[32,256]{1,0:T(8,128)S(1)}, u32[]{:S(2)}, u32[]{:S(2)}) collective-permute-start(f32[32,256]{1,0:T(8,128)S(1)} %fusion.1), channel_id=1, source_target_pairs={{0,2},{2,0},{1,3},{3,1},{4,6},{6,4},{5,7},{7,5},{8,10},{10,8},{9,1... | collective-permute-start | bytes 98312 | tf_op jit(solution)/shard_map/ppermute | solution.py:568
  123.7 6.8 %collective-permute-start.9 = (f32[32,256]{1,0:T(8,128)S(1)}, f32[32,256]{1,0:T(8,128)S(1)}, u32[]{:S(2)}, u32[]{:S(2)}) collective-permute-start(f32[32,256]{1,0:T(8,128)S(1)} %add.86), channel_id=1, source_target_pairs={{0,1},{1,0},{2,3},{3,2},{4,5},{5,4},{6,7},{7,6},{8,9},{9,8},{10,11... | collective-permute-start | bytes 98312 | tf_op jit(solution)/shard_map/ppermute | solution.py:527
  128.1 3.2 %collective-permute-start.10 = (f32[1,512]{1,0:T(1,128)S(1)}, f32[1,512]{1,0:T(1,128)S(1)}, u32[]{:S(2)}, u32[]{:S(2)}) collective-permute-start(f32[1,512]{1,0:T(1,128)S(1)} %slice.58), channel_id=1, source_target_pairs={{0,1},{1,2},{2,3},{4,5},{5,6},{6,7},{8,9},{9,10},{10,11},{12,13},{... | collective-permute-start | bytes 6152 | tf_op jit(solution)/shard_map/ppermute | solution.py:646
  131.3 6.9 %copy-start.7 = (f32[1,512]{1,0:T(1,128)}, f32[1,512]{1,0:T(1,128)S(1)}, u32[]{:S(2)}) copy-start(f32[1,512]{1,0:T(1,128)S(1)} %collective-permute-done.10.refs_2_) | copy-start | bytes 6148
  134.1 13.4 %all-to-all-start.5 = ((bf16[8,64,256]{2,1,0:T(8,128)(2,1)}), bf16[8,64,256]{2,1,0:T(8,128)(2,1)}, u32[]{:S(2)}, u32[]{:S(2)}) async-start(bf16[8,64,256]{2,1,0:T(8,128)(2,1)} %bitcast.19), calls=%async_computation.5 | async-start | bytes 524288 | tf_op jit(solution)/shard_map/all_to_all | solution.py:559
  148.5 7.0 %collective-permute-start.11 = (f32[64,256]{1,0:T(8,128)S(1)}, f32[64,256]{1,0:T(8,128)S(1)}, u32[]{:S(2)}, u32[]{:S(2)}) collective-permute-start(f32[64,256]{1,0:T(8,128)S(1)} %convert_reduce_fusion.2.mine_ref), channel_id=1, source_target_pairs={{0,1},{1,0},{2,3},{3,2},{4,5},{5,4},{6,7},{7,6},{8,9},{9,8},{10,11... | collective-permute-start | bytes 196616 | tf_op jit(solution)/shard_map/ppermute | solution.py:527
